TPU v7x, 32 devices: a whole 2x2x4 slice. The times are simulated.
32 devices in a mesh: dp: 8 (over z, x), mp: 4 (over y, core).
Axes of the slice: x: 2, y: 2, z: 4, core: 2. Of those that a mesh axis runs over, the one named last changes fastest.
Arguments:
- tokens: bfloat16 [32768, 768], P(('dp', 'mp')), may hold values from -6 to 6
- cotangent: bfloat16 [32768, 768], P(('dp', 'mp'))
- lengths: int32 [32], P('dp'), may hold values from 64 to 1024, as said below
- input_weight: float32 [768, 3, 768], P('dp', None, 'mp'), may hold values from -0.21875 to 0.21875
- output_weight: float32 [768, 768], P('mp', 'dp')
- expand_weight: float32 [768, 3072], P('dp', 'mp'), may hold values from -0.21875 to 0.21875
- shrink_weight: float32 [3072, 768], P('mp', 'dp')
- layer_vectors: float32 [6, 768], replicated
- head_bias: float32 [2, 768], P(None, 'mp'), may hold values from -1 to 1
- expand_bias: float32 [3072], P('mp'), may hold values from -1 to 1
- first_input: float32 [768, 3, 768], P('dp', None, 'mp')
- first_output: float32 [768, 768], P('mp', 'dp')
- first_expand: float32 [768, 3072], P('dp', 'mp')
- first_shrink: float32 [3072, 768], P('mp', 'dp')
- first_vectors: float32 [6, 768], replicated
- first_head: float32 [2, 768], P(None, 'mp')
- first_bias: float32 [3072], P('mp')
- second_input: float32 [768, 3, 768], P('dp', None, 'mp'), as said below
- second_output: float32 [768, 768], P('mp', 'dp'), as said below
- second_expand: float32 [768, 3072], P('dp', 'mp'), as said below
- second_shrink: float32 [3072, 768], P('mp', 'dp'), as said below
- second_vectors: float32 [6, 768], replicated, as said below
- second_head: float32 [2, 768], P(None, 'mp'), as said below
- second_bias: float32 [3072], P('mp'), as said below
Outputs:
- block_out: bfloat16 [32768, 768], P(('dp', 'mp'))
- token_grad: bfloat16 [32768, 768], P(('dp', 'mp'))
- grad_norm: float32 [], replicated
- moment_input: float32 [768, 3, 768], P('dp', None, 'mp')
- square_input: float32 [768, 3, 768], P('dp', None, 'mp')
- updated_input: float32 [768, 3, 768], P('dp', None, 'mp')
- moment_output: float32 [768, 768], P('mp', 'dp')
- square_output: float32 [768, 768], P('mp', 'dp')
- updated_output: float32 [768, 768], P('mp', 'dp')
- moment_expand: float32 [768, 3072], P('dp', 'mp')
- square_expand: float32 [768, 3072], P('dp', 'mp')
- updated_expand: float32 [768, 3072], P('dp', 'mp')
- moment_shrink: float32 [3072, 768], P('mp', 'dp')
- square_shrink: float32 [3072, 768], P('mp', 'dp')
- updated_shrink: float32 [3072, 768], P('mp', 'dp')
- moment_vectors: float32 [6, 768], replicated
- square_vectors: float32 [6, 768], replicated
- updated_vectors: float32 [6, 768], replicated
- moment_head: float32 [2, 768], P(None, 'mp')
- square_head: float32 [2, 768], P(None, 'mp')
- updated_head: float32 [2, 768], P(None, 'mp')
- moment_bias: float32 [3072], P('mp')
- square_bias: float32 [3072], P('mp')
- updated_bias: float32 [3072], P('mp')
Inputs may be any that keep to these rules, and one draw needn't show every extreme that they name: lengths of the sequences; some sequence has all 1024 positions valid. `second_input`: positive. `second_output`: positive. `second_expand`: positive. `second_shrink`: positive. `second_vectors`: positive. `second_head`: positive. `second_bias`: positive.
All inputs are finite; a program needn't handle non-finite values.
Results may differ from a plain program's by a relative error of at most 0.012.
Values may be sent and summed in bfloat16 or wider, within the bound.
No kernel may reach another device: no remote copies, remote signals or barrier semaphores. Data moves between devices by JAX's collectives and lax.ppermute only.
A program may use at most 192 MiB of HBM per device.

v0:
```python
import jax
import jax.numpy as jnp
from jax import lax
from jax.sharding import PartitionSpec as P

HEAD_DIM = 64
BLOCK = 512
STEP = 10


eps_norm = 1e-05
clip_norm = 1.0
beta_one = 0.9
beta_two = 0.999
adam_eps = 1e-08
rate = 0.05
vector_rate = 0.5
decay = 0.01
excluded = -1e30


def layer_norm(values, norm_gain, norm_shift):
    average = jnp.mean(values, axis=-1, keepdims=True)
    centred = values - average
    inverse = lax.rsqrt(jnp.mean(centred * centred, axis=-1, keepdims=True) + eps_norm)
    return centred * inverse * norm_gain + norm_shift


def gelu_tanh(values):
    return jax.nn.gelu(values, approximate=True)


def block_scores(queries, key_rows, first_row, length):
    scores = jnp.einsum(
        "qhd,khd->hqk", queries, key_rows, preferred_element_type=jnp.float32
    ) * HEAD_DIM ** (-0.5)
    row_ids = first_row + jnp.arange(queries.shape[0])[:, None]
    col_ids = jnp.arange(key_rows.shape[0])[None, :]
    visible = (col_ids <= row_ids) & (col_ids < length)
    return (jnp.where(visible[None], scores, excluded), visible)


def forward_block(queries, key_rows, value_rows, first_row, length):
    scores, visible = block_scores(queries, key_rows, first_row, length)
    row_max = jnp.max(scores, axis=-1, keepdims=True)
    weights = jnp.exp(scores - row_max)
    totals = jnp.sum(weights, axis=-1, keepdims=True)
    probabilities = (weights / totals).astype(jnp.bfloat16)
    mixture = jnp.einsum(
        "hqk,khd->qhd", probabilities, value_rows, preferred_element_type=jnp.float32
    )
    row_live = (first_row + jnp.arange(queries.shape[0]) < length)[:, None, None]
    mixture = jnp.where(row_live, mixture, 0.0).astype(jnp.bfloat16)
    return (mixture, (row_max + jnp.log(totals))[..., 0])


def attend_forward(packed, length):
    mixtures = []
    log_parts = []
    for block_index in range(packed.shape[0] // BLOCK):
        first_row = block_index * BLOCK
        last_row = first_row + BLOCK
        queries = packed[first_row:last_row, 0]
        key_rows = packed[:last_row, 1]
        value_rows = packed[:last_row, 2]
        mixture, log_total = forward_block(queries, key_rows, value_rows, first_row, length)
        mixtures.append(mixture)
        log_parts.append(log_total)
    return (jnp.concatenate(mixtures, axis=0), jnp.concatenate(log_parts, axis=1))


def backward_block(queries, key_rows, value_rows, upstream, log_total, first_row, length):
    scores, visible = block_scores(queries, key_rows, first_row, length)
    probabilities = jnp.exp(scores - log_total[..., None])
    prob_grad = jnp.einsum("qhd,khd->hqk", upstream, value_rows, preferred_element_type=jnp.float32)
    inner = jnp.sum(probabilities * prob_grad, axis=-1, keepdims=True)
    score_grad = jnp.where(visible[None], probabilities * (prob_grad - inner), 0.0).astype(
        jnp.bfloat16
    )
    scale_factor = HEAD_DIM ** (-0.5)
    query_grad = (
        jnp.einsum("hqk,khd->qhd", score_grad, key_rows, preferred_element_type=jnp.float32)
        * scale_factor
    )
    key_grad = (
        jnp.einsum("hqk,qhd->khd", score_grad, queries, preferred_element_type=jnp.float32)
        * scale_factor
    )
    value_grad = jnp.einsum(
        "hqk,qhd->khd",
        probabilities.astype(jnp.bfloat16),
        upstream,
        preferred_element_type=jnp.float32,
    )
    return (query_grad, key_grad, value_grad)


def attend_backward(packed, mixture_grad, log_totals, length):
    seq_length = packed.shape[0]
    key_sum = jnp.zeros(packed[:, 1].shape, jnp.float32)
    value_sum = jnp.zeros(packed[:, 2].shape, jnp.float32)
    query_parts = []
    for block_index in range(seq_length // BLOCK):
        first_row = block_index * BLOCK
        last_row = first_row + BLOCK
        queries = packed[first_row:last_row, 0]
        key_rows = packed[:last_row, 1]
        value_rows = packed[:last_row, 2]
        upstream = mixture_grad[first_row:last_row]
        log_total = log_totals[:, first_row:last_row]
        query_grad, key_grad, value_grad = backward_block(
            queries, key_rows, value_rows, upstream, log_total, first_row, length
        )
        query_parts.append(query_grad)
        key_sum = key_sum.at[:last_row].add(key_grad)
        value_sum = value_sum.at[:last_row].add(value_grad)
    query_all = jnp.concatenate(query_parts, axis=0)
    return jnp.stack([query_all, key_sum, value_sum], axis=1).astype(jnp.bfloat16)


def attend_bundle(bundle):
    return attend_forward(bundle[0], bundle[1])


def backward_bundle(bundle):
    return attend_backward(bundle[0], bundle[1], bundle[2], bundle[3])


def adam_step(weight, gradient, first_old, second_old, factor, step_rate):
    scaled = gradient * factor
    moment = beta_one * first_old + (1.0 - beta_one) * scaled
    square = beta_two * second_old + (1.0 - beta_two) * scaled * scaled
    corrected = moment / (1.0 - beta_one**STEP)
    spread = jnp.sqrt(square / (1.0 - beta_two**STEP))
    updated = weight - step_rate * (corrected / (spread + adam_eps) + decay * weight)
    return (moment, square, updated)


def squares(values):
    return jnp.sum(values * values)


def shards(
    tokens,
    cotangent,
    lengths,
    input_weight,
    output_weight,
    expand_weight,
    shrink_weight,
    layer_vectors,
    head_bias,
    expand_bias,
    first_input,
    first_output,
    first_expand,
    first_shrink,
    first_vectors,
    first_head,
    first_bias,
    second_input,
    second_output,
    second_expand,
    second_shrink,
    second_vectors,
    second_head,
    second_bias,
):
    lowered = (
        input_weight.astype(jnp.bfloat16),
        output_weight.astype(jnp.bfloat16),
        expand_weight.astype(jnp.bfloat16),
        shrink_weight.astype(jnp.bfloat16),
    )
    wide_input, wide_output, wide_expand, wide_shrink = (
        lax.all_gather(lowered[0], "dp", axis=0, tiled=True),
        lax.all_gather(lowered[1], "dp", axis=1, tiled=True),
        lax.all_gather(lowered[2], "dp", axis=0, tiled=True),
        lax.all_gather(lowered[3], "dp", axis=1, tiled=True),
    )
    own_rows = tokens.shape[0]
    model_count = lax.axis_size("mp")
    model_index = lax.axis_index("mp")
    head_width = head_bias.shape[1]
    bias_width = expand_bias.shape[0]
    residual = tokens.astype(jnp.float32)
    back_rows = cotangent.astype(jnp.float32)
    norm_one, pull_one = jax.vjp(layer_norm, residual, layer_vectors[0], layer_vectors[1])
    seq_count = lengths.shape[0]
    head_count = wide_input.shape[2] // HEAD_DIM
    normed = lax.all_gather(norm_one.astype(jnp.bfloat16), "mp", axis=0, tiled=True)
    row_total = normed.shape[0]
    seq_length = row_total // seq_count
    projected = jnp.einsum("td,dce->tce", normed, wide_input, preferred_element_type=jnp.float32)
    bias_rows = jnp.stack([head_bias[0], jnp.zeros_like(head_bias[0]), head_bias[1]])
    packed = (
        (projected + bias_rows[None])
        .astype(jnp.bfloat16)
        .reshape(seq_count, seq_length, 3, head_count, HEAD_DIM)
    )
    mixture, log_totals = lax.map(attend_bundle, (packed, lengths))
    mixture_flat = mixture.reshape(row_total, head_count * HEAD_DIM)
    row_piece = lax.slice_in_dim(mixture_flat, 0, lax.axis_size("mp") * own_rows, axis=0)
    attended = lax.psum_scatter(
        jnp.dot(row_piece, wide_output, preferred_element_type=jnp.float32),
        "mp",
        scatter_dimension=0,
        tiled=True,
    )
    middle = residual + attended + layer_vectors[4]
    norm_two, pull_two = jax.vjp(layer_norm, middle, layer_vectors[2], layer_vectors[3])
    hidden_in, upstream = (
        lax.all_gather(norm_two.astype(jnp.bfloat16), "mp", axis=0, tiled=True),
        lax.all_gather(cotangent, "mp", axis=0, tiled=True),
    )
    pre_act = jnp.dot(hidden_in, wide_expand, preferred_element_type=jnp.float32) + expand_bias
    activation, pull_gelu = jax.vjp(gelu_tanh, pre_act)
    activation = activation.astype(jnp.bfloat16)
    row_piece = lax.slice_in_dim(activation, 0, own_rows * lax.axis_size("mp"), axis=0)
    shrunk = lax.psum_scatter(
        jnp.dot(row_piece, wide_shrink, preferred_element_type=jnp.float32).astype(jnp.bfloat16),
        "mp",
        scatter_dimension=0,
        tiled=True,
    ).astype(jnp.float32)
    block_out = (middle + shrunk + layer_vectors[5]).astype(jnp.bfloat16)
    grad_shrink = jnp.einsum("tf,td->fd", activation, upstream, preferred_element_type=jnp.float32)
    act_grad = jnp.einsum("td,fd->tf", upstream, wide_shrink, preferred_element_type=jnp.float32)
    pre_grad = pull_gelu(act_grad)[0].astype(jnp.bfloat16)
    grad_expand = jnp.einsum("td,tf->df", hidden_in, pre_grad, preferred_element_type=jnp.float32)
    expand_bias_grad = jnp.sum(pre_grad.astype(jnp.float32), axis=0)
    row_piece = lax.slice_in_dim(pre_grad, 0, lax.axis_size("mp") * own_rows, axis=0)
    norm_two_grad = lax.psum_scatter(
        jnp.einsum("tf,df->td", row_piece, wide_expand, preferred_element_type=jnp.float32),
        "mp",
        scatter_dimension=0,
        tiled=True,
    )
    middle_part, gain_two_grad, shift_two_grad = pull_two(norm_two_grad)
    middle_grad = back_rows + middle_part
    attend_grad = lax.all_gather(middle_grad.astype(jnp.bfloat16), "mp", axis=0, tiled=True)
    grad_output = jnp.einsum(
        "tc,td->cd", mixture_flat, attend_grad, preferred_element_type=jnp.float32
    )
    mixture_grad = jnp.einsum(
        "td,cd->tc", attend_grad, wide_output, preferred_element_type=jnp.float32
    ).astype(jnp.bfloat16)
    mixture_grad = mixture_grad.reshape(seq_count, seq_length, head_count, HEAD_DIM)
    row_alive = (jnp.arange(seq_length)[None, :] < lengths[:, None])[:, :, None, None]
    mixture_grad = jnp.where(row_alive, mixture_grad, jnp.zeros_like(mixture_grad))
    packed_grad = lax.map(backward_bundle, (packed, mixture_grad, log_totals, lengths))
    packed_grad = packed_grad.reshape(row_total, 3, head_count * HEAD_DIM)
    grad_input = jnp.einsum("td,tce->dce", normed, packed_grad, preferred_element_type=jnp.float32)
    part_sums = jnp.sum(packed_grad.astype(jnp.float32), axis=0)
    head_local = jnp.stack([part_sums[0], part_sums[2]])
    row_piece = lax.slice_in_dim(packed_grad, 0, lax.axis_size("mp") * own_rows, axis=0)
    norm_one_grad = lax.psum_scatter(
        jnp.einsum("tce,dce->td", row_piece, wide_input, preferred_element_type=jnp.float32),
        "mp",
        scatter_dimension=0,
        tiled=True,
    )
    head_full = lax.dynamic_update_slice(
        jnp.zeros((2, head_width * model_count), jnp.float32),
        head_local,
        (0, model_index * head_width),
    )
    bias_full = lax.dynamic_update_slice(
        jnp.zeros((bias_width * model_count,), jnp.float32),
        expand_bias_grad,
        (model_index * bias_width,),
    )
    input_part, gain_one_grad, shift_one_grad = pull_one(norm_one_grad)
    token_grad = (middle_grad + input_part).astype(jnp.bfloat16)
    vector_local = jnp.stack(
        [
            gain_one_grad,
            shift_one_grad,
            gain_two_grad,
            shift_two_grad,
            jnp.sum(middle_grad, axis=0),
            jnp.sum(back_rows, axis=0),
        ]
    )
    vector_grad, head_summed, bias_summed = lax.psum(
        (vector_local, head_full, bias_full), ("dp", "mp")
    )
    head_total = lax.dynamic_slice_in_dim(head_summed, model_index * head_width, head_width, 1)
    bias_total = lax.dynamic_slice_in_dim(bias_summed, model_index * bias_width, bias_width, 0)
    input_total, output_total, expand_total, shrink_total = (
        lax.psum_scatter(grad_input, "dp", scatter_dimension=0, tiled=True),
        lax.psum_scatter(grad_output, "dp", scatter_dimension=1, tiled=True),
        lax.psum_scatter(grad_expand, "dp", scatter_dimension=0, tiled=True),
        lax.psum_scatter(grad_shrink, "dp", scatter_dimension=1, tiled=True),
    )
    owned = (
        squares(input_total) + squares(output_total) + squares(expand_total) + squares(shrink_total)
    )
    data_first = (lax.axis_index("dp") == 0).astype(jnp.float32)
    model_first = (model_index == 0).astype(jnp.float32)
    local_squares = (
        owned
        + data_first * (squares(head_total) + squares(bias_total))
        + data_first * model_first * squares(vector_grad)
    )
    squared = lax.psum(local_squares, ("dp", "mp"))
    grad_norm = jnp.sqrt(squared)
    factor = clip_norm / jnp.maximum(grad_norm, clip_norm)
    moment_input, square_input, updated_input = adam_step(
        input_weight, input_total, first_input, second_input, factor, rate
    )
    moment_output, square_output, updated_output = adam_step(
        output_weight, output_total, first_output, second_output, factor, rate
    )
    moment_expand, square_expand, updated_expand = adam_step(
        expand_weight, expand_total, first_expand, second_expand, factor, rate
    )
    moment_shrink, square_shrink, updated_shrink = adam_step(
        shrink_weight, shrink_total, first_shrink, second_shrink, factor, rate
    )
    moment_vectors, square_vectors, updated_vectors = adam_step(
        layer_vectors, vector_grad, first_vectors, second_vectors, factor, vector_rate
    )
    moment_head, square_head, updated_head = adam_step(
        head_bias, head_total, first_head, second_head, factor, vector_rate
    )
    moment_bias, square_bias, updated_bias = adam_step(
        expand_bias, bias_total, first_bias, second_bias, factor, vector_rate
    )
    return (
        block_out,
        token_grad,
        grad_norm,
        moment_input,
        square_input,
        updated_input,
        moment_output,
        square_output,
        updated_output,
        moment_expand,
        square_expand,
        updated_expand,
        moment_shrink,
        square_shrink,
        updated_shrink,
        moment_vectors,
        square_vectors,
        updated_vectors,
        moment_head,
        square_head,
        updated_head,
        moment_bias,
        square_bias,
        updated_bias,
    )


def solution(mesh):
    in_specs = (
        P(("dp", "mp"), None),
        P(("dp", "mp"), None),
        P("dp"),
        P("dp", None, "mp"),
        P("mp", "dp"),
        P("dp", "mp"),
        P("mp", "dp"),
        P(),
        P(None, "mp"),
        P("mp"),
        P("dp", None, "mp"),
        P("mp", "dp"),
        P("dp", "mp"),
        P("mp", "dp"),
        P(),
        P(None, "mp"),
        P("mp"),
        P("dp", None, "mp"),
        P("mp", "dp"),
        P("dp", "mp"),
        P("mp", "dp"),
        P(),
        P(None, "mp"),
        P("mp"),
    )
    out_specs = (
        P(("dp", "mp"), None),
        P(("dp", "mp"), None),
        P(),
        P("dp", None, "mp"),
        P("dp", None, "mp"),
        P("dp", None, "mp"),
        P("mp", "dp"),
        P("mp", "dp"),
        P("mp", "dp"),
        P("dp", "mp"),
        P("dp", "mp"),
        P("dp", "mp"),
        P("mp", "dp"),
        P("mp", "dp"),
        P("mp", "dp"),
        P(),
        P(),
        P(),
        P(None, "mp"),
        P(None, "mp"),
        P(None, "mp"),
        P("mp"),
        P("mp"),
        P("mp"),
    )
    return jax.shard_map(shards, mesh=mesh, in_specs=in_specs, out_specs=out_specs, check_vma=False)
```

profile of v0, /device:TPU:0, one launch (start us, length us, event | category | flops | bytes accessed | tf_op | source)
XLA Modules:
  0.0 1290.3 jit_solution(105321271778164482)
XLA Ops:
  16.0 38.8 %all_gather.25 = bf16[768,3,192]{2,1,0:T(4,128)(2,1)S(1)} all-gather(bf16[96,3,192]{2,1,0:T(4,128)(2,1)S(1)} %copy.88), channel_id=1, replica_groups=mesh['dp'=8,'mp'=4] {'dp'}, dimensions={0}, use_global_device_ids=true | all-gather | bytes 995328 | tf_op jit(solution)/shard_map/all_gather | solution.py:176
  57.0 31.4 %all_gather.26 = bf16[192,768]{0,1:T(8,128)(2,1)S(1)} all-gather(bf16[192,96]{0,1:T(8,128)(2,1)} %copy.92), channel_id=1, replica_groups=mesh['dp'=8,'mp'=4] {'dp'}, dimensions={1}, use_global_device_ids=true | all-gather | bytes 331776 | tf_op jit(solution)/shard_map/all_gather | solution.py:177
  88.4 6.4 fusion.195
  94.8 3.7 add_convert_fusion
  98.4 8.8 reshape.538
  107.3 6.1 copy.90
  113.4 49.3 %while.33 = (s32[]{:T(128)}, bf16[4,1024,3,64]{1,3,2,0:T(8,128)(2,1)S(1)}, f32[4,3,1024]{2,1,0:T(4,128)}, s32[4]{0:T(128)S(1)}, bf16[4,1024,3,3,64]{1,4,3,2,0:T(8,128)(2,1)}) while((s32[]{:T(128)}, bf16[4,1024,3,64]{1,3,2,0:T(8,128)(2,1)S(1)}, f32[4,3,1024]{2,1,0:T(4,128)}, s32[4]{0:T(128)S(1)}, ...), condition=%wide.region_7.8_spmd.clone, body=%wide.region_2.7_spmd.sunk.clone | while | flops 635046912 | bytes 36713060 | solution.py:201
  165.8 6.5 fusion.196
  173.9 96.9 %reduce-scatter.11.cloned.1.call-done = f32[1024,768]{1,0:T(8,128)} async-done(((f32[4096,768]{1,0:T(8,128)}), f32[1024,768]{1,0:T(8,128)}) %reduce-scatter.11.cloned.1.call-update) | async-done | bytes 3145744 | tf_op jit(solution)/shard_map/reduce_scatter | solution.py:204
  270.8 2.8 fusion.190
  278.6 43.8 %all-gather.9.cloned.1.call-done = bf16[4096,768]{1,0:T(8,128)(2,1)} async-done(((bf16[1024,768]{1,0:T(8,128)(2,1)}), bf16[4096,768]{1,0:T(8,128)(2,1)}) %all-gather.9.cloned.1.call-update) | async-done | bytes 6291472 | tf_op jit(solution)/shard_map/all_gather | solution.py:213
  322.4 10.1 fusion.197
  332.6 34.0 %all-gather.13.cloned.1.call-done = bf16[768,768]{0,1:T(8,128)(2,1)} async-done(((bf16[768,96]{0,1:T(8,128)(2,1)}), bf16[768,768]{0,1:T(8,128)(2,1)}) %all-gather.13.cloned.1.call-update) | async-done | bytes 1179664 | tf_op jit(solution)/shard_map/all_gather | solution.py:179
  366.6 46.3 %all-gather.15.cloned.1.call-done = bf16[4096,768]{1,0:T(8,128)(2,1)} async-done(((bf16[1024,768]{1,0:T(8,128)(2,1)}), bf16[4096,768]{1,0:T(8,128)(2,1)}) %all-gather.15.cloned.1.call-update) | async-done | bytes 6291472 | tf_op jit(solution)/shard_map/all_gather | solution.py:214
  412.9 19.5 %convert_reduce_fusion = (f32[768]{0:T(1024)}, bf16[4096,768]{1,0:T(8,128)(2,1)S(1)}, bf16[4096,768]{1,0:T(8,128)(2,1)}) fusion(f32[4096,768]{1,0:T(8,128)} %fusion.197, f32[768]{0:T(1024)} %param.49, bf16[4096,768]{1,0:T(8,128)(2,1)} %all-gather.15.cloned.1.call-done, bf16[768,768]{0,1:T(8,128)(2,1)} %all-gather.13.cloned.1.call-done), kind=kOutput, calls=%fused_computation.141 | convolution fusion | flops 4910480384 | bytes 32643072 | tf_op jit(solution)/shard_map/td,fd->tf/dot_general | solution.py:228
  432.4 2.7 copy-done.50
  435.1 8.1 fusion.198
  443.3 9.8 convolution_convert_fusion
  453.2 89.1 %reduce-scatter.15.cloned.1.call-done = f32[1024,768]{1,0:T(8,128)} async-done(((f32[4096,768]{1,0:T(8,128)}), f32[1024,768]{1,0:T(8,128)}) %reduce-scatter.15.cloned.1.call-update) | async-done | bytes 3145744 | tf_op jit(solution)/shard_map/reduce_scatter | solution.py:233
  542.3 3.4 multiply_reduce_fusion.2
  546.3 56.8 %reduce-scatter.13.cloned.1.call-done = bf16[1024,768]{1,0:T(8,128)(2,1)} async-done(((bf16[4096,768]{1,0:T(8,128)(2,1)}), bf16[1024,768]{1,0:T(8,128)(2,1)}) %reduce-scatter.13.cloned.1.call-update) | async-done | bytes 1572880 | tf_op jit(solution)/shard_map/reduce_scatter | solution.py:220
  603.1 4.4 fusion.189
  610.8 10.1 fusion.199
  621.1 10.3 fusion.200
  631.5 25.9 %all-gather.17.cloned.1.call-done = bf16[4096,768]{1,0:T(8,128)(2,1)} async-done(((bf16[1024,768]{1,0:T(8,128)(2,1)}), bf16[4096,768]{1,0:T(8,128)(2,1)}) %all-gather.17.cloned.1.call-update) | async-done | bytes 6291472 | tf_op jit(solution)/shard_map/all_gather | solution.py:241
  657.3 5.0 convolution_convert_fusion.1
  667.1 251.7 %while.34 = (s32[]{:T(128)}, bf16[4,1024,3,3,64]{1,4,3,2,0:T(8,128)(2,1)}, bf16[4,1024,3,3,64]{1,4,3,2,0:T(8,128)(2,1)}, s32[4]{0:T(128)S(1)}, f32[4,3,1024]{2,1,0:T(4,128)}, /*index=5*/bf16[4,1024,3,64]{1,3,2,0:T(8,128)(2,1)S(1)}) while((s32[]{:T(128)}, bf16[4,1024,3,3,64]{1,4,3,2,0:T(8,128)(2,1)}, ...), condition=%wide.region_18.19_spmd.clone, body=%wide.region_15.18_spmd.sunk.clone | while | flops 1569238016 | bytes 159816960 | solution.py:251
  678.2 6.4 fusion.307
  684.6 6.6 fusion.304
  692.2 2.8 fusion.301
  695.0 3.7 fusion.302
  698.7 14.6 %fusion.305 = bf16[1,1024,1,3,64]{1,4,3,2,0:T(8,128)(2,1)} fusion(f32[3,512,1024]{2,1,0:T(8,128)} %fusion.302, f32[3,512,1024]{2,1,0:T(8,128)} %copy-done, f32[3,512]{1,0:T(4,128)S(1)} %get-tuple-element.462, pred[512,1024]{1,0:T(8,128)(4,1)S(1)} %fusion.298, f32[512,3,64]{0,2,1:T(8,128)} %fusion.304, ...), kind=kOutput, calls=%fused_computation.87.clone.1.clone | convolution fusion | flops 219220480 | bytes 27213824 | tf_op jit(solution)/shard_map/while/body/eval_jaxpr/hqk,qhd->khd/dot_general | solution.py:86
  713.3 13.7 %fusion.306 = bf16[512,3,64]{0,2,1:T(8,128)(2,1)} fusion(f32[3,512,1024]{2,1,0:T(8,128)} %fusion.302, f32[3,512,1024]{2,1,0:T(8,128)} %copy-done, f32[3,512]{1,0:T(4,128)S(1)} %get-tuple-element.462, pred[512,1024]{1,0:T(8,128)(4,1)S(1)} %fusion.298, bf16[1024,3,3,64]{0,3,2,1:T(8,128)(2,1)S(1)} %dynamic-slice_bitcast_fusion.28), kind=kOutput, calls=%fused_computation.99.clone.1.clone | convolution fusion | flops 218827264 | bytes 26820608 | tf_op jit(solution)/shard_map/while/body/eval_jaxpr/hqk,khd->qhd/dot_general | solution.py:82
  741.1 6.4 fusion.307
  747.5 6.4 fusion.304
  755.0 2.8 fusion.301
  757.8 3.7 fusion.302
  761.5 14.6 %fusion.305 = bf16[1,1024,1,3,64]{1,4,3,2,0:T(8,128)(2,1)} fusion(f32[3,512,1024]{2,1,0:T(8,128)} %fusion.302, f32[3,512,1024]{2,1,0:T(8,128)} %copy-done, f32[3,512]{1,0:T(4,128)S(1)} %get-tuple-element.462, pred[512,1024]{1,0:T(8,128)(4,1)S(1)} %fusion.298, f32[512,3,64]{0,2,1:T(8,128)} %fusion.304, ...), kind=kOutput, calls=%fused_computation.87.clone.1.clone | convolution fusion | flops 219220480 | bytes 27213824 | tf_op jit(solution)/shard_map/while/body/eval_jaxpr/hqk,qhd->khd/dot_general | solution.py:86
  776.1 13.7 %fusion.306 = bf16[512,3,64]{0,2,1:T(8,128)(2,1)} fusion(f32[3,512,1024]{2,1,0:T(8,128)} %fusion.302, f32[3,512,1024]{2,1,0:T(8,128)} %copy-done, f32[3,512]{1,0:T(4,128)S(1)} %get-tuple-element.462, pred[512,1024]{1,0:T(8,128)(4,1)S(1)} %fusion.298, bf16[1024,3,3,64]{0,3,2,1:T(8,128)(2,1)S(1)} %dynamic-slice_bitcast_fusion.28), kind=kOutput, calls=%fused_computation.99.clone.1.clone | convolution fusion | flops 218827264 | bytes 26820608 | tf_op jit(solution)/shard_map/while/body/eval_jaxpr/hqk,khd->qhd/dot_general | solution.py:82
  803.9 6.4 fusion.307
  810.2 6.4 fusion.304
  817.7 2.8 fusion.301
  820.5 3.7 fusion.302
  824.2 14.6 %fusion.305 = bf16[1,1024,1,3,64]{1,4,3,2,0:T(8,128)(2,1)} fusion(f32[3,512,1024]{2,1,0:T(8,128)} %fusion.302, f32[3,512,1024]{2,1,0:T(8,128)} %copy-done, f32[3,512]{1,0:T(4,128)S(1)} %get-tuple-element.462, pred[512,1024]{1,0:T(8,128)(4,1)S(1)} %fusion.298, f32[512,3,64]{0,2,1:T(8,128)} %fusion.304, ...), kind=kOutput, calls=%fused_computation.87.clone.1.clone | convolution fusion | flops 219220480 | bytes 27213824 | tf_op jit(solution)/shard_map/while/body/eval_jaxpr/hqk,qhd->khd/dot_general | solution.py:86
  838.8 13.7 %fusion.306 = bf16[512,3,64]{0,2,1:T(8,128)(2,1)} fusion(f32[3,512,1024]{2,1,0:T(8,128)} %fusion.302, f32[3,512,1024]{2,1,0:T(8,128)} %copy-done, f32[3,512]{1,0:T(4,128)S(1)} %get-tuple-element.462, pred[512,1024]{1,0:T(8,128)(4,1)S(1)} %fusion.298, bf16[1024,3,3,64]{0,3,2,1:T(8,128)(2,1)S(1)} %dynamic-slice_bitcast_fusion.28), kind=kOutput, calls=%fused_computation.99.clone.1.clone | convolution fusion | flops 218827264 | bytes 26820608 | tf_op jit(solution)/shard_map/while/body/eval_jaxpr/hqk,khd->qhd/dot_general | solution.py:82
  866.6 6.4 fusion.307
  872.9 6.4 fusion.304
  880.4 2.8 fusion.301
  883.2 3.7 fusion.302
  886.9 14.6 %fusion.305 = bf16[1,1024,1,3,64]{1,4,3,2,0:T(8,128)(2,1)} fusion(f32[3,512,1024]{2,1,0:T(8,128)} %fusion.302, f32[3,512,1024]{2,1,0:T(8,128)} %copy-done, f32[3,512]{1,0:T(4,128)S(1)} %get-tuple-element.462, pred[512,1024]{1,0:T(8,128)(4,1)S(1)} %fusion.298, f32[512,3,64]{0,2,1:T(8,128)} %fusion.304, ...), kind=kOutput, calls=%fused_computation.87.clone.1.clone | convolution fusion | flops 219220480 | bytes 27213824 | tf_op jit(solution)/shard_map/while/body/eval_jaxpr/hqk,qhd->khd/dot_general | solution.py:86
  901.5 13.7 %fusion.306 = bf16[512,3,64]{0,2,1:T(8,128)(2,1)} fusion(f32[3,512,1024]{2,1,0:T(8,128)} %fusion.302, f32[3,512,1024]{2,1,0:T(8,128)} %copy-done, f32[3,512]{1,0:T(4,128)S(1)} %get-tuple-element.462, pred[512,1024]{1,0:T(8,128)(4,1)S(1)} %fusion.298, bf16[1024,3,3,64]{0,3,2,1:T(8,128)(2,1)S(1)} %dynamic-slice_bitcast_fusion.28), kind=kOutput, calls=%fused_computation.99.clone.1.clone | convolution fusion | flops 218827264 | bytes 26820608 | tf_op jit(solution)/shard_map/while/body/eval_jaxpr/hqk,khd->qhd/dot_general | solution.py:82
  918.8 8.2 copy.95
  927.0 8.9 reshape.541
  935.9 6.2 convolution_bitcast_fusion.1
  942.2 9.7 fusion.154
  952.0 10.4 convolution_bitcast_fusion
  967.2 3.1 convert_reduce_fusion.1
  970.6 34.4 %reduce-scatter.25.cloned.1.call-done = f32[96,192]{1,0:T(8,128)} async-done(((f32[768,192]{1,0:T(8,128)}), f32[96,192]{1,0:T(8,128)}) %reduce-scatter.25.cloned.1.call-update) | async-done | bytes 73744
  1006.6 69.9 %reduce-scatter.19.cloned.1.call-done = f32[96,3,192]{2,0,1:T(8,128)} async-done(((f32[768,3,192]{2,0,1:T(8,128)}), f32[96,3,192]{2,0,1:T(8,128)}) %reduce-scatter.19.cloned.1.call-update) | async-done | bytes 221200 | tf_op jit(solution)/shard_map/reduce_scatter | solution.py:291
  1080.8 96.3 %reduce-scatter.17.cloned.1.call-done = f32[1024,768]{1,0:T(8,128)} async-done(((f32[4096,768]{1,0:T(8,128)}), f32[1024,768]{1,0:T(8,128)}) %reduce-scatter.17.cloned.1.call-update) | async-done | bytes 3145744 | tf_op jit(solution)/shard_map/reduce_scatter | solution.py:257
  1177.1 2.9 fusion.180
  1183.0 2.7 convert_reduce_fusion.3
  1186.6 40.2 %all-reduce.2 = (f32[2,768]{1,0:T(2,128)S(1)}, f32[3072]{0:T(1024)S(1)}, f32[6,768]{1,0:T(8,128)S(1)}) all-reduce(f32[2,768]{1,0:T(2,128)} %copy-done.41, f32[3072]{0:T(1024)S(1)} %dynamic_update_slice.23, f32[6,768]{1,0:T(8,128)S(1)} %stack.35), channel_id=1, replica_groups=mesh['dp'=8,'mp'=4] {'dp','mp'}, use_global_device_ids=true, to_apply=%region_31.32 | all-reduce | flops 9216 | bytes 73728 | tf_op jit(solution)/shard_map/psum | solution.py:285
  1230.7 41.1 %psum.31 = f32[]{:T(128)} all-reduce(f32[]{:T(128)S(6)} %add.374), channel_id=1, replica_groups=mesh['dp'=8,'mp'=4] {'dp','mp'}, use_global_device_ids=true, to_apply=%region_44.45 | all-reduce | flops 1 | bytes 8 | tf_op jit(solution)/shard_map/psum | solution.py:306
  (348 shorter events, 160.7 us)
Async XLA Ops:
  8.0 5.2 copy-start.2
  8.0 4.6 copy-start.34
  8.0 80.4 %all-gather.7.cloned.1.call-start = ((), (), s32[]{:S(2)}) async-start(), calls=%async_computation.8 | async-start | bytes 7864320 | tf_op jit(solution)/shard_map/all_gather | solution.py:191
  9.9 5.1 copy-start.30
  9.9 5.2 copy-start.22
  9.9 5.9 copy-start.13
  12.6 2.5 copy-start.35
  13.2 1.9 copy-start.32
  15.0 73.3 %copy-start.45 = (f32[2,192]{1,0:T(2,128)S(1)}, f32[2,192]{1,0:T(2,128)}, u32[]{:S(2)}) copy-start(f32[2,192]{1,0:T(2,128)} %param.48) | copy-start | bytes 4612
  15.0 255.8 %reduce-scatter.11.cloned.1.call-start = ((), (), s32[]{:S(2)}) async-start(), calls=%async_computation.9 | async-start | bytes 15728640 | tf_op jit(solution)/shard_map/reduce_scatter | solution.py:204
  107.3 6.1 copy-start.47
  172.2 106.4 %all-gather.11.cloned.1.call-start = ((), (), s32[]{:S(2)}) async-start(), calls=%async_computation.11 | async-start | bytes 1327104 | tf_op jit(solution)/shard_map/all_gather | solution.py:178
  173.9 148.5 %all-gather.9.cloned.1.call-start = ((), (), s32[]{:S(2)}) async-start(), calls=%async_computation.10 | async-start | bytes 7864320 | tf_op jit(solution)/shard_map/all_gather | solution.py:213
  276.1 90.5 %all-gather.13.cloned.1.call-start = ((), (), s32[]{:S(2)}) async-start(), calls=%async_computation.12 | async-start | bytes 1327104 | tf_op jit(solution)/shard_map/all_gather | solution.py:179
  277.8 135.1 %all-gather.15.cloned.1.call-start = ((), (), s32[]{:S(2)}) async-start(), calls=%async_computation.14 | async-start | bytes 7864320 | tf_op jit(solution)/shard_map/all_gather | solution.py:214
  278.6 263.7 %reduce-scatter.15.cloned.1.call-start = ((), (), s32[]{:S(2)}) async-start(), calls=%async_computation.15 | async-start | bytes 15728640 | tf_op jit(solution)/shard_map/reduce_scatter | solution.py:233
  412.9 22.2 %copy-start.49 = (bf16[768,768]{1,0:T(8,128)(2,1)S(1)}, bf16[768,768]{1,0:T(8,128)(2,1)}, u32[]{:S(2)}) copy-start(bf16[768,768]{1,0:T(8,128)(2,1)} %all-gather.11.cloned.1.call-done) | copy-start | bytes 3538948
  432.4 2.7 copy-start.50
  443.2 159.9 %reduce-scatter.13.cloned.1.call-start = ((), (), s32[]{:S(2)}) async-start(), calls=%async_computation.13 | async-start | bytes 7864320 | tf_op jit(solution)/shard_map/reduce_scatter | solution.py:220
  453.1 204.2 %all-gather.17.cloned.1.call-start = ((), (), s32[]{:S(2)}) async-start(), calls=%async_computation.16 | async-start | bytes 7864320 | tf_op jit(solution)/shard_map/all_gather | solution.py:241
  603.1 6.1 copy-start.7
  607.5 1.7 copy-start.5
  607.5 1.7 copy-start.39
  610.8 10.2 copy-start.48
  610.8 352.5 %reduce-scatter.21.cloned.1.call-start = ((), (), s32[]{:S(2)}) async-start(), calls=%async_computation.19 | async-start | bytes 2654208 | tf_op jit(solution)/shard_map/reduce_scatter | solution.py:293
  621.0 344.0 %reduce-scatter.23.cloned.1.call-start = ((), (), s32[]{:S(2)}) async-start(), calls=%async_computation.20 | async-start | bytes 2654208 | tf_op jit(solution)/shard_map/reduce_scatter | solution.py:294
  631.4 373.6 %reduce-scatter.25.cloned.1.call-start = ((), (), s32[]{:S(2)}) async-start(), calls=%async_computation.21 | async-start | bytes 884736
  692.2 2.8 copy-start
  713.3 13.7 %copy-start.12 = (bf16[512,3,64]{0,2,1:T(8,128)(2,1)S(1)}, bf16[512,3,64]{0,2,1:T(8,128)(2,1)}, u32[]{:S(2)}) copy-start(bf16[512,3,64]{0,2,1:T(8,128)(2,1)} %fusion.307) | copy-start | bytes 589828 | tf_op jit(solution)/shard_map/while
  755.0 2.8 copy-start
  776.1 13.7 %copy-start.12 = (bf16[512,3,64]{0,2,1:T(8,128)(2,1)S(1)}, bf16[512,3,64]{0,2,1:T(8,128)(2,1)}, u32[]{:S(2)}) copy-start(bf16[512,3,64]{0,2,1:T(8,128)(2,1)} %fusion.307) | copy-start | bytes 589828 | tf_op jit(solution)/shard_map/while
  817.7 2.8 copy-start
  838.8 13.7 %copy-start.12 = (bf16[512,3,64]{0,2,1:T(8,128)(2,1)S(1)}, bf16[512,3,64]{0,2,1:T(8,128)(2,1)}, u32[]{:S(2)}) copy-start(bf16[512,3,64]{0,2,1:T(8,128)(2,1)} %fusion.307) | copy-start | bytes 589828 | tf_op jit(solution)/shard_map/while
  880.4 2.8 copy-start
  901.5 13.7 %copy-start.12 = (bf16[512,3,64]{0,2,1:T(8,128)(2,1)S(1)}, bf16[512,3,64]{0,2,1:T(8,128)(2,1)}, u32[]{:S(2)}) copy-start(bf16[512,3,64]{0,2,1:T(8,128)(2,1)} %fusion.307) | copy-start | bytes 589828 | tf_op jit(solution)/shard_map/while
  927.0 8.9 copy-start.11
  942.2 9.8 copy-start.21
  942.2 134.4 %reduce-scatter.19.cloned.1.call-start = ((), (), s32[]{:S(2)}) async-start(), calls=%async_computation.18 | async-start | bytes 2654208 | tf_op jit(solution)/shard_map/reduce_scatter | solution.py:291
  951.9 225.1 %reduce-scatter.17.cloned.1.call-start = ((), (), s32[]{:S(2)}) async-start(), calls=%async_computation.17 | async-start | bytes 15728640 | tf_op jit(solution)/shard_map/reduce_scatter | solution.py:257
  962.4 4.2 copy-start.43
  962.4 4.2 copy-start.42
  962.5 214.6 %copy-start.3 = (bf16[1024,768]{1,0:T(8,128)(2,1)S(1)}, bf16[1024,768]{1,0:T(8,128)(2,1)}, u32[]{:S(2)}) copy-start(bf16[1024,768]{1,0:T(8,128)(2,1)} %param.40) | copy-start | bytes 4718596
  962.5 214.6 %copy-start.31 = (f32[1024]{0:T(1024)S(1)}, f32[1024]{0:T(1024)}, u32[]{:S(2)}) copy-start(f32[1024]{0:T(1024)} %copy-done.30) | copy-start | bytes 12292
  962.5 214.6 %copy-start.33 = (f32[768]{0:T(1024)S(1)}, f32[768]{0:T(1024)}, u32[]{:S(2)}) copy-start(f32[768]{0:T(1024)} %copy-done.32) | copy-start | bytes 9220
  970.2 210.4 %copy-start.38 = (f32[1024]{0:T(1024)S(1)}, f32[1024]{0:T(1024)}, u32[]{:S(2)}) copy-start(f32[1024]{0:T(1024)} %copy-done.37) | copy-start | bytes 12292
  970.2 210.4 %copy-start.36 = (f32[1024]{0:T(1024)S(1)}, f32[1024]{0:T(1024)}, u32[]{:S(2)}) copy-start(f32[1024]{0:T(1024)} %copy-done.35) | copy-start | bytes 12292
  970.6 206.4 %copy-start.41 = (f32[2,768]{1,0:T(2,128)}, f32[2,768]{1,0:T(2,128)S(1)}, u32[]{:S(2)}) copy-start(f32[2,768]{1,0:T(2,128)S(1)} %dynamic_update_slice.22) | copy-start | bytes 18436
  1177.1 3.6 copy-start.4
  1180.0 2.9 copy-start.6
  1180.0 2.9 copy-start.8
  1180.0 2.9 copy-start.40
  1183.0 93.8 %copy-start.23 = (f32[192,96]{1,0:T(8,128)S(1)}, f32[192,96]{1,0:T(8,128)}, u32[]{:S(2)}) copy-start(f32[192,96]{1,0:T(8,128)} %param.44) | copy-start | bytes 221188
  1183.0 95.5 %copy-start.14 = (f32[96,3,192]{2,0,1:T(8,128)S(1)}, f32[96,3,192]{2,0,1:T(8,128)}, u32[]{:S(2)}) copy-start(f32[96,3,192]{2,0,1:T(8,128)} %param.43) | copy-start | bytes 663556
  1183.0 95.5 %copy-start.20 = (f32[96,3,192]{2,0,1:T(8,128)S(1)}, f32[96,3,192]{2,0,1:T(8,128)}, u32[]{:S(2)}) copy-start(f32[96,3,192]{2,0,1:T(8,128)} %reduce-scatter.19.cloned.1.call-done) | copy-start | bytes 663556
  1183.0 95.5 %copy-start.24 = (f32[96,3,192]{2,0,1:T(8,128)S(1)}, f32[96,3,192]{2,0,1:T(8,128)}, u32[]{:S(2)}) copy-start(f32[96,3,192]{2,0,1:T(8,128)} %param.57) | copy-start | bytes 663556
  1183.0 95.5 %copy-start.25 = (f32[96,3,192]{2,0,1:T(8,128)S(1)}, f32[96,3,192]{2,0,1:T(8,128)}, u32[]{:S(2)}) copy-start(f32[96,3,192]{2,0,1:T(8,128)} %param.50) | copy-start | bytes 663556
  1185.7 93.9 %copy-start.16 = (f32[96,768]{1,0:T(8,128)S(1)}, f32[96,768]{1,0:T(8,128)}, u32[]{:S(2)}) copy-start(f32[96,768]{1,0:T(8,128)} %param.45) | copy-start | bytes 884740
  1185.7 93.9 %copy-start.18 = (f32[96,768]{1,0:T(8,128)S(1)}, f32[96,768]{1,0:T(8,128)}, u32[]{:S(2)}) copy-start(f32[96,768]{1,0:T(8,128)} %reduce-scatter.21.cloned.1.call-done) | copy-start | bytes 884740
  1185.7 93.9 %copy-start.26 = (f32[96,768]{1,0:T(8,128)S(1)}, f32[96,768]{1,0:T(8,128)}, u32[]{:S(2)}) copy-start(f32[96,768]{1,0:T(8,128)} %param.59) | copy-start | bytes 884740
  1185.7 93.9 %copy-start.27 = (f32[96,768]{1,0:T(8,128)S(1)}, f32[96,768]{1,0:T(8,128)}, u32[]{:S(2)}) copy-start(f32[96,768]{1,0:T(8,128)} %param.52) | copy-start | bytes 884740
  1185.7 94.9 %copy-start.17 = (f32[768,96]{0,1:T(8,128)S(1)}, f32[768,96]{0,1:T(8,128)}, u32[]{:S(2)}) copy-start(f32[768,96]{0,1:T(8,128)} %param.46) | copy-start | bytes 884740
  1185.7 94.9 %copy-start.19 = (f32[768,96]{0,1:T(8,128)S(1)}, f32[768,96]{0,1:T(8,128)}, u32[]{:S(2)}) copy-start(f32[768,96]{0,1:T(8,128)} %reduce-scatter.23.cloned.1.call-done) | copy-start | bytes 884740
  1185.7 94.9 %copy-start.28 = (f32[768,96]{0,1:T(8,128)S(1)}, f32[768,96]{0,1:T(8,128)}, u32[]{:S(2)}) copy-start(f32[768,96]{0,1:T(8,128)} %param.60) | copy-start | bytes 884740
  1272.5 8.1 copy-start.29
  (13 other events, 14.7 us)
Sparse Core Ops, SparseCore 0:
  15.1 49.0 all-gather.6
  172.4 98.4 reduce-scatter.10
  610.9 46.3 all-gather.16
Sparse Core Ops, SparseCore 1:
  175.5 40.9 all-gather.10
  276.2 46.2 all-gather.8
  325.1 41.5 all-gather.12
  368.2 44.7 all-gather.14
  443.3 98.9 reduce-scatter.14
  544.8 58.2 reduce-scatter.12
  621.1 69.1 reduce-scatter.20
  693.9 68.3 reduce-scatter.22
  942.2 62.7 reduce-scatter.24
  1008.5 68.0 reduce-scatter.18
  1079.0 98.0 reduce-scatter.16
where the time goes:
time: 1300 us; the launch traced here: 1290 us
  waiting for transfers between devices  594 us (46%)
  matrix products  346 us (27%)
  blocking collectives  151 us (12%)
  other arithmetic  96.2 us (7%)
  local copies, waits for them, and re-layouts  77.1 us (6%)
  between operations  22.8 us (2%)
    reduce_scatter x1, waiting for transfers between devices, shards(): lax.psum_scatter(jnp.dot(row_piece, wide_output, preferred_element_type=j...  96.9 us
    reduce_scatter x1, waiting for transfers between devices, shards(): lax.psum_scatter(jnp.einsum('tce,dce->td', row_piece, wide_input, preferr...  96.3 us
    reduce_scatter x1, waiting for transfers between devices, shards(): lax.psum_scatter(jnp.einsum('tf,df->td', row_piece, wide_expand, preferre...  89.1 us
    dot_general x8, matrix products, backward_block(): jnp.einsum('hqk,qhd->khd', score_grad, queries, preferred_element_type=jn...  84.3 us
    dot_general x8, matrix products, backward_block(): jnp.einsum('hqk,khd->qhd', score_grad, key_rows, preferred_element_type=j...  80.2 us
    reduce_scatter x1, waiting for transfers between devices, shards(): lax.psum_scatter(grad_input, 'dp', scatter_dimension=0, tiled=True)  69.9 us
    reduce_scatter x1, waiting for transfers between devices, shards(): lax.psum_scatter(jnp.dot(row_piece, wide_shrink, preferred_element_type=j...  56.8 us
    all_gather x1, waiting for transfers between devices, shards(): lax.all_gather(cotangent, 'mp', axis=0, tiled=True)  46.3 us
  transfers between devices with their start and end apart: 14, of which 10 were waited for; matrix products, arithmetic and copies ran while one was open for 28% of the time, Pallas kernels for 0%

commit v1 on v0

--- a/solution.py
+++ b/solution.py
@@ -118,12 +118,64 @@
     return jnp.stack([query_all, key_sum, value_sum], axis=1).astype(jnp.bfloat16)
 
 
-def attend_bundle(bundle):
-    return attend_forward(bundle[0], bundle[1])
-
-
-def backward_bundle(bundle):
-    return attend_backward(bundle[0], bundle[1], bundle[2], bundle[3])
+CORE_ORDERS = ((4, 3, 2, 1), (1, 4, 3, 2))
+
+
+def flat_index():
+    return lax.axis_index("dp") * lax.axis_size("mp") + lax.axis_index("mp")
+
+
+def cube_permute(values, stage):
+    pairs = []
+    for device in range(32):
+        pairs.append((device, device ^ (1 << CORE_ORDERS[device & 1][stage])))
+    return lax.ppermute(values, ("dp", "mp"), pairs)
+
+
+def twin_permute(values):
+    return lax.ppermute(values, ("dp", "mp"), [(device, device ^ 1) for device in range(32)])
+
+
+def place(relative, core):
+    spots = []
+    for order in CORE_ORDERS:
+        spots.append(sum(((relative >> bit) & 1) << step for step, bit in enumerate(order)))
+    return jnp.where(core == 0, spots[0], spots[1])
+
+
+def gather_blocks(shard):
+    count = lax.axis_size("dp") * lax.axis_size("mp")
+    if count != 32:
+        first = lax.all_gather(shard, ("dp", "mp"), axis=0, tiled=False)
+        return first
+    held = shard[None]
+    for stage in range(4):
+        held = jnp.concatenate([held, cube_permute(held, stage)], axis=0)
+    both = jnp.concatenate([held, twin_permute(held)], axis=0)
+    me = flat_index()
+    core = me & 1
+    distance = jnp.arange(32) ^ me
+    other = distance & 1
+    index = place(distance, core ^ other) + 16 * other
+    return jnp.take(both, index, axis=0)
+
+
+def scatter_blocks(blocks):
+    count = lax.axis_size("dp") * lax.axis_size("mp")
+    if count != 32:
+        return lax.psum_scatter(blocks, ("dp", "mp"), scatter_dimension=0, tiled=False)
+    me = flat_index()
+    core = me & 1
+    devices = jnp.arange(32)
+    distance = devices ^ me
+    spots = place(distance, core ^ (distance & 1)) + 16 * (distance & 1)
+    index = jnp.zeros((32,), jnp.int32).at[spots].set(devices)
+    sorted_blocks = jnp.take(blocks, index, axis=0)
+    held = sorted_blocks[:16] + twin_permute(sorted_blocks[16:])
+    for stage in reversed(range(4)):
+        half = 1 << stage
+        held = held[:half] + cube_permute(held[half:], stage)
+    return held[0]
 
 
 def adam_step(weight, gradient, first_old, second_old, factor, step_rate):
@@ -166,112 +218,112 @@
     second_head,
     second_bias,
 ):
-    lowered = (
-        input_weight.astype(jnp.bfloat16),
-        output_weight.astype(jnp.bfloat16),
-        expand_weight.astype(jnp.bfloat16),
-        shrink_weight.astype(jnp.bfloat16),
-    )
-    wide_input, wide_output, wide_expand, wide_shrink = (
-        lax.all_gather(lowered[0], "dp", axis=0, tiled=True),
-        lax.all_gather(lowered[1], "dp", axis=1, tiled=True),
-        lax.all_gather(lowered[2], "dp", axis=0, tiled=True),
-        lax.all_gather(lowered[3], "dp", axis=1, tiled=True),
-    )
-    own_rows = tokens.shape[0]
-    model_count = lax.axis_size("mp")
+    dp_count = lax.axis_size("dp")
+    mp_count = lax.axis_size("mp")
+    count = dp_count * mp_count
+    rows = input_weight.shape[0]
+    width = input_weight.shape[2]
+    hidden = expand_weight.shape[1]
+    depth = tokens.shape[1]
+    seq_length = tokens.shape[0]
     model_index = lax.axis_index("mp")
-    head_width = head_bias.shape[1]
-    bias_width = expand_bias.shape[0]
+    low = jnp.bfloat16
+    packed_shard = jnp.concatenate(
+        [
+            input_weight.astype(low).reshape(rows, 3 * width),
+            output_weight.astype(low).T,
+            expand_weight.astype(low),
+            shrink_weight.astype(low).T,
+        ],
+        axis=1,
+    )
+    columns = packed_shard.shape[1]
+    gathered = gather_blocks(packed_shard).reshape(dp_count, mp_count, rows, columns)
+    wide_input = (
+        gathered[..., : 3 * width]
+        .reshape(dp_count, mp_count, rows, 3, width)
+        .transpose(0, 2, 3, 1, 4)
+        .reshape(depth, 3, mp_count * width)
+    )
+
+    def wide(first, last):
+        piece = gathered[..., first:last]
+        return piece.transpose(0, 2, 1, 3).reshape(depth, mp_count * (last - first))
+
+    output_t = wide(3 * width, 4 * width)
+    wide_expand = wide(4 * width, 4 * width + hidden)
+    shrink_t = wide(4 * width + hidden, columns)
+
+    local_length = lax.dynamic_index_in_dim(lengths, model_index, 0, keepdims=False)
     residual = tokens.astype(jnp.float32)
     back_rows = cotangent.astype(jnp.float32)
     norm_one, pull_one = jax.vjp(layer_norm, residual, layer_vectors[0], layer_vectors[1])
-    seq_count = lengths.shape[0]
-    head_count = wide_input.shape[2] // HEAD_DIM
-    normed = lax.all_gather(norm_one.astype(jnp.bfloat16), "mp", axis=0, tiled=True)
-    row_total = normed.shape[0]
-    seq_length = row_total // seq_count
+    normed = norm_one.astype(low)
     projected = jnp.einsum("td,dce->tce", normed, wide_input, preferred_element_type=jnp.float32)
-    bias_rows = jnp.stack([head_bias[0], jnp.zeros_like(head_bias[0]), head_bias[1]])
-    packed = (
-        (projected + bias_rows[None])
-        .astype(jnp.bfloat16)
-        .reshape(seq_count, seq_length, 3, head_count, HEAD_DIM)
-    )
-    mixture, log_totals = lax.map(attend_bundle, (packed, lengths))
-    mixture_flat = mixture.reshape(row_total, head_count * HEAD_DIM)
-    row_piece = lax.slice_in_dim(mixture_flat, 0, lax.axis_size("mp") * own_rows, axis=0)
-    attended = lax.psum_scatter(
-        jnp.dot(row_piece, wide_output, preferred_element_type=jnp.float32),
-        "mp",
-        scatter_dimension=0,
-        tiled=True,
-    )
+    full_head = lax.all_gather(head_bias, "mp", axis=1, tiled=True)
+    full_bias = lax.all_gather(expand_bias, "mp", axis=0, tiled=True)
+    bias_rows = jnp.stack([full_head[0], jnp.zeros_like(full_head[0]), full_head[1]])
+    head_count = depth // HEAD_DIM
+    packed = (projected + bias_rows[None]).astype(low).reshape(seq_length, 3, head_count, HEAD_DIM)
+    mixture, log_totals = attend_forward(packed, local_length)
+    mixture_flat = mixture.reshape(seq_length, depth)
+    attended = jnp.einsum("tc,dc->td", mixture_flat, output_t, preferred_element_type=jnp.float32)
     middle = residual + attended + layer_vectors[4]
     norm_two, pull_two = jax.vjp(layer_norm, middle, layer_vectors[2], layer_vectors[3])
-    hidden_in, upstream = (
-        lax.all_gather(norm_two.astype(jnp.bfloat16), "mp", axis=0, tiled=True),
-        lax.all_gather(cotangent, "mp", axis=0, tiled=True),
-    )
-    pre_act = jnp.dot(hidden_in, wide_expand, preferred_element_type=jnp.float32) + expand_bias
+    hidden_in = norm_two.astype(low)
+    pre_act = jnp.dot(hidden_in, wide_expand, preferred_element_type=jnp.float32) + full_bias
     activation, pull_gelu = jax.vjp(gelu_tanh, pre_act)
-    activation = activation.astype(jnp.bfloat16)
-    row_piece = lax.slice_in_dim(activation, 0, own_rows * lax.axis_size("mp"), axis=0)
-    shrunk = lax.psum_scatter(
-        jnp.dot(row_piece, wide_shrink, preferred_element_type=jnp.float32).astype(jnp.bfloat16),
-        "mp",
-        scatter_dimension=0,
-        tiled=True,
-    ).astype(jnp.float32)
-    block_out = (middle + shrunk + layer_vectors[5]).astype(jnp.bfloat16)
-    grad_shrink = jnp.einsum("tf,td->fd", activation, upstream, preferred_element_type=jnp.float32)
-    act_grad = jnp.einsum("td,fd->tf", upstream, wide_shrink, preferred_element_type=jnp.float32)
-    pre_grad = pull_gelu(act_grad)[0].astype(jnp.bfloat16)
+    activation = activation.astype(low)
+    shrunk = jnp.einsum("tf,df->td", activation, shrink_t, preferred_element_type=jnp.float32)
+    block_out = (middle + shrunk + layer_vectors[5]).astype(low)
+    grad_shrink_t = jnp.einsum("td,tf->df", cotangent, activation, preferred_element_type=jnp.float32)
+    act_grad = jnp.dot(cotangent, shrink_t, preferred_element_type=jnp.float32)
+    pre_grad = pull_gelu(act_grad)[0].astype(low)
     grad_expand = jnp.einsum("td,tf->df", hidden_in, pre_grad, preferred_element_type=jnp.float32)
-    expand_bias_grad = jnp.sum(pre_grad.astype(jnp.float32), axis=0)
-    row_piece = lax.slice_in_dim(pre_grad, 0, lax.axis_size("mp") * own_rows, axis=0)
-    norm_two_grad = lax.psum_scatter(
-        jnp.einsum("tf,df->td", row_piece, wide_expand, preferred_element_type=jnp.float32),
-        "mp",
-        scatter_dimension=0,
-        tiled=True,
-    )
+    bias_grad = jnp.sum(pre_grad.astype(jnp.float32), axis=0)
+    norm_two_grad = jnp.einsum("tf,df->td", pre_grad, wide_expand, preferred_element_type=jnp.float32)
     middle_part, gain_two_grad, shift_two_grad = pull_two(norm_two_grad)
     middle_grad = back_rows + middle_part
-    attend_grad = lax.all_gather(middle_grad.astype(jnp.bfloat16), "mp", axis=0, tiled=True)
-    grad_output = jnp.einsum(
-        "tc,td->cd", mixture_flat, attend_grad, preferred_element_type=jnp.float32
-    )
-    mixture_grad = jnp.einsum(
-        "td,cd->tc", attend_grad, wide_output, preferred_element_type=jnp.float32
-    ).astype(jnp.bfloat16)
-    mixture_grad = mixture_grad.reshape(seq_count, seq_length, head_count, HEAD_DIM)
-    row_alive = (jnp.arange(seq_length)[None, :] < lengths[:, None])[:, :, None, None]
-    mixture_grad = jnp.where(row_alive, mixture_grad, jnp.zeros_like(mixture_grad))
-    packed_grad = lax.map(backward_bundle, (packed, mixture_grad, log_totals, lengths))
-    packed_grad = packed_grad.reshape(row_total, 3, head_count * HEAD_DIM)
+    attend_grad = middle_grad.astype(low)
+    grad_output_t = jnp.einsum("td,tc->dc", attend_grad, mixture_flat, preferred_element_type=jnp.float32)
+    mixture_grad = jnp.dot(attend_grad, output_t, preferred_element_type=jnp.float32).astype(low)
+    alive = (jnp.arange(seq_length) < local_length)[:, None]
+    mixture_grad = jnp.where(alive, mixture_grad, jnp.zeros_like(mixture_grad))
+    packed_grad = attend_backward(
+        packed, mixture_grad.reshape(seq_length, head_count, HEAD_DIM), log_totals, local_length
+    ).reshape(seq_length, 3, depth)
     grad_input = jnp.einsum("td,tce->dce", normed, packed_grad, preferred_element_type=jnp.float32)
     part_sums = jnp.sum(packed_grad.astype(jnp.float32), axis=0)
-    head_local = jnp.stack([part_sums[0], part_sums[2]])
-    row_piece = lax.slice_in_dim(packed_grad, 0, lax.axis_size("mp") * own_rows, axis=0)
-    norm_one_grad = lax.psum_scatter(
-        jnp.einsum("tce,dce->td", row_piece, wide_input, preferred_element_type=jnp.float32),
-        "mp",
-        scatter_dimension=0,
-        tiled=True,
-    )
-    head_full = lax.dynamic_update_slice(
-        jnp.zeros((2, head_width * model_count), jnp.float32),
-        head_local,
-        (0, model_index * head_width),
-    )
-    bias_full = lax.dynamic_update_slice(
-        jnp.zeros((bias_width * model_count,), jnp.float32),
-        expand_bias_grad,
-        (model_index * bias_width,),
-    )
+    head_grad = jnp.stack([part_sums[0], part_sums[2]])
+    norm_one_grad = jnp.einsum("tce,dce->td", packed_grad, wide_input, preferred_element_type=jnp.float32)
     input_part, gain_one_grad, shift_one_grad = pull_one(norm_one_grad)
-    token_grad = (middle_grad + input_part).astype(jnp.bfloat16)
+    token_grad = (middle_grad + input_part).astype(low)
+
+    def blocks(values):
+        return (
+            values.astype(low)
+            .reshape(dp_count, rows, mp_count, values.shape[1] // mp_count)
+            .transpose(0, 2, 1, 3)
+        )
+
+    grad_blocks = jnp.concatenate(
+        [
+            grad_input.astype(low)
+            .reshape(dp_count, rows, 3, mp_count, width)
+            .transpose(0, 3, 1, 2, 4)
+            .reshape(dp_count, mp_count, rows, 3 * width),
+            blocks(grad_output_t),
+            blocks(grad_expand),
+            blocks(grad_shrink_t),
+        ],
+        axis=3,
+    ).reshape(count, rows, columns)
+    own = scatter_blocks(grad_blocks).astype(jnp.float32)
+    input_total = own[:, : 3 * width].reshape(rows, 3, width)
+    output_total = own[:, 3 * width : 4 * width].T
+    expand_total = own[:, 4 * width : 4 * width + hidden]
+    shrink_total = own[:, 4 * width + hidden :].T
+
     vector_local = jnp.stack(
         [
             gain_one_grad,
@@ -283,27 +335,19 @@
         ]
     )
     vector_grad, head_summed, bias_summed = lax.psum(
-        (vector_local, head_full, bias_full), ("dp", "mp")
-    )
-    head_total = lax.dynamic_slice_in_dim(head_summed, model_index * head_width, head_width, 1)
-    bias_total = lax.dynamic_slice_in_dim(bias_summed, model_index * bias_width, bias_width, 0)
-    input_total, output_total, expand_total, shrink_total = (
-        lax.psum_scatter(grad_input, "dp", scatter_dimension=0, tiled=True),
-        lax.psum_scatter(grad_output, "dp", scatter_dimension=1, tiled=True),
-        lax.psum_scatter(grad_expand, "dp", scatter_dimension=0, tiled=True),
-        lax.psum_scatter(grad_shrink, "dp", scatter_dimension=1, tiled=True),
-    )
+        (vector_local, head_grad, bias_grad), ("dp", "mp")
+    )
+    head_total = lax.dynamic_slice_in_dim(head_summed, model_index * width, width, 1)
+    bias_total = lax.dynamic_slice_in_dim(bias_summed, model_index * hidden, hidden, 0)
     owned = (
         squares(input_total) + squares(output_total) + squares(expand_total) + squares(shrink_total)
     )
-    data_first = (lax.axis_index("dp") == 0).astype(jnp.float32)
-    model_first = (model_index == 0).astype(jnp.float32)
-    local_squares = (
-        owned
-        + data_first * (squares(head_total) + squares(bias_total))
-        + data_first * model_first * squares(vector_grad)
-    )
-    squared = lax.psum(local_squares, ("dp", "mp"))
+    squared = (
+        lax.psum(owned, ("dp", "mp"))
+        + squares(vector_grad)
+        + squares(head_summed)
+        + squares(bias_summed)
+    )
     grad_norm = jnp.sqrt(squared)
     factor = clip_norm / jnp.maximum(grad_norm, clip_norm)
     moment_input, square_input, updated_input = adam_step(

time: 1300 us -> 915 us (0.70)
  waiting for transfers between devices: 594 us -> 164 us
  local copies, waits for them, and re-layouts: 77.1 us -> 283 us
  blocking collectives: 151 us -> 60.3 us
  matrix products: 346 us -> 287 us
  starting transfers between devices: 0.6 us -> 15.4 us
  between operations: 22.8 us -> 8.54 us
    reduce_scatter x7 -> x0, waiting for transfers between devices: 409 us -> none  [the longest x1 96.9 us: shards(): lax.psum_scatter(jnp.dot(row_piece, wide_output, preferred_element_type=j...]
    ppermute x0 -> x10, waiting for transfers between devices: none -> 164 us  [the longest x8 153 us: cube_permute(): return lax.ppermute(values, ('dp', 'mp'), pairs)]
    all_gather x6 -> x0, waiting for transfers between devices: 150 us -> none  [the longest x1 46.3 us: shards(): lax.all_gather(cotangent, 'mp', axis=0, tiled=True)]
    all_gather x2, blocking collectives: 70.2 us -> 18.1 us  [the longest x1 12.1 us: shards(): full_head = lax.all_gather(head_bias, 'mp', axis=1, tiled=True)]
    transpose x0 -> x7, local copies, waits for them, and re-layouts: none -> 47.9 us  [the longest x5 36.5 us: wide(): return piece.transpose(0, 2, 1, 3).reshape(depth, mp_count * (last - first))]
    reshape x3 -> x10, local copies, waits for them, and re-layouts: 20.1 us -> 61.2 us  [the longest x5 29.4 us: blocks(): return values.astype(low).reshape(dp_count, rows, mp_count, values.shape[...]
    psum x2 -> x1, blocking collectives: 81.2 us -> 42.2 us  [shards(): lax.psum(owned, ('dp', 'mp')) + squares(vector_grad) + squares(head_summed)]
    concatenate x0 -> x5, local copies, waits for them, and re-layouts: none -> 38.8 us  [the longest x2 28.6 us: shards(): jnp.concatenate([grad_input.astype(low).reshape(dp_count, rows, 3, mp_cou...]
  transfers between devices with their start and end apart: 14 -> 10, of which waited for: 10 -> 8; matrix products, arithmetic and copies ran while one was open for 28% -> 7% of each run, Pallas kernels for 0% -> 0%
where the time goes in v1:
time: 915 us; the launch traced here: 907 us
  matrix products  287 us (31%)
  local copies, waits for them, and re-layouts  283 us (31%)
  waiting for transfers between devices  164 us (18%)
  other arithmetic  89.4 us (10%)
  blocking collectives  60.3 us (7%)
  starting transfers between devices  15.4 us (2%)
    ppermute x8, waiting for transfers between devices, cube_permute(): return lax.ppermute(values, ('dp', 'mp'), pairs)  153 us
    dot_general x2, matrix products, backward_block(): jnp.einsum('hqk,qhd->khd', score_grad, queries, preferred_element_type=jn...  68.2 us
    dot_general x2, matrix products, backward_block(): jnp.einsum('hqk,khd->qhd', score_grad, key_rows, preferred_element_type=j...  65.4 us
    unnamed x194, local copies, waits for them, and re-layouts  45.6 us
    psum x1, blocking collectives, shards(): lax.psum(owned, ('dp', 'mp')) + squares(vector_grad) + squares(head_summed)  42.2 us
    transpose x5, local copies, waits for them, and re-layouts, wide(): return piece.transpose(0, 2, 1, 3).reshape(depth, mp_count * (last - first))  36.5 us
    reshape x5, local copies, waits for them, and re-layouts, blocks(): return values.astype(low).reshape(dp_count, rows, mp_count, values.shape[...  29.4 us
    concatenate x2, local copies, waits for them, and re-layouts, shards(): jnp.concatenate([grad_input.astype(low).reshape(dp_count, rows, 3, mp_cou...  28.6 us
  transfers between devices with their start and end apart: 10, of which 8 were waited for; matrix products, arithmetic and copies ran while one was open for 7% of the time, Pallas kernels for 0%

profile of v1, /device:TPU:0, one launch (start us, length us, event | category | flops | bytes accessed | tf_op | source)
XLA Modules:
  0.0 907.4 jit_solution(7131694017853501870)
XLA Ops:
  5.1 4.1 collective-permute-start
  9.2 23.2 %collective-permute-done = bf16[1,96,2304]{2,1,0:T(8,128)(2,1)S(1)} collective-permute-done((bf16[1,96,2304]{2,1,0:T(8,128)(2,1)S(1)}, bf16[1,96,2304]{2,1,0:T(8,128)(2,1)S(1)}, u32[]{:S(2)}, u32[]{:S(2)}) %collective-permute-start) | collective-permute-done | bytes 442400 | tf_op jit(solution)/shard_map/ppermute | solution.py:132
  33.7 21.6 %collective-permute-done.1 = bf16[2,96,2304]{2,1,0:T(8,128)(2,1)S(1)} collective-permute-done((bf16[2,96,2304]{2,1,0:T(8,128)(2,1)S(1)}, bf16[2,96,2304]{2,1,0:T(8,128)(2,1)S(1)}, u32[]{:S(2)}, u32[]{:S(2)}) %collective-permute-start.1) | collective-permute-done | bytes 884768 | tf_op jit(solution)/shard_map/ppermute | solution.py:132
  57.4 27.9 %collective-permute-done.2 = bf16[4,96,2304]{2,1,0:T(8,128)(2,1)S(1)} collective-permute-done((bf16[4,96,2304]{2,1,0:T(8,128)(2,1)S(1)}, bf16[4,96,2304]{2,1,0:T(8,128)(2,1)S(1)}, u32[]{:S(2)}, u32[]{:S(2)}) %collective-permute-start.2) | collective-permute-done | bytes 1769504 | tf_op jit(solution)/shard_map/ppermute | solution.py:132
  92.9 34.2 %collective-permute-done.3 = bf16[8,96,2304]{2,1,0:T(8,128)(2,1)S(1)} collective-permute-done((bf16[8,96,2304]{2,1,0:T(8,128)(2,1)S(1)}, bf16[8,96,2304]{2,1,0:T(8,128)(2,1)S(1)}, u32[]{:S(2)}, u32[]{:S(2)}) %collective-permute-start.3) | collective-permute-done | bytes 3538976 | tf_op jit(solution)/shard_map/ppermute | solution.py:132
  127.1 3.7 constant_dynamic-update-slice_fusion
  130.9 12.1 %all-gather = f32[4,192,2]{1,2,0:T(2,128)S(1)} all-gather(f32[1,192,2]{1,2,0:T(2,128)S(1)} %bitcast.234), channel_id=1, replica_groups=mesh['dp'=8,'mp'=4] {'mp'}, dimensions={0}, use_global_device_ids=true | all-gather | bytes 7680 | tf_op jit(solution)/shard_map/all_gather | solution.py:263
  148.4 6.1 all-gather.1
  159.8 6.4 constant_dynamic-update-slice_fusion.5
  166.2 12.3 %gather_fusion = bf16[32,96,2304]{2,1,0:T(8,128)(2,1)} fusion(bf16[32,96,2304]{2,1,0:T(8,128)(2,1)} %constant_dynamic-update-slice_fusion.5, s32[1024]{0:T(1024)S(1)} %pad_clamp_fusion.1), kind=kCustom, calls=%fused_computation.clone | custom fusion | bytes 28311680 | tf_op jit(solution)/shard_map/jit(_take)/gather | solution.py:160
  178.5 10.7 %broadcast_select_fusion.1 = bf16[32,96,2304]{2,1,0:T(8,128)(2,1)} fusion(bf16[32,96,2304]{2,1,0:T(8,128)(2,1)} %gather_fusion, pred[32]{0:T(512)(128)(4,1)S(1)} %get-tuple-element.202), kind=kLoop, calls=%fused_computation.17 | loop fusion | flops 7077888 | bytes 28311584 | tf_op jit(solution)/shard_map/jit(_take)/select_n | solution.py:160
  189.2 21.3 %copy.130 = bf16[32,96,2304]{1,2,0:T(8,128)(2,1)} copy(bf16[32,96,2304]{2,1,0:T(8,128)(2,1)} %broadcast_select_fusion.1) | data formatting | bytes 28311552 | tf_op jit(solution)/shard_map/jit(_take)/select_n | solution.py:160
  215.0 12.0 %slice_bitcast_fusion.1 = (bf16[8,96,4,768]{1,3,2,0:T(8,128)(2,1)}, bf16[8,96,4,768]{1,3,2,0:T(8,128)(2,1)}) fusion(bf16[8,4,96,2304]{2,3,1,0:T(8,128)(2,1)} %bitcast.186), kind=kLoop, calls=%fused_computation.53 | loop fusion | bytes 18874368 | tf_op jit(solution)/shard_map/transpose | solution.py:251
  227.0 6.0 copy.131
  233.0 8.7 reshape.525
  241.8 6.0 add_convert_fusion
  254.6 5.5 fusion.95
  265.4 10.6 %copy.136 = bf16[8,96,4,768]{3,2,1,0:T(4,128)(2,1)} copy(bf16[8,96,4,768]{1,3,2,0:T(8,128)(2,1)} %get-tuple-element.204) | data formatting | bytes 9437184 | tf_op jit(solution)/shard_map/transpose | solution.py:251
  276.0 5.5 copy.182
  281.5 10.2 %copy.137 = bf16[8,96,4,768]{3,2,1,0:T(4,128)(2,1)} copy(bf16[8,96,4,768]{1,3,2,0:T(8,128)(2,1)} %get-tuple-element.205) | data formatting | bytes 9437184 | tf_op jit(solution)/shard_map/transpose | solution.py:251
  291.7 5.6 copy.183
  297.2 14.3 %fusion.4 = (f32[12,512]{1,0:T(8,128)S(1)}, f32[12,512,1024]{2,1,0:T(8,128)}) fusion(pred[512,1024]{1,0:T(8,128)(4,1)S(1)} %copy-done.19, bf16[1024,3,12,64]{0,3,2,1:T(8,128)(2,1)} %bitcast.202), kind=kOutput, calls=%fused_computation.15 | convolution fusion | flops 824174592 | bytes 28073984 | tf_op jit(solution)/shard_map/qhd,khd->hqk/dot_general | solution.py:34
  311.5 12.3 %fusion.3 = f32[12,512]{1,0:T(8,128)S(1)} fusion(f32[12,512,1024]{2,1,0:T(8,128)} %get-tuple-element.224, f32[12,512]{1,0:T(8,128)S(1)} %get-tuple-element.223, pred[512,1024]{1,0:T(8,128)(4,1)S(1)} %copy-done.19), kind=kLoop, calls=%fused_computation.12 | loop fusion | flops 25159680 | bytes 25739264 | tf_op jit(solution)/shard_map/reduce_sum | solution.py:47
  326.9 9.4 %fusion.99 = bf16[512,12,64]{0,2,1:T(8,128)(2,1)S(1)} fusion(f32[12,512,1024]{2,1,0:T(8,128)S(1)} %copy-done, f32[12,512]{1,0:T(8,128)S(1)} %fusion.3, f32[12,512]{1,0:T(8,128)S(1)} %get-tuple-element.223, pred[512,1024]{1,0:T(8,128)(4,1)S(1)} %copy-done.19, bf16[1024,3,12,64]{0,3,2,1:T(8,128)(2,1)} %bitcast.203, pred[512]{0:T(512)(128)(4,1)S(1)} %get-tuple-element.236), kind=kOutput, calls=%fused_computation.128 | convolution fusion | flops 837550080 | bytes 28099072 | tf_op jit(solution)/shard_map/hqk,khd->qhd/dot_general | solution.py:49
  340.0 5.6 fusion.154
  345.6 10.0 %fusion.64 = bf16[768,3072]{0,1:T(8,128)(2,1)} fusion(bf16[1024,768]{1,0:T(8,128)(2,1)S(1)} %copy-done.26, f32[1024,3072]{1,0:T(8,128)S(1)} %fusion.154, f32[3072]{0:T(1024)S(1)} %bitcast.231), kind=kOutput, calls=%fused_computation.79 | convolution fusion | flops 4865654784 | bytes 18886656 | tf_op jit(solution)/shard_map/td,tf->df/dot_general | solution.py:279
  355.5 16.2 %convert_reduce_fusion = (f32[3072]{0:T(1024)}, bf16[1024,3072]{1,0:T(8,128)(2,1)}) fusion(f32[1024,3072]{1,0:T(8,128)S(1)} %fusion.154, f32[3072]{0:T(1024)S(1)} %bitcast.232, bf16[1024,768]{1,0:T(8,128)(2,1)S(1)} %copy-done.26, bf16[768,3072]{1,0:T(8,128)(2,1)} %bitcast.218), kind=kOutput, calls=%fused_computation.30 | convolution fusion | flops 4904186880 | bytes 25190400 | tf_op jit(solution)/shard_map/dot_general | solution.py:280
  371.7 9.5 %fusion.170 = (f32[768]{0:T(1024)}, f32[1024,768]{1,0:T(8,128)}) fusion(bf16[1024,3072]{1,0:T(8,128)(2,1)} %get-tuple-element.234, bf16[768,3072]{1,0:T(8,128)(2,1)S(1)} %bitcast.193), kind=kOutput, calls=%fused_computation.266 | convolution fusion | flops 4832623616 | bytes 14158848 | tf_op jit(solution)/shard_map/tf,df->td/dot_general | solution.py:284
  381.2 7.2 convolution_convert_fusion.1
  388.5 3.7 copy.140
  392.1 3.5 multiply_reduce_fusion.2
  402.3 8.1 fusion.103
  410.5 3.9 fusion.81
  414.4 20.5 %fusion.92 = bf16[512,12,64]{0,2,1:T(8,128)(2,1)} fusion(f32[12,512,512]{1,2,0:T(8,128)} %fusion.103, f32[12,512,512]{1,2,0:T(8,128)} %copy-done.3, f32[12,512]{1,0:T(8,128)S(1)} %copy-done.54, pred[512,512]{0,1:T(8,128)(4,1)S(1)} %copy-done.24, bf16[1024,3,12,64]{0,3,2,1:T(8,128)(2,1)} %bitcast.205), kind=kOutput, calls=%fused_computation.125 | convolution fusion | flops 438049280 | bytes 52494336 | tf_op jit(solution)/shard_map/hqk,khd->qhd/dot_general | solution.py:82
  434.8 21.0 %multiply_bitcast_fusion = f32[512,12,64]{0,2,1:T(8,128)} fusion(f32[12,512,512]{1,2,0:T(8,128)} %fusion.103, f32[12,512,512]{1,2,0:T(8,128)} %copy-done.3, f32[12,512]{1,0:T(8,128)S(1)} %copy-done.54, pred[512,512]{0,1:T(8,128)(4,1)S(1)} %copy-done.24, bf16[1024,3,12,64]{0,3,2,1:T(8,128)(2,1)} %bitcast.206), kind=kOutput, calls=%fused_computation.115 | convolution fusion | flops 437656064 | bytes 53280768 | tf_op jit(solution)/shard_map/hqk,qhd->khd/dot_general | solution.py:86
  455.9 6.7 copy.152
  462.6 9.7 %reshape.534 = bf16[8,96,4,768]{3,2,1,0:T(4,128)(2,1)} reshape(bf16[768,3072]{1,0:T(8,128)(2,1)} %copy.152) | data formatting | bytes 9437184 | tf_op jit(solution)/shard_map/reshape | solution.py:305
  472.3 5.4 copy.153
  477.7 9.8 %reshape.533 = bf16[8,96,4,768]{3,2,1,0:T(4,128)(2,1)} reshape(bf16[768,3072]{1,0:T(8,128)(2,1)} %convolution_convert_fusion.1) | data formatting | bytes 9437184 | tf_op jit(solution)/shard_map/reshape | solution.py:305
  487.4 5.5 copy.151
  497.4 11.7 %fusion.90 = f32[12,512,1024]{2,1,0:T(8,128)} fusion(bf16[512,12,64]{0,2,1:T(8,128)(2,1)S(1)} %bitcast.214, bf16[1024,3,12,64]{0,3,2,1:T(8,128)(2,1)} %bitcast.207), kind=kOutput, calls=%fused_computation.123 | convolution fusion | flops 805306368 | bytes 27525120 | tf_op jit(solution)/shard_map/qhd,khd->hqk/dot_general | solution.py:75
  509.1 12.8 %fusion.73 = bf16[1024,12,64]{0,2,1:T(8,128)(2,1)} fusion(f32[512,12,64]{0,2,1:T(8,128)S(1)} %copy-done.76, bf16[512,12,64]{0,2,1:T(8,128)(2,1)S(1)} %bitcast.215, f32[12,512]{1,0:T(8,128)S(1)} %copy-done.53, f32[12,512,1024]{2,1,0:T(8,128)} %get-tuple-element.224, pred[512,1024]{1,0:T(8,128)(4,1)S(1)} %copy-done.20), kind=kOutput, calls=%fused_computation.93 | convolution fusion | flops 832045056 | bytes 29646848 | tf_op jit(solution)/shard_map/hqk,qhd->khd/dot_general | solution.py:89
  524.5 44.9 %fusion.96 = bf16[512,12,64]{0,2,1:T(8,128)(2,1)} fusion(f32[12,512,1024]{2,1,0:T(8,128)} %fusion.90, pred[512,1024]{1,0:T(8,128)(4,1)S(1)} %copy-done.20, f32[12,512]{1,0:T(8,128)S(1)} %copy-done.53, f32[12,512,1024]{2,1,0:T(8,128)} %get-tuple-element.224, bf16[1024,3,12,64]{0,3,2,1:T(8,128)(2,1)} %bitcast.208), kind=kOutput, calls=%fused_computation.127 | convolution fusion | flops 875305984 | bytes 104136704 | tf_op jit(solution)/shard_map/hqk,khd->qhd/dot_general | solution.py:82
  569.4 47.2 %fusion.74 = bf16[1024,12,64]{0,2,1:T(8,128)(2,1)} fusion(f32[512,12,64]{0,2,1:T(8,128)} %multiply_bitcast_fusion, f32[12,512,1024]{2,1,0:T(8,128)} %fusion.90, pred[512,1024]{1,0:T(8,128)(4,1)S(1)} %copy-done.20, f32[12,512]{1,0:T(8,128)S(1)} %copy-done.53, f32[12,512,1024]{2,1,0:T(8,128)} %get-tuple-element.224, bf16[1024,3,12,64]{0,3,2,1:T(8,128)(2,1)} %bitcast.209), kind=kOutput, calls=%fused_computation.95 | convolution fusion | flops 876878848 | bytes 105709568 | tf_op jit(solution)/shard_map/hqk,qhd->khd/dot_general | solution.py:86
  624.7 8.2 convolution_convert_fusion.2
  632.9 10.1 %reshape.531 = bf16[8,96,3,4,192]{4,3,1,0,2:T(4,128)(2,1)} reshape(bf16[768,3,768]{2,0,1:T(8,128)(2,1)} %convolution_convert_fusion.2) | data formatting | bytes 7077888 | tf_op jit(solution)/shard_map/reshape | solution.py:312
  643.0 9.7 %copy.149 = bf16[8,96,3,4,192]{1,4,2,3,0:T(8,128)(2,1)} copy(bf16[8,96,3,4,192]{4,3,1,0,2:T(4,128)(2,1)} %reshape.531) | data formatting | bytes 7077888 | tf_op jit(solution)/shard_map/reshape | solution.py:312
  652.7 7.2 copy.154
  659.9 21.4 %concatenate.63 = bf16[32,96,2304]{2,1,0:T(8,128)(2,1)} concatenate(bf16[32,96,576]{2,1,0:T(8,128)(2,1)} %copy.154, bf16[32,96,192]{2,1,0:T(8,128)(2,1)S(1)} %bitcast.216, bf16[32,96,768]{2,1,0:T(8,128)(2,1)} %bitcast.194, bf16[32,96,768]{2,1,0:T(8,128)(2,1)} %bitcast.189), dimensions={2} | concatenate | bytes 28311552 | tf_op jit(solution)/shard_map/concatenate | solution.py:309
  681.3 12.9 %gather_fusion.1 = bf16[32,96,2304]{2,1,0:T(8,128)(2,1)} fusion(bf16[32,96,2304]{2,1,0:T(8,128)(2,1)} %concatenate.63, s32[1024]{0:T(1024)} %pad_clamp_fusion), kind=kCustom, calls=%fused_computation.1.clone | custom fusion | bytes 28311680 | tf_op jit(solution)/shard_map/jit(_take)/gather | solution.py:173
  694.2 10.7 %broadcast_select_fusion = bf16[32,96,2304]{2,1,0:T(8,128)(2,1)} fusion(bf16[32,96,2304]{2,1,0:T(8,128)(2,1)} %gather_fusion.1, pred[32]{0:T(512)(128)(4,1)S(1)} %copy-done.74), kind=kLoop, calls=%fused_computation.16 | loop fusion | flops 7077888 | bytes 28311584 | tf_op jit(solution)/shard_map/jit(_take)/select_n | solution.py:173
  704.9 3.5 slice.257
  708.7 11.1 %collective-permute-done.5 = bf16[16,96,2304]{2,1,0:T(8,128)(2,1)} collective-permute-done((bf16[16,96,2304]{2,1,0:T(8,128)(2,1)S(1)}, bf16[16,96,2304]{2,1,0:T(8,128)(2,1)}, u32[]{:S(2)}, u32[]{:S(2)}) %collective-permute-start.5) | collective-permute-done | bytes 7077920 | tf_op jit(solution)/shard_map/ppermute | solution.py:136
  719.8 8.6 slice_add_fusion
  728.4 4.1 slice.259
  740.6 9.2 %fusion.169 = (f32[768]{0:T(1024)}, f32[1024,768]{1,0:T(8,128)}) fusion(bf16[768,3,768]{0,2,1:T(8,128)(2,1)} %reshape.525, bf16[1024,1,768]{2,0,1:T(8,128)(2,1)S(1)} %copy-done.15, bf16[1024,1,768]{2,0,1:T(8,128)(2,1)} %copy.145, bf16[1024,1,768]{2,0,1:T(8,128)(2,1)} %copy.144), kind=kOutput, calls=%fused_computation.265 | convolution fusion | flops 3629382912 | bytes 11406336 | tf_op jit(solution)/shard_map/tce,dce->td/dot_general | solution.py:298
  749.8 3.6 copy.148
  755.9 18.4 %collective-permute-done.6 = bf16[8,96,2304]{2,1,0:T(8,128)(2,1)} collective-permute-done((bf16[8,96,2304]{2,1,0:T(8,128)(2,1)}, bf16[8,96,2304]{2,1,0:T(8,128)(2,1)}, u32[]{:S(2)}, u32[]{:S(2)}) %collective-permute-start.6) | collective-permute-done | bytes 3538976 | tf_op jit(solution)/shard_map/ppermute | solution.py:132
  774.4 3.4 slice_add_fusion.1
  779.8 9.5 %add_convert_fusion.2 = bf16[1024,768]{0,1:T(8,128)(2,1)} fusion(f32[1024,768]{0,1:T(8,128)S(1)} %copy-done.6, bf16[768,3072]{1,0:T(8,128)(2,1)S(1)} %bitcast.221, f32[768]{0:T(1024)S(1)} %copy-done.66, f32[1024,3072]{1,0:T(8,128)} %copy-done.13, f32[3072]{0:T(1024)S(1)} %bitcast.233), kind=kOutput, calls=%fused_computation.99 | convolution fusion | flops 4865654784 | bytes 22035456 | tf_op jit(solution)/shard_map/tf,df->td/dot_general | solution.py:277
  789.3 11.2 %collective-permute-done.7 = bf16[4,96,2304]{2,1,0:T(8,128)(2,1)S(1)} collective-permute-done((bf16[4,96,2304]{2,1,0:T(8,128)(2,1)S(1)}, bf16[4,96,2304]{2,1,0:T(8,128)(2,1)S(1)}, u32[]{:S(2)}, u32[]{:S(2)}) %collective-permute-start.7) | collective-permute-done | bytes 1769504 | tf_op jit(solution)/shard_map/ppermute | solution.py:132
  802.2 3.8 convert_reduce_fusion.3
  806.1 16.1 %collective-permute-done.8 = bf16[2,96,2304]{2,1,0:T(8,128)(2,1)S(1)} collective-permute-done((bf16[2,96,2304]{2,1,0:T(8,128)(2,1)S(1)}, bf16[2,96,2304]{2,1,0:T(8,128)(2,1)S(1)}, u32[]{:S(2)}, u32[]{:S(2)}) %collective-permute-start.8) | collective-permute-done | bytes 884768 | tf_op jit(solution)/shard_map/ppermute | solution.py:132
  844.3 42.2 %all-reduce.2 = (f32[]{:T(128)}, f32[6,768]{1,0:T(8,128)S(1)}, f32[2,768]{1,0:T(2,128)S(1)}, f32[3072]{0:T(1024)S(1)}) all-reduce(f32[]{:T(128)S(6)} %add.490, f32[6,768]{1,0:T(8,128)S(1)} %stack.38, f32[2,768]{1,0:T(2,128)S(1)} %pad_maximum_fusion.7, f32[3072]{0:T(1024)} %get-tuple-element.233), channel_id=1, replica_groups=mesh['dp'=8,'mp'=4] {'dp','mp'}, use_global_device_ids=true, to_apply=%region_19.21 | all-reduce | flops 9217 | bytes 73736 | tf_op jit(solution)/shard_map/psum | solution.py:346
  (300 shorter events, 121.3 us)
Async XLA Ops:
  5.1 27.3 %collective-permute-start = (bf16[1,96,2304]{2,1,0:T(8,128)(2,1)S(1)}, bf16[1,96,2304]{2,1,0:T(8,128)(2,1)S(1)}, u32[]{:S(2)}, u32[]{:S(2)}) collective-permute-start(bf16[1,96,2304]{2,1,0:T(8,128)(2,1)S(1)} %bitcast.210), channel_id=1, source_target_pairs={{0,16},{1,3},{2,18},{3,1},{4,20},{5,7},{6,22},{7,5},{8,24},{9,11},... | collective-permute-start | bytes 1327112 | tf_op jit(solution)/shard_map/ppermute | solution.py:132
  32.4 22.9 %collective-permute-start.1 = (bf16[2,96,2304]{2,1,0:T(8,128)(2,1)S(1)}, bf16[2,96,2304]{2,1,0:T(8,128)(2,1)S(1)}, u32[]{:S(2)}, u32[]{:S(2)}) collective-permute-start(bf16[2,96,2304]{2,1,0:T(8,128)(2,1)S(1)} %pad_maximum_fusion.5), channel_id=1, source_target_pairs={{0,8},{1,17},{2,10},{3,19},{4,12},{5,21},{6,14},{7,23},{8,0},{9,25... | collective-permute-start | bytes 2654216 | tf_op jit(solution)/shard_map/ppermute | solution.py:132
  55.5 29.7 %collective-permute-start.2 = (bf16[4,96,2304]{2,1,0:T(8,128)(2,1)S(1)}, bf16[4,96,2304]{2,1,0:T(8,128)(2,1)S(1)}, u32[]{:S(2)}, u32[]{:S(2)}) collective-permute-start(bf16[4,96,2304]{2,1,0:T(8,128)(2,1)S(1)} %pad_maximum_fusion.2), channel_id=1, source_target_pairs={{0,4},{1,9},{2,6},{3,11},{4,0},{5,13},{6,2},{7,15},{8,12},{9,1},{1... | collective-permute-start | bytes 5308424 | tf_op jit(solution)/shard_map/ppermute | solution.py:132
  85.6 41.5 %collective-permute-start.3 = (bf16[8,96,2304]{2,1,0:T(8,128)(2,1)S(1)}, bf16[8,96,2304]{2,1,0:T(8,128)(2,1)S(1)}, u32[]{:S(2)}, u32[]{:S(2)}) collective-permute-start(bf16[8,96,2304]{2,1,0:T(8,128)(2,1)S(1)} %pad_maximum_fusion.1), channel_id=1, source_target_pairs={{0,2},{1,5},{2,0},{3,7},{4,6},{5,1},{6,4},{7,3},{8,10},{9,13},{10,... | collective-permute-start | bytes 10616840 | tf_op jit(solution)/shard_map/ppermute | solution.py:132
  127.1 15.9 %copy-start.25 = (bf16[1024,768]{1,0:T(8,128)(2,1)S(1)}, bf16[1024,768]{1,0:T(8,128)(2,1)}, u32[]{:S(2)}) copy-start(bf16[1024,768]{1,0:T(8,128)(2,1)} %param.38) | copy-start | bytes 4718596
  130.9 16.1 %copy-start.75 = (s32[4]{0:T(128)S(1)}, s32[4]{0:T(128)}, u32[]{:S(2)}) copy-start(s32[4]{0:T(128)} %param.40) | copy-start | bytes 52
  130.9 25.5 %copy-start.43 = (f32[6,768]{1,0:T(8,128)S(1)}, f32[6,768]{1,0:T(8,128)}, u32[]{:S(2)}) copy-start(f32[6,768]{1,0:T(8,128)} %param.45) | copy-start | bytes 55300
  130.9 28.9 %collective-permute-start.4 = (bf16[16,96,2304]{2,1,0:T(8,128)(2,1)}, bf16[16,96,2304]{2,1,0:T(8,128)(2,1)}, u32[]{:S(2)}, u32[]{:S(2)}) collective-permute-start(bf16[16,96,2304]{2,1,0:T(8,128)(2,1)} %get-tuple-element.207), channel_id=1, source_target_pairs={{0,1},{1,0},{2,3},{3,2},{4,5},{5,4},{6,7},{7,6},{8,9},{9,8},{10,11... | collective-permute-start | bytes 21233672 | tf_op jit(solution)/shard_map/ppermute | solution.py:136
  143.8 192.8 %copy-start.1 = (bf16[1024,768]{0,1:T(8,128)(2,1)}, bf16[1024,768]{0,1:T(8,128)(2,1)S(1)}, u32[]{:S(2)}) copy-start(bf16[1024,768]{0,1:T(8,128)(2,1)S(1)} %copy.126) | copy-start | bytes 4718596
  155.1 11.1 %copy-start.72 = (pred[1024]{0:T(1024)(128)(4,1)}, pred[1024]{0:T(1024)(128)(4,1)S(1)}, u32[]{:S(2)}) copy-start(pred[1024]{0:T(1024)(128)(4,1)S(1)} %iota_compare_fusion.2) | copy-start | bytes 3076
  157.0 84.7 %copy-start.45 = (f32[768]{0:T(1024)}, f32[768]{0:T(1024)S(1)}, u32[]{:S(2)}) copy-start(f32[768]{0:T(1024)S(1)} %get-tuple-element.173) | copy-start | bytes 9220
  157.0 84.7 %copy-start.67 = (f32[768]{0:T(1024)}, f32[768]{0:T(1024)S(1)}, u32[]{:S(2)}) copy-start(f32[768]{0:T(1024)S(1)} %get-tuple-element.172) | copy-start | bytes 9220
  157.8 83.9 %copy-start.41 = (f32[1024]{0:T(1024)}, f32[1024]{0:T(1024)S(1)}, u32[]{:S(2)}) copy-start(f32[1024]{0:T(1024)S(1)} %broadcast_multiply_fusion.1) | copy-start | bytes 12292
  158.3 83.4 %copy-start.47 = (f32[1024]{0:T(1024)}, f32[1024]{0:T(1024)S(1)}, u32[]{:S(2)}) copy-start(f32[1024]{0:T(1024)S(1)} %fusion.118) | copy-start | bytes 12292
  158.5 95.3 %copy-start.23 = (pred[512,512]{0,1:T(8,128)(4,1)}, pred[512,512]{0,1:T(8,128)(4,1)S(1)}, u32[]{:S(2)}) copy-start(pred[512,512]{0,1:T(8,128)(4,1)S(1)} %fusion.100) | copy-start | bytes 786436
  265.4 71.2 %copy-start.34 = (bf16[768,768]{0,1:T(8,128)(2,1)}, bf16[768,768]{0,1:T(8,128)(2,1)S(1)}, u32[]{:S(2)}) copy-start(bf16[768,768]{0,1:T(8,128)(2,1)S(1)} %reshape.528) | copy-start | bytes 3538948
  311.5 15.4 %copy-start = (f32[12,512,1024]{2,1,0:T(8,128)S(1)}, f32[12,512,1024]{2,1,0:T(8,128)}, u32[]{:S(2)}) copy-start(f32[12,512,1024]{2,1,0:T(8,128)} %get-tuple-element.224) | copy-start | bytes 75497472
  326.9 9.4 %copy-start.38 = (bf16[512,12,64]{0,2,1:T(8,128)(2,1)S(1)}, bf16[512,12,64]{0,2,1:T(8,128)(2,1)}, u32[]{:S(2)}) copy-start(bf16[512,12,64]{0,2,1:T(8,128)(2,1)} %fusion.95) | copy-start | bytes 2359300
  326.9 9.7 %copy-start.69 = (f32[768]{0:T(1024)S(1)}, f32[768]{0:T(1024)}, u32[]{:S(2)}) copy-start(f32[768]{0:T(1024)} %get-tuple-element.171) | copy-start | bytes 9220
  338.3 42.9 %copy-start.4 = (f32[1024,768]{0,1:T(8,128)}, f32[1024,768]{0,1:T(8,128)S(1)}, u32[]{:S(2)}) copy-start(f32[1024,768]{0,1:T(8,128)S(1)} %get-tuple-element.228) | copy-start | bytes 9437188
  345.5 10.0 %copy-start.13 = (f32[1024,3072]{1,0:T(8,128)}, f32[1024,3072]{1,0:T(8,128)S(1)}, u32[]{:S(2)}) copy-start(f32[1024,3072]{1,0:T(8,128)S(1)} %fusion.154) | copy-start | bytes 37748740
  371.7 9.5 %copy-start.77 = (bf16[1024,3072]{1,0:T(8,128)(2,1)S(1)}, bf16[1024,3072]{1,0:T(8,128)(2,1)}, u32[]{:S(2)}) copy-start(bf16[1024,3072]{1,0:T(8,128)(2,1)} %get-tuple-element.234) | copy-start | bytes 18874372
  400.7 9.7 %slice-start = ((s8[12582912]{0:T(1024)(128)(4,1)}), s8[4194304]{0:T(1024)(128)(4,1)S(1)}, s32[]{:S(2)}) async-start(s8[12582912]{0:T(1024)(128)(4,1)} %bitcast.187), calls=%async_computation | async-start | bytes 8388608
  400.7 9.7 %slice-start.1 = ((s8[12582912]{0:T(1024)(128)(4,1)}), s8[4194304]{0:T(1024)(128)(4,1)S(1)}, s32[]{:S(2)}) async-start(s8[12582912]{0:T(1024)(128)(4,1)} %bitcast.187), calls=%async_computation.1 | async-start | bytes 8388608
  402.2 8.2 slice-start.2
  402.3 8.2 copy-start.24
  402.3 8.2 copy-start.54
  497.4 11.7 %copy-start.20 = (pred[512,1024]{1,0:T(8,128)(4,1)S(1)}, pred[512,1024]{1,0:T(8,128)(4,1)}, u32[]{:S(2)}) copy-start(pred[512,1024]{1,0:T(8,128)(4,1)} %fusion.75) | copy-start | bytes 1572868
  497.4 11.7 %copy-start.53 = (f32[12,512]{1,0:T(8,128)S(1)}, f32[12,512]{1,0:T(8,128)}, u32[]{:S(2)}) copy-start(f32[12,512]{1,0:T(8,128)} %log_add_fusion) | copy-start | bytes 73732
  497.4 11.7 %copy-start.76 = (f32[512,12,64]{0,2,1:T(8,128)S(1)}, f32[512,12,64]{0,2,1:T(8,128)}, u32[]{:S(2)}) copy-start(f32[512,12,64]{0,2,1:T(8,128)} %fusion.81) | copy-start | bytes 4718596
  681.3 12.9 %copy-start.74 = (pred[32]{0:T(512)(128)(4,1)S(1)}, pred[32]{0:T(512)(128)(4,1)}, u32[]{:S(2)}) copy-start(pred[32]{0:T(512)(128)(4,1)} %compare_and_fusion) | copy-start | bytes 100
  708.3 11.5 %collective-permute-start.5 = (bf16[16,96,2304]{2,1,0:T(8,128)(2,1)S(1)}, bf16[16,96,2304]{2,1,0:T(8,128)(2,1)}, u32[]{:S(2)}, u32[]{:S(2)}) collective-permute-start(bf16[16,96,2304]{2,1,0:T(8,128)(2,1)S(1)} %slice.257), channel_id=1, source_target_pairs={{0,1},{1,0},{2,3},{3,2},{4,5},{5,4},{6,7},{7,6},{8,9},{9,8},{10,11... | collective-permute-start | bytes 21233672 | tf_op jit(solution)/shard_map/ppermute | solution.py:136
  728.4 12.2 %copy-start.15 = (bf16[1024,1,768]{2,0,1:T(8,128)(2,1)S(1)}, bf16[1024,1,768]{2,0,1:T(8,128)(2,1)}, u32[]{:S(2)}) copy-start(bf16[1024,1,768]{2,0,1:T(8,128)(2,1)} %copy.146) | copy-start | bytes 4718596
  732.6 41.8 %collective-permute-start.6 = (bf16[8,96,2304]{2,1,0:T(8,128)(2,1)}, bf16[8,96,2304]{2,1,0:T(8,128)(2,1)}, u32[]{:S(2)}, u32[]{:S(2)}) collective-permute-start(bf16[8,96,2304]{2,1,0:T(8,128)(2,1)} %slice.259), channel_id=1, source_target_pairs={{0,2},{1,5},{2,0},{3,7},{4,6},{5,1},{6,4},{7,3},{8,10},{9,13},{10,... | collective-permute-start | bytes 10616840 | tf_op jit(solution)/shard_map/ppermute | solution.py:132
  755.9 23.9 %slice-start.5 = ((s8[4718592]{0:T(1024)(128)(4,1)}), s8[4194304]{0:T(1024)(128)(4,1)S(1)}, s32[]{:S(2)}) async-start(s8[4718592]{0:T(1024)(128)(4,1)} %bitcast.219), calls=%async_computation.5 | async-start | bytes 8388608
  755.9 23.8 %copy-start.6 = (f32[1024,768]{0,1:T(8,128)S(1)}, f32[1024,768]{0,1:T(8,128)}, u32[]{:S(2)}) copy-start(f32[1024,768]{0,1:T(8,128)} %copy-done.4) | copy-start | bytes 9437188
  755.9 23.8 %slice-start.6 = ((s8[4718592]{0:T(1024)(128)(4,1)}), s8[524288]{0:T(1024)(128)(4,1)S(1)}, s32[]{:S(2)}) async-start(s8[4718592]{0:T(1024)(128)(4,1)} %bitcast.219), calls=%async_computation.6 | async-start | bytes 1048576
  755.9 23.8 %copy-start.60 = (f32[4,1,768]{2,1,0:T(1,128)S(1)}, f32[4,1,768]{2,1,0:T(1,128)}, u32[]{:S(2)}) copy-start(f32[4,1,768]{2,1,0:T(1,128)} %all-gather.1) | copy-start | bytes 36868
  755.9 23.8 %copy-start.66 = (f32[768]{0:T(1024)S(1)}, f32[768]{0:T(1024)}, u32[]{:S(2)}) copy-start(f32[768]{0:T(1024)} %get-tuple-element.174) | copy-start | bytes 9220
  777.9 22.6 %collective-permute-start.7 = (bf16[4,96,2304]{2,1,0:T(8,128)(2,1)S(1)}, bf16[4,96,2304]{2,1,0:T(8,128)(2,1)S(1)}, u32[]{:S(2)}, u32[]{:S(2)}) collective-permute-start(bf16[4,96,2304]{2,1,0:T(8,128)(2,1)S(1)} %slice.261), channel_id=1, source_target_pairs={{0,4},{1,9},{2,6},{3,11},{4,0},{5,13},{6,2},{7,15},{8,12},{9,1},{1... | collective-permute-start | bytes 5308424 | tf_op jit(solution)/shard_map/ppermute | solution.py:132
  789.2 11.6 %copy-start.7 = (f32[1024,768]{0,1:T(8,128)S(1)}, f32[1024,768]{0,1:T(8,128)}, u32[]{:S(2)}) copy-start(f32[1024,768]{0,1:T(8,128)} %copy.148) | copy-start | bytes 9437188
  789.2 13.0 %copy-start.9 = (f32[1024,768]{0,1:T(8,128)S(1)}, f32[1024,768]{0,1:T(8,128)}, u32[]{:S(2)}) copy-start(f32[1024,768]{0,1:T(8,128)} %copy-done.8) | copy-start | bytes 9437188
  789.2 13.0 %copy-start.12 = (bf16[1024,768]{0,1:T(8,128)(2,1)S(1)}, bf16[1024,768]{0,1:T(8,128)(2,1)}, u32[]{:S(2)}) copy-start(bf16[1024,768]{0,1:T(8,128)(2,1)} %copy.139) | copy-start | bytes 4718596
  789.3 13.0 %copy-start.52 = (f32[1024]{0:T(1024)S(1)}, f32[1024]{0:T(1024)}, u32[]{:S(2)}) copy-start(f32[1024]{0:T(1024)} %copy-done.51) | copy-start | bytes 12292
  800.8 21.4 %collective-permute-start.8 = (bf16[2,96,2304]{2,1,0:T(8,128)(2,1)S(1)}, bf16[2,96,2304]{2,1,0:T(8,128)(2,1)S(1)}, u32[]{:S(2)}, u32[]{:S(2)}) collective-permute-start(bf16[2,96,2304]{2,1,0:T(8,128)(2,1)S(1)} %slice.263), channel_id=1, source_target_pairs={{0,8},{1,17},{2,10},{3,19},{4,12},{5,21},{6,14},{7,23},{8,0},{9,25... | collective-permute-start | bytes 2654216 | tf_op jit(solution)/shard_map/ppermute | solution.py:132
  802.2 24.0 %copy-start.16 = (bf16[1024,1,768]{2,0,1:T(8,128)(2,1)S(1)}, bf16[1024,1,768]{2,0,1:T(8,128)(2,1)}, u32[]{:S(2)}) copy-start(bf16[1024,1,768]{2,0,1:T(8,128)(2,1)} %copy.144) | copy-start | bytes 4718596
  802.2 24.0 %copy-start.17 = (bf16[1024,1,768]{2,0,1:T(8,128)(2,1)S(1)}, bf16[1024,1,768]{2,0,1:T(8,128)(2,1)}, u32[]{:S(2)}) copy-start(bf16[1024,1,768]{2,0,1:T(8,128)(2,1)} %copy.145) | copy-start | bytes 4718596
  823.2 12.9 %copy-start.18 = (bf16[1024,768]{0,1:T(8,128)(2,1)S(1)}, bf16[1024,768]{0,1:T(8,128)(2,1)}, u32[]{:S(2)}) copy-start(bf16[1024,768]{0,1:T(8,128)(2,1)} %get-tuple-element.206) | copy-start | bytes 4718596
  824.0 14.6 %collective-permute-start.9 = (bf16[1,96,2304]{2,1,0:T(8,128)(2,1)}, bf16[1,96,2304]{2,1,0:T(8,128)(2,1)}, u32[]{:S(2)}, u32[]{:S(2)}) collective-permute-start(bf16[1,96,2304]{2,1,0:T(8,128)(2,1)} %slice.265), channel_id=1, source_target_pairs={{0,16},{1,3},{2,18},{3,1},{4,20},{5,7},{6,22},{7,5},{8,24},{9,11},... | collective-permute-start | bytes 1327112 | tf_op jit(solution)/shard_map/ppermute | solution.py:132
  827.0 11.5 %copy-start.22 = (bf16[2,96,2304]{2,1,0:T(8,128)(2,1)S(1)}, bf16[2,96,2304]{2,1,0:T(8,128)(2,1)}, u32[]{:S(2)}) copy-start(bf16[2,96,2304]{2,1,0:T(8,128)(2,1)} %copy-done.21) | copy-start | bytes 2654212
  827.0 64.0 %copy-start.37 = (f32[192,96]{0,1:T(8,128)S(1)}, f32[192,96]{0,1:T(8,128)}, u32[]{:S(2)}) copy-start(f32[192,96]{0,1:T(8,128)} %copy-done.36) | copy-start | bytes 221188
  829.7 64.8 %copy-start.32 = (f32[96,3,192]{0,2,1:T(8,128)S(1)}, f32[96,3,192]{0,2,1:T(8,128)}, u32[]{:S(2)}) copy-start(f32[96,3,192]{0,2,1:T(8,128)} %copy.161) | copy-start | bytes 663556
  829.7 64.8 %copy-start.33 = (f32[96,3,192]{0,2,1:T(8,128)S(1)}, f32[96,3,192]{0,2,1:T(8,128)}, u32[]{:S(2)}) copy-start(f32[96,3,192]{0,2,1:T(8,128)} %copy.159) | copy-start | bytes 663556
  837.6 62.0 %copy-start.29 = (f32[768,96]{0,1:T(8,128)S(1)}, f32[768,96]{0,1:T(8,128)}, u32[]{:S(2)}) copy-start(f32[768,96]{0,1:T(8,128)} %param.44) | copy-start | bytes 884740
  839.6 59.4 %copy-start.44 = (f32[6,768]{1,0:T(8,128)S(1)}, f32[6,768]{1,0:T(8,128)}, u32[]{:S(2)}) copy-start(f32[6,768]{1,0:T(8,128)} %param.45) | copy-start | bytes 55300
  839.6 59.4 %copy-start.55 = (f32[6,768]{1,0:T(8,128)S(1)}, f32[6,768]{1,0:T(8,128)}, u32[]{:S(2)}) copy-start(f32[6,768]{1,0:T(8,128)} %param.59) | copy-start | bytes 55300
  839.6 59.4 %copy-start.56 = (f32[6,768]{1,0:T(8,128)S(1)}, f32[6,768]{1,0:T(8,128)}, u32[]{:S(2)}) copy-start(f32[6,768]{1,0:T(8,128)} %param.52) | copy-start | bytes 55300
  839.6 62.1 %copy-start.30 = (f32[96,768]{1,0:T(8,128)S(1)}, f32[96,768]{1,0:T(8,128)}, u32[]{:S(2)}) copy-start(f32[96,768]{1,0:T(8,128)} %param.43) | copy-start | bytes 884740
  892.0 11.8 %copy-start.63 = (f32[2,192]{1,0:T(2,128)S(1)}, f32[2,192]{1,0:T(2,128)}, u32[]{:S(2)}) copy-start(f32[2,192]{1,0:T(2,128)} %param.46) | copy-start | bytes 4612
  892.0 11.8 %copy-start.70 = (f32[2,192]{1,0:T(2,128)S(1)}, f32[2,192]{1,0:T(2,128)}, u32[]{:S(2)}) copy-start(f32[2,192]{1,0:T(2,128)} %param.60) | copy-start | bytes 4612
  892.1 11.8 %copy-start.71 = (f32[2,192]{1,0:T(2,128)S(1)}, f32[2,192]{1,0:T(2,128)}, u32[]{:S(2)}) copy-start(f32[2,192]{1,0:T(2,128)} %param.53) | copy-start | bytes 4612
  892.1 13.2 %copy-start.58 = (f32[768]{0:T(1024)S(1)}, f32[768]{0:T(1024)}, u32[]{:S(2)}) copy-start(f32[768]{0:T(1024)} %param.47) | copy-start | bytes 9220
  892.1 13.2 %copy-start.64 = (f32[768]{0:T(1024)S(1)}, f32[768]{0:T(1024)}, u32[]{:S(2)}) copy-start(f32[768]{0:T(1024)} %param.61) | copy-start | bytes 9220
  892.1 13.2 %copy-start.65 = (f32[768]{0:T(1024)S(1)}, f32[768]{0:T(1024)}, u32[]{:S(2)}) copy-start(f32[768]{0:T(1024)} %param.54) | copy-start | bytes 9220
  (31 other events, 136.0 us)

commit v2 on v0

v2 whole, which is shorter than its diff:
```python
import functools
import jax
import jax.numpy as jnp
from jax import lax
from jax.experimental import pallas as pl
from jax.experimental.pallas import tpu as pltpu
from jax.sharding import PartitionSpec as P

HEAD_DIM = 64
TILE = 256
STEP = 10

eps_norm = 1e-05
clip_norm = 1.0
beta_one = 0.9
beta_two = 0.999
adam_eps = 1e-08
rate = 0.05
vector_rate = 0.5
decay = 0.01
excluded = -1e30
low = jnp.bfloat16
f32 = jnp.float32
GELU_A = 0.7978845608028654
GELU_B = GELU_A * 0.044715


def params(limit_mib, **kw):
    return pltpu.CompilerParams(vmem_limit_bytes=limit_mib * 1024 * 1024, **kw)


def cost(flops, moved, special=0):
    return pl.CostEstimate(flops=int(flops), bytes_accessed=int(moved), transcendentals=int(special))


def mm(a, b):
    return jnp.dot(a, b, preferred_element_type=f32)


def mm_nt(a, b):
    return lax.dot_general(a, b, (((1,), (1,)), ((), ())), preferred_element_type=f32)


def whole(shape):
    zeros = (0,) * len(shape)
    return pl.BlockSpec(shape, lambda *_: zeros)


def sds(shape, dtype):
    return jax.ShapeDtypeStruct(shape, dtype)


def live_blocks(length_ref, count, body):
    length = length_ref[0]
    for blocks in range(1, count + 1):
        low_end = (blocks - 1) * TILE
        high_end = blocks * TILE
        @pl.when((length > low_end) & (length <= high_end))
        def _(blocks=blocks):
            body(length, blocks)


def forward_body(length_ref, q_ref, k_ref, v_ref, o_ref, lse_ref, vt_ref):
    seq = q_ref.shape[0]
    vt_ref[...] = v_ref[...].T
    lane = lax.broadcasted_iota(jnp.int32, (TILE, 2 * HEAD_DIM), 1)
    causal = lax.broadcasted_iota(jnp.int32, (TILE, TILE), 0) <= lax.broadcasted_iota(jnp.int32, (TILE, TILE), 1)

    def run(length, blocks):
        tasks = [(b, h) for b in range(blocks) for h in range(2)]

        def scores(i):
            b, h = tasks[i]
            q = q_ref[b * TILE : (b + 1) * TILE, :] * jnp.asarray(HEAD_DIM**-0.5, low)
            qh = jnp.where((lane < HEAD_DIM) if h == 0 else (lane >= HEAD_DIM), q, jnp.zeros_like(q))
            return mm_nt(k_ref[: (b + 1) * TILE, :], qh)

        now = scores(0)
        outs = []
        for i, (b, h) in enumerate(tasks):
            start, stop = b * TILE, (b + 1) * TILE
            later = scores(i + 1) if i + 1 < len(tasks) else None
            last = jnp.where(causal, now[start:, :], excluded)
            top = jnp.max(last, axis=0, keepdims=True)
            if b:
                top = jnp.maximum(top, jnp.max(now[:start], axis=0, keepdims=True))
            p = jnp.exp(last - top)
            total = jnp.sum(p, axis=0, keepdims=True)
            pb = p.astype(low)
            if b:
                pf = jnp.exp(now[:start] - top)
                total = total + jnp.sum(pf, axis=0, keepdims=True)
                pb = jnp.concatenate([pf.astype(low), pb], axis=0)
            out = mm(vt_ref[h * HEAD_DIM : (h + 1) * HEAD_DIM, :stop], pb)
            outs.append(out / total)
            lse_ref[0, h : h + 1, start:stop] = top + jnp.log(total)
            if h:
                both = jnp.concatenate(outs, axis=0).T
                outs = []
                row = start + lax.broadcasted_iota(jnp.int32, both.shape, 0)
                o_ref[start:stop, :] = jnp.where(row < length, both, 0.0).astype(low)
            now = later
        if blocks * TILE < seq:
            o_ref[blocks * TILE :, :] = jnp.zeros((seq - blocks * TILE, 2 * HEAD_DIM), low)
            lse_ref[0, :, blocks * TILE :] = jnp.zeros((2, seq - blocks * TILE), f32)

    live_blocks(length_ref, seq // TILE, run)


def attend_forward(length, qkv):
    seq, width = qkv.shape[0], qkv.shape[1] // 3
    pair = 2 * HEAD_DIM
    pairs = width // pair
    half = seq * seq * 5 // 8
    spec = lambda part: pl.BlockSpec((seq, pair), lambda i, s: (0, part * pairs + i))
    return pl.pallas_call(
        forward_body,
        grid_spec=pltpu.PrefetchScalarGridSpec(
            num_scalar_prefetch=1,
            grid=(pairs,),
            in_specs=[spec(0), spec(1), spec(2)],
            out_specs=[
                pl.BlockSpec((seq, pair), lambda i, s: (0, i)),
                pl.BlockSpec((1, 2, seq), lambda i, s: (i, 0, 0)),
            ],
            scratch_shapes=[pltpu.VMEM((pair, seq), low)],
        ),
        out_shape=[sds((seq, width), low), sds((pairs, 2, seq), f32)],
        compiler_params=params(40),
        cost_estimate=cost(pairs * 2 * half * 2 * 2 * 256, seq * width * 8, pairs * 2 * half),
        name="attend_forward",
    )(length, qkv, qkv, qkv)


def backward_body(length_ref, q_ref, k_ref, v_ref, do_ref, lse_ref, out_ref, kt_ref, ksum, vsum):
    seq = q_ref.shape[0]
    scale = HEAD_DIM**-0.5
    kt_ref[...] = k_ref[...].T
    lane = lax.broadcasted_iota(jnp.int32, (TILE, 2 * HEAD_DIM), 1)
    causal = lax.broadcasted_iota(jnp.int32, (TILE, TILE), 0) <= lax.broadcasted_iota(jnp.int32, (TILE, TILE), 1)

    def run(length, blocks):
        tasks = [(b, h) for b in reversed(range(blocks)) for h in range(2)]

        def scores(i):
            b, h = tasks[i]
            mine = (lane < HEAD_DIM) if h == 0 else (lane >= HEAD_DIM)
            q = q_ref[b * TILE : (b + 1) * TILE, :] * jnp.asarray(scale, low)
            up = do_ref[b * TILE : (b + 1) * TILE, :]
            qh = jnp.where(mine, q, jnp.zeros_like(q))
            uh = jnp.where(mine, up, jnp.zeros_like(up))
            stop = (b + 1) * TILE
            return qh, uh, mm_nt(k_ref[:stop, :], qh), mm_nt(v_ref[:stop, :], uh)

        now = scores(0)
        dqs, dss, pbs, qs, us = [], [], [], [], []
        for i, (b, h) in enumerate(tasks):
            start, stop = b * TILE, (b + 1) * TILE
            later = scores(i + 1) if i + 1 < len(tasks) else None
            qh, uh, s, dp = now
            lse = lse_ref[0, h : h + 1, start:stop]
            p = jnp.exp(jnp.where(causal, s[start:], excluded) - lse)
            inner = jnp.sum(p * dp[start:], axis=0, keepdims=True)
            if b:
                pf = jnp.exp(s[:start] - lse)
                inner = inner + jnp.sum(pf * dp[:start], axis=0, keepdims=True)
            ds = (p * (dp[start:] - inner)).astype(low)
            pb = p.astype(low)
            if b:
                ds = jnp.concatenate([(pf * (dp[:start] - inner)).astype(low), ds], axis=0)
                pb = jnp.concatenate([pf.astype(low), pb], axis=0)
            dqs.append(mm(kt_ref[h * HEAD_DIM : (h + 1) * HEAD_DIM, :stop], ds))
            dss.append(ds)
            pbs.append(pb)
            qs.append(qh)
            us.append(uh)
            if h:
                dk = mm(jnp.concatenate(dss, axis=1), jnp.concatenate(qs, axis=0))
                dv = mm(jnp.concatenate(pbs, axis=1), jnp.concatenate(us, axis=0))
                if b == blocks - 1:
                    ksum[:stop, :] = dk
                    vsum[:stop, :] = dv
                else:
                    ksum[:stop, :] += dk
                    vsum[:stop, :] += dv
                out_ref[1, start:stop, :] = ksum[start:stop, :].astype(low)
                out_ref[2, start:stop, :] = vsum[start:stop, :].astype(low)
                out_ref[0, start:stop, :] = (jnp.concatenate(dqs, axis=0).T * scale).astype(low)
                dqs, dss, pbs, qs, us = [], [], [], [], []
            now = later
        if blocks * TILE < seq:
            rest = jnp.zeros((seq - blocks * TILE, 2 * HEAD_DIM), low)
            for part in range(3):
                out_ref[part, blocks * TILE :, :] = rest

    live_blocks(length_ref, seq // TILE, run)


def attend_backward(length, qkv, upstream, lse):
    seq, width = upstream.shape
    pair = 2 * HEAD_DIM
    pairs = width // pair
    half = seq * seq * 5 // 8
    spec = lambda part: pl.BlockSpec((seq, pair), lambda i, s: (0, part * pairs + i))
    own = pl.BlockSpec((seq, pair), lambda i, s: (0, i))
    return pl.pallas_call(
        backward_body,
        grid_spec=pltpu.PrefetchScalarGridSpec(
            num_scalar_prefetch=1,
            grid=(pairs,),
            in_specs=[spec(0), spec(1), spec(2), own, pl.BlockSpec((1, 2, seq), lambda i, s: (i, 0, 0))],
            out_specs=pl.BlockSpec((3, seq, pair), lambda i, s: (0, 0, i)),
            scratch_shapes=[
                pltpu.VMEM((pair, seq), low),
                pltpu.VMEM((seq, pair), f32),
                pltpu.VMEM((seq, pair), f32),
            ],
        ),
        out_shape=sds((3, seq, width), low),
        compiler_params=params(48),
        cost_estimate=cost(pairs * 2 * half * 5 * 2 * 256, seq * width * 14, pairs * 2 * half),
        name="attend_backward",
    )(length, qkv, qkv, qkv, upstream, lse)


def normalize(values):
    average = jnp.mean(values, axis=-1, keepdims=True)
    centred = values - average
    inverse = lax.rsqrt(jnp.mean(centred * centred, axis=-1, keepdims=True) + eps_norm)
    return centred * inverse, inverse


def pull_norm(scaled, unit, inverse):
    first = jnp.mean(scaled, axis=-1, keepdims=True)
    second = jnp.mean(scaled * unit, axis=-1, keepdims=True)
    return inverse * (scaled - first - unit * second)


def columns_of(values):
    return jnp.sum(values, axis=0, keepdims=True)


def prepare_body(x_ref, up_ref, vec_ref, h_ref, ht_ref, upt_ref):
    unit, _ = normalize(x_ref[...].astype(f32))
    h = (unit * vec_ref[0:1, :] + vec_ref[1:2, :]).astype(low)
    h_ref[...] = h
    ht_ref[...] = h.T
    upt_ref[...] = up_ref[...].T


def prepare(x, up, vectors):
    seq, depth = x.shape
    rows = pl.BlockSpec((TILE, depth), lambda i: (i, 0))
    turned = pl.BlockSpec((depth, TILE), lambda i: (0, i))
    return pl.pallas_call(
        prepare_body,
        grid=(seq // TILE,),
        in_specs=[rows, rows, whole(vectors.shape)],
        out_specs=[rows, turned, turned],
        out_shape=[sds((seq, depth), low), sds((depth, seq), low), sds((depth, seq), low)],
        compiler_params=params(24),
        cost_estimate=cost(seq * depth * 10, seq * depth * 10),
        name="prepare",
    )(x, up, vectors)


def project_body(core_ref, spots_ref, h_ref, mine_ref, twin_ref, bias_ref, qkv_ref, wide_ref):
    part = pl.program_id(0)
    rows = mine_ref.shape[1]
    width = mine_ref.shape[2] // 4
    groups = wide_ref.shape[1] // rows

    def collect(sources, index):
        at = slice(index * width, (index + 1) * width)
        for group in range(groups):
            pieces = [sources[model % 2][spots_ref[model, group], :, at] for model in range(4)]
            wide_ref[0, group * rows : (group + 1) * rows, :] = jnp.concatenate(pieces, axis=1)

    for index in range(4):
        for core in range(2):

            @pl.when((part == index) & (core_ref[0] == core))
            def _(index=index, core=core):
                collect((mine_ref, twin_ref) if core == 0 else (twin_ref, mine_ref), index)

    @pl.when(part < 3)
    def _():
        qkv_ref[...] = (mm(h_ref[...], wide_ref[0]) + bias_ref[0]).astype(low)


def project(core, spots, h, mine, twin, bias):
    seq, depth = h.shape
    return pl.pallas_call(
        project_body,
        grid_spec=pltpu.PrefetchScalarGridSpec(
            num_scalar_prefetch=2,
            grid=(4,),
            in_specs=[
                whole((seq, depth)),
                whole(mine.shape),
                whole(twin.shape),
                pl.BlockSpec((1, 1, depth), lambda i, *_: (jnp.minimum(i, 2), 0, 0)),
            ],
            out_specs=[
                pl.BlockSpec((seq, depth), lambda i, *_: (0, jnp.minimum(i, 2))),
                pl.BlockSpec((1, depth, depth), lambda i, *_: (i, 0, 0)),
            ],
        ),
        out_shape=[sds((seq, 3 * depth), low), sds((4, depth, depth), low)],
        compiler_params=params(40),
        cost_estimate=cost(2 * seq * depth * depth * 3, seq * depth * 16),
        name="project",
    )(core, spots, h, mine, twin, bias)


def attend_out_body(o_ref, w_ref, x_ref, vec_ref, middle_ref, h_ref, ht_ref):
    middle = x_ref[...].astype(f32) + mm_nt(o_ref[...], w_ref[0]) + vec_ref[4:5, :]
    middle_ref[...] = middle
    unit, _ = normalize(middle)
    h = (unit * vec_ref[2:3, :] + vec_ref[3:4, :]).astype(low)
    h_ref[...] = h
    ht_ref[...] = h.T


def attend_out(o, wide, x, vectors):
    seq, depth = x.shape
    rows = pl.BlockSpec((TILE, depth), lambda i: (i, 0))
    turned = pl.BlockSpec((depth, TILE), lambda i: (0, i))
    return pl.pallas_call(
        attend_out_body,
        grid=(seq // TILE,),
        in_specs=[
            rows,
            pl.BlockSpec((1, depth, depth), lambda i: (3, 0, 0)),
            rows,
            whole(vectors.shape),
        ],
        out_specs=[rows, rows, turned],
        out_shape=[sds((seq, depth), f32), sds((seq, depth), low), sds((depth, seq), low)],
        compiler_params=params(24),
        cost_estimate=cost(2 * seq * depth * depth, seq * depth * 14),
        name="attend_out",
    )(o, wide, x, vectors)


def feed_body(
    spots_ref,
    h2_ref,
    h2t_ref,
    up_ref,
    upt_ref,
    mine_a,
    mine_b,
    twin_a,
    twin_b,
    bias_ref,
    out_ref,
    back_ref,
    keep_a,
    keep_b,
    send_a,
    send_b,
    bias_grad_ref,
    wide_ref,
    act_ref,
    pre_ref,
):
    step = pl.program_id(0)
    side = lax.rem(step, 2)
    half = mine_a.shape[1]
    part = mine_a.shape[2] // 2
    groups = wide_ref.shape[0] // (2 * half)

    @pl.when(step == 0)
    def _():
        out_ref[...] = jnp.zeros_like(out_ref)
        back_ref[...] = jnp.zeros_like(back_ref)

    for group in range(groups):
        for which, (mine, twin) in enumerate(((mine_a, twin_a), (mine_b, twin_b))):
            first = (2 * group + which) * half
            own = mine[spots_ref[0, side, group]]
            other = twin[spots_ref[1, side, group]]
            wide_ref[first : first + half, :part] = own[:, :part]
            wide_ref[first : first + half, part : 2 * part] = other[:, :part]
            wide_ref[first : first + half, 2 * part : 3 * part] = own[:, part:]
            wide_ref[first : first + half, 3 * part :] = other[:, part:]

    expand = wide_ref[:, : 2 * part]
    shrink = wide_ref[:, 2 * part :]
    bias = bias_ref[0]
    sums = jnp.zeros((1, 2 * part), f32)
    for tile in range(h2_ref.shape[0] // TILE):
        at = slice(tile * TILE, (tile + 1) * TILE)
        u = mm(h2_ref[at, :], expand) + bias
        square = u * u
        th = jnp.tanh(u * (GELU_A + GELU_B * square))
        gate = 0.5 * th + 0.5
        slope = gate + (gate * (1.0 - gate)) * (u * (2.0 * GELU_A + (6.0 * GELU_B) * square))
        pre = (mm(up_ref[at, :], shrink) * slope).astype(low)
        act_ref[at, :] = (u * gate).astype(low)
        pre_ref[at, :] = pre
        sums = sums + columns_of(pre.astype(f32))
    bias_grad_ref[0] = sums
    out_ref[...] += mm_nt(act_ref[...], shrink)
    back_ref[...] += mm_nt(pre_ref[...], expand)
    grad_expand = mm(h2t_ref[...], pre_ref[...]).astype(low)
    grad_shrink = mm(upt_ref[...], act_ref[...]).astype(low)
    for group in range(groups):
        for which, (keep, send) in enumerate(((keep_a, send_a), (keep_b, send_b))):
            first = (2 * group + which) * half
            at = slice(first, first + half)
            own, other = spots_ref[0, side, group], spots_ref[1, side, group]
            keep[own, :, :part] = grad_expand[at, :part]
            keep[own, :, part:] = grad_shrink[at, :part]
            send[other, :, :part] = grad_expand[at, part:]
            send[other, :, part:] = grad_shrink[at, part:]


def feed(spots, h2, h2t, up, upt, pieces, bias):
    seq, depth = h2.shape
    slots, half, columns = pieces[0].shape
    steps = bias.shape[0]
    part = bias.shape[2] // 2
    piece = pl.BlockSpec((slots, half, 2 * part), lambda i, s: (0, 0, i // 2))
    bias_spec = pl.BlockSpec((1, 1, 2 * part), lambda i, s: (i, 0, 0))
    return pl.pallas_call(
        feed_body,
        grid_spec=pltpu.PrefetchScalarGridSpec(
            num_scalar_prefetch=1,
            grid=(steps,),
            in_specs=[
                whole((seq, depth)),
                whole((depth, seq)),
                whole((seq, depth)),
                whole((depth, seq)),
                piece,
                piece,
                piece,
                piece,
                bias_spec,
            ],
            out_specs=[whole((seq, depth)), whole((seq, depth)), piece, piece, piece, piece, bias_spec],
            scratch_shapes=[
                pltpu.VMEM((depth, 4 * part), low),
                pltpu.VMEM((seq, 2 * part), low),
                pltpu.VMEM((seq, 2 * part), low),
            ],
        ),
        out_shape=[sds((seq, depth), f32), sds((seq, depth), f32)]
        + [sds(pieces[0].shape, low)] * 4
        + [sds(bias.shape, f32)],
        compiler_params=params(60),
        cost_estimate=cost(12 * seq * depth * steps * 2 * part, seq * depth * 40, seq * steps * part),
        name="feed",
    )(spots, h2, h2t, up, upt, *pieces, bias)


def middle_back_body(
    length_ref,
    back_ref,
    out_ref,
    middle_ref,
    up_ref,
    o_ref,
    w_ref,
    vec_ref,
    block_ref,
    grad_ref,
    mixture_ref,
    weight_ref,
    sums_ref,
):
    step = pl.program_id(0)
    middle = middle_ref[...]
    block_ref[...] = (middle + out_ref[...] + vec_ref[5:6, :]).astype(low)
    unit, inverse = normalize(middle)
    back = back_ref[...]
    up = up_ref[...].astype(f32)
    grad = up + pull_norm(back * vec_ref[2:3, :], unit, inverse)
    grad_ref[...] = grad
    rounded = grad.astype(low)
    first = step * TILE
    row = first + lax.broadcasted_iota(jnp.int32, (TILE, grad.shape[1]), 0)
    mixture_ref[...] = jnp.where(row < length_ref[0], mm(rounded, w_ref[0]), 0.0).astype(low)
    share = mm(rounded.T, o_ref[...])
    sums = jnp.concatenate(
        [columns_of(back * unit), columns_of(back), columns_of(grad), columns_of(up)], axis=0
    )

    @pl.when(step == 0)
    def _():
        weight_ref[...] = share
        sums_ref[...] = sums

    @pl.when(step > 0)
    def _():
        weight_ref[...] += share
        sums_ref[...] += sums


def middle_back(length, back, out, middle, up, o, wide, vectors):
    seq, depth = middle.shape
    rows = pl.BlockSpec((TILE, depth), lambda i, s: (i, 0))
    return pl.pallas_call(
        middle_back_body,
        grid_spec=pltpu.PrefetchScalarGridSpec(
            num_scalar_prefetch=1,
            grid=(seq // TILE,),
            in_specs=[
                rows,
                rows,
                rows,
                rows,
                rows,
                pl.BlockSpec((1, depth, depth), lambda i, s: (3, 0, 0)),
                whole(vectors.shape),
            ],
            out_specs=[rows, rows, rows, whole((depth, depth)), whole((4, depth))],
        ),
        out_shape=[
            sds((seq, depth), low),
            sds((seq, depth), f32),
            sds((seq, depth), low),
            sds((depth, depth), f32),
            sds((4, depth), f32),
        ],
        compiler_params=params(32),
        cost_estimate=cost(4 * seq * depth * depth, seq * depth * 28),
        name="middle_back",
    )(length, back, out, middle, up, o, wide, vectors)


def input_grad_body(core_ref, spots_ref, ht_ref, back_ref, out_grad_ref, keep_ref, send_ref, sums_ref):
    part = pl.program_id(0)
    rows = keep_ref.shape[1]
    width = keep_ref.shape[2] // 4
    groups = ht_ref.shape[0] // rows

    def spread(targets, index, grad):
        at = slice(index * width, (index + 1) * width)
        for group in range(groups):
            for model in range(4):
                targets[model % 2][spots_ref[model, group], :, at] = grad[
                    group * rows : (group + 1) * rows, model * width : (model + 1) * width
                ]

    for index in range(4):

        @pl.when(part == index)
        def _(index=index):
            if index < 3:
                sums_ref[0] = columns_of(back_ref[0].astype(f32))
                grad = mm(ht_ref[...], back_ref[0]).astype(low)
            else:
                grad = out_grad_ref[...].astype(low)
            for core in range(2):

                @pl.when(core_ref[0] == core)
                def _(core=core):
                    spread((keep_ref, send_ref) if core == 0 else (send_ref, keep_ref), index, grad)


def input_grad(core, spots, ht, back, out_grad, slots, rows):
    depth, seq = ht.shape
    shape = (slots, rows, 4 * (depth // 4))
    return pl.pallas_call(
        input_grad_body,
        grid_spec=pltpu.PrefetchScalarGridSpec(
            num_scalar_prefetch=2,
            grid=(4,),
            in_specs=[
                whole((depth, seq)),
                pl.BlockSpec((1, seq, depth), lambda i, *_: (jnp.minimum(i, 2), 0, 0)),
                whole((depth, depth)),
            ],
            out_specs=[
                whole(shape),
                whole(shape),
                pl.BlockSpec((1, 1, depth), lambda i, *_: (jnp.minimum(i, 2), 0, 0)),
            ],
        ),
        out_shape=[sds(shape, low), sds(shape, low), sds((3, 1, depth), f32)],
        compiler_params=params(40),
        cost_estimate=cost(6 * seq * depth * depth, seq * depth * 14),
        name="input_grad",
    )(core, spots, ht, back, out_grad)


def token_back_body(back_ref, w_ref, x_ref, grad_ref, vec_ref, token_ref, sums_ref):
    step = pl.program_id(0)
    back = mm_nt(back_ref[0], w_ref[0]) + mm_nt(back_ref[1], w_ref[1]) + mm_nt(back_ref[2], w_ref[2])
    unit, inverse = normalize(x_ref[...].astype(f32))
    token_ref[...] = (grad_ref[...] + pull_norm(back * vec_ref[0:1, :], unit, inverse)).astype(low)
    sums = jnp.concatenate([columns_of(back * unit), columns_of(back)], axis=0)

    @pl.when(step == 0)
    def _():
        sums_ref[...] = sums

    @pl.when(step > 0)
    def _():
        sums_ref[...] += sums


def token_back(back, wide, x, grad, vectors):
    seq, depth = x.shape
    rows = pl.BlockSpec((TILE, depth), lambda i: (i, 0))
    return pl.pallas_call(
        token_back_body,
        grid=(seq // TILE,),
        in_specs=[
            pl.BlockSpec((3, TILE, depth), lambda i: (0, i, 0)),
            pl.BlockSpec((3, depth, depth), lambda i: (0, 0, 0)),
            rows,
            rows,
            whole(vectors.shape),
        ],
        out_specs=[rows, whole((2, depth))],
        out_shape=[sds((seq, depth), low), sds((2, depth), f32)],
        compiler_params=params(32),
        cost_estimate=cost(6 * seq * depth * depth, seq * depth * 16),
        name="token_back",
    )(back, wide, x, grad, vectors)


CORE_ORDERS = ((4, 3, 2, 1), (1, 4, 3, 2))
STAGES = 4


def cube_permute(values, stage):
    pairs = [(device, device ^ (1 << CORE_ORDERS[device & 1][stage])) for device in range(32)]
    return lax.ppermute(values, ("dp", "mp"), pairs)


def bit_permute(values, bit):
    return lax.ppermute(values, ("dp", "mp"), [(device, device ^ (1 << bit)) for device in range(32)])


def place(distance, core):
    spots = [
        sum(((distance >> bit) & 1) << step for step, bit in enumerate(order)) for order in CORE_ORDERS
    ]
    return jnp.where(core == 0, spots[0], spots[1])


def cube_gather(shard):
    held = shard[None]
    for stage in range(STAGES):
        held = jnp.concatenate([held, cube_permute(held, stage)], axis=0)
    return held, bit_permute(held, 0)


def cube_scatter(keep, send):
    other = bit_permute(send, 0)
    for stage in reversed(range(STAGES)):
        half = 1 << stage
        away = keep[half:] + other[half:]
        arrived = cube_permute(away, stage)
        keep, other = keep[:half] + other[:half], arrived
    return keep[0].astype(f32) + other[0].astype(f32)


def cube_sum(values):
    for bit in range(5):
        values = values + bit_permute(values, bit)
    return values


def adam_step(weight, gradient, first_old, second_old, factor, step_rate):
    scaled = gradient * factor
    moment = beta_one * first_old + (1.0 - beta_one) * scaled
    square = beta_two * second_old + (1.0 - beta_two) * scaled * scaled
    corrected = moment / (1.0 - beta_one**STEP)
    spread = jnp.sqrt(square / (1.0 - beta_two**STEP))
    updated = weight - step_rate * (corrected / (spread + adam_eps) + decay * weight)
    return (moment, square, updated)


def squares(values):
    return jnp.sum(values * values)


def shards(
    tokens,
    cotangent,
    lengths,
    input_weight,
    output_weight,
    expand_weight,
    shrink_weight,
    layer_vectors,
    head_bias,
    expand_bias,
    first_input,
    first_output,
    first_expand,
    first_shrink,
    first_vectors,
    first_head,
    first_bias,
    second_input,
    second_output,
    second_expand,
    second_shrink,
    second_vectors,
    second_head,
    second_bias,
):
    dp_count = lax.axis_size("dp")
    mp_count = lax.axis_size("mp")
    cube = dp_count == 8 and mp_count == 4
    rows = input_weight.shape[0]
    width = input_weight.shape[2]
    hidden = expand_weight.shape[1]
    seq, depth = tokens.shape
    part = hidden // 3
    model_index = lax.axis_index("mp")
    me = lax.axis_index("dp") * mp_count + model_index

    attend_shard = jnp.concatenate(
        [input_weight.astype(low).reshape(rows, 3 * width), output_weight.astype(low).T], axis=1
    )
    expand_low = expand_weight.astype(low)
    shrink_low = shrink_weight.astype(low).T
    feed_shard = jnp.concatenate(
        [
            piece[:, index * part : (index + 1) * part]
            for index in range(3)
            for piece in (expand_low, shrink_low)
        ],
        axis=1,
    )
    bias_shard = jnp.concatenate([head_bias.reshape(1, 2 * width), expand_bias[None]], axis=1)

    if cube:
        core = me & 1
        mine_attend, twin_attend = cube_gather(attend_shard)
        mine_a, twin_a = cube_gather(feed_shard[: rows // 2])
        mine_b, twin_b = cube_gather(feed_shard[rows // 2 :])
        bias_full = jnp.where(jnp.arange(4)[:, None] == model_index, bias_shard, 0.0)
        bias_full = bias_full + bit_permute(bias_full, 0)
        bias_full = bias_full + bit_permute(bias_full, 1)
        devices = jnp.arange(32).reshape(8, 4).T
        spots = place(devices ^ me, devices & 1).astype(jnp.int32)
        near = model_index
    else:
        core = jnp.zeros((), jnp.int32)

        def planes(shard):
            full = lax.all_gather(lax.all_gather(shard, "dp", axis=0, tiled=True), "mp", axis=0)
            full = full.reshape(2, 2, 8, depth // 8, shard.shape[1]).transpose(1, 0, 2, 3, 4)
            return full.reshape(2, 16, depth // 8, shard.shape[1])

        mine_attend, twin_attend = planes(attend_shard)
        feed_planes = planes(feed_shard)
        middle_row = depth // 16
        mine_a, twin_a = feed_planes[:, :, :middle_row]
        mine_b, twin_b = feed_planes[:, :, middle_row:]
        bias_full = lax.all_gather(bias_shard, "mp", axis=0, tiled=True)
        spots = (jnp.arange(4)[:, None] // 2 * 8 + jnp.arange(8)[None]).astype(jnp.int32)
        near = jnp.zeros((), jnp.int32)
    near_models = near ^ jnp.arange(4)
    near_spots = jnp.take(spots, near_models, axis=0).reshape(2, 2, 8).transpose(1, 0, 2)
    core = core.astype(jnp.int32).reshape(1)

    length = lax.dynamic_slice_in_dim(lengths, model_index, 1, 0)
    head_full = bias_full[:, : 2 * width].reshape(4, 2, width).transpose(1, 0, 2).reshape(2, depth)
    qkv_bias = jnp.stack([head_full[0], jnp.zeros_like(head_full[0]), head_full[1]])[:, None]
    feed_bias = (
        jnp.take(bias_full[:, 2 * width :], near_models, axis=0)
        .reshape(2, 2, 3, part)
        .transpose(2, 0, 1, 3)
        .reshape(6, 1, 2 * part)
    )

    normed, normed_t, upstream_t = prepare(tokens, cotangent, layer_vectors)
    qkv, wide = project(core, spots, normed, mine_attend, twin_attend, qkv_bias)
    mixture, log_totals = attend_forward(length, qkv)
    middle, hidden_in, hidden_t = attend_out(mixture, wide, tokens, layer_vectors)
    out, back, keep_a, keep_b, send_a, send_b, feed_bias_grad = feed(
        near_spots, hidden_in, hidden_t, cotangent, upstream_t, (mine_a, mine_b, twin_a, twin_b), feed_bias
    )
    block_out, middle_grad, mixture_grad, output_grad, middle_sums = middle_back(
        length, back, out, middle, cotangent, mixture, wide, layer_vectors
    )
    packed_grad = attend_backward(length, qkv, mixture_grad, log_totals)
    keep_attend, send_attend, head_sums = input_grad(
        core, spots, normed_t, packed_grad, output_grad, 16, depth // 8
    )
    token_grad, token_sums = token_back(packed_grad, wide, tokens, middle_grad, layer_vectors)

    bias_near = feed_bias_grad.reshape(3, 2, 2, part).transpose(1, 2, 0, 3).reshape(4, hidden)
    bias_grad = jnp.take(bias_near, near_models, axis=0)
    vector_local = jnp.concatenate(
        [token_sums, middle_sums, head_sums[0], head_sums[2], bias_grad.reshape(4, depth)], axis=0
    )
    if cube:
        feed_a = cube_scatter(keep_a, send_a)
        feed_b = cube_scatter(keep_b, send_b)
        attend_total = cube_scatter(keep_attend, send_attend)
        vector_total = cube_sum(vector_local)
        feed_total = jnp.concatenate([feed_a, feed_b], axis=0)
    else:

        def own_block(keep, send):
            full = jnp.stack([keep, send]).reshape(2, 2, 8, depth // 8, keep.shape[2])
            full = full.transpose(1, 0, 2, 3, 4).reshape(4, depth, keep.shape[2])
            full = lax.psum_scatter(full, "mp", scatter_dimension=0, tiled=False)
            return lax.psum_scatter(full, "dp", scatter_dimension=0, tiled=True).astype(f32)

        attend_total = own_block(keep_attend, send_attend)
        feed_total = own_block(
            jnp.concatenate([keep_a, keep_b], axis=1), jnp.concatenate([send_a, send_b], axis=1)
        )
        vector_total = lax.psum(vector_local, ("dp", "mp"))
    input_total = attend_total[:, : 3 * width].reshape(rows, 3, width)
    output_total = attend_total[:, 3 * width :].T
    pieces = feed_total.reshape(rows, 3, 2, part)
    expand_total = pieces[:, :, 0].reshape(rows, hidden)
    shrink_total = pieces[:, :, 1].reshape(rows, hidden).T
    vector_grad = vector_total[:6]
    head_total = lax.dynamic_slice_in_dim(vector_total[6:8], model_index * width, width, 1)
    bias_total = lax.dynamic_slice_in_dim(vector_total[8:].reshape(-1), model_index * hidden, hidden, 0)
    owned = jnp.sum(attend_total * attend_total) + jnp.sum(feed_total * feed_total)
    if cube:
        owned = cube_sum(jnp.full((8, 128), owned, f32))[0, 0]
    else:
        owned = lax.psum(owned, ("dp", "mp"))
    grad_norm = jnp.sqrt(owned + jnp.sum(vector_total * vector_total))
    factor = clip_norm / jnp.maximum(grad_norm, clip_norm)
    moment_input, square_input, updated_input = adam_step(
        input_weight, input_total, first_input, second_input, factor, rate
    )
    moment_output, square_output, updated_output = adam_step(
        output_weight, output_total, first_output, second_output, factor, rate
    )
    moment_expand, square_expand, updated_expand = adam_step(
        expand_weight, expand_total, first_expand, second_expand, factor, rate
    )
    moment_shrink, square_shrink, updated_shrink = adam_step(
        shrink_weight, shrink_total, first_shrink, second_shrink, factor, rate
    )
    moment_vectors, square_vectors, updated_vectors = adam_step(
        layer_vectors, vector_grad, first_vectors, second_vectors, factor, vector_rate
    )
    moment_head, square_head, updated_head = adam_step(
        head_bias, head_total, first_head, second_head, factor, vector_rate
    )
    moment_bias, square_bias, updated_bias = adam_step(
        expand_bias, bias_total, first_bias, second_bias, factor, vector_rate
    )
    return (
        block_out,
        token_grad,
        grad_norm,
        moment_input,
        square_input,
        updated_input,
        moment_output,
        square_output,
        updated_output,
        moment_expand,
        square_expand,
        updated_expand,
        moment_shrink,
        square_shrink,
        updated_shrink,
        moment_vectors,
        square_vectors,
        updated_vectors,
        moment_head,
        square_head,
        updated_head,
        moment_bias,
        square_bias,
        updated_bias,
    )


def solution(mesh):
    in_specs = (
        P(("dp", "mp"), None),
        P(("dp", "mp"), None),
        P("dp"),
        P("dp", None, "mp"),
        P("mp", "dp"),
        P("dp", "mp"),
        P("mp", "dp"),
        P(),
        P(None, "mp"),
        P("mp"),
        P("dp", None, "mp"),
        P("mp", "dp"),
        P("dp", "mp"),
        P("mp", "dp"),
        P(),
        P(None, "mp"),
        P("mp"),
        P("dp", None, "mp"),
        P("mp", "dp"),
        P("dp", "mp"),
        P("mp", "dp"),
        P(),
        P(None, "mp"),
        P("mp"),
    )
    out_specs = (
        P(("dp", "mp"), None),
        P(("dp", "mp"), None),
        P(),
        P("dp", None, "mp"),
        P("dp", None, "mp"),
        P("dp", None, "mp"),
        P("mp", "dp"),
        P("mp", "dp"),
        P("mp", "dp"),
        P("dp", "mp"),
        P("dp", "mp"),
        P("dp", "mp"),
        P("mp", "dp"),
        P("mp", "dp"),
        P("mp", "dp"),
        P(),
        P(),
        P(),
        P(None, "mp"),
        P(None, "mp"),
        P(None, "mp"),
        P("mp"),
        P("mp"),
        P("mp"),
    )
    return jax.shard_map(shards, mesh=mesh, in_specs=in_specs, out_specs=out_specs, check_vma=False)
```

time: 1300 us -> 392 us (0.30)
  waiting for transfers between devices: 594 us -> 98.4 us
  matrix products: 346 us -> 0 us
  blocking collectives: 151 us -> 0 us
  starting transfers between devices: 0.6 us -> 109 us
  Pallas kernels: 0 us -> 97 us
  other arithmetic: 96.2 us -> 26.3 us
  local copies, waits for them, and re-layouts: 77.1 us -> 52.5 us
  between operations: 22.8 us -> 5.51 us
    reduce_scatter x7 -> x0, waiting for transfers between devices: 409 us -> none  [the longest x1 96.9 us: shards(): lax.psum_scatter(jnp.dot(row_piece, wide_output, preferred_element_type=j...]
    dot_general x66 -> x0, matrix products: 333 us -> none  [the longest x8 84.3 us: backward_block(): jnp.einsum('hqk,qhd->khd', score_grad, queries, preferred_element_type=jn...]
    all_gather x6 -> x0, waiting for transfers between devices: 150 us -> none  [the longest x1 46.3 us: shards(): lax.all_gather(cotangent, 'mp', axis=0, tiled=True)]
    ppermute x0 -> x42, starting transfers between devices: none -> 109 us  [the longest x24 63.7 us: cube_permute(): return lax.ppermute(values, ('dp', 'mp'), pairs)]
    ppermute x0 -> x42, waiting for transfers between devices: none -> 98.4 us  [the longest x24 64 us: cube_permute(): return lax.ppermute(values, ('dp', 'mp'), pairs)]
    pallas_call x0 -> x9, Pallas kernels: none -> 97 us  [the longest x1 40.9 us: feed(): pl.pallas_call(feed_body, grid_spec=pltpu.PrefetchScalarGridSpec(num_scal...]
    psum x2 -> x0, blocking collectives: 81.2 us -> none  [the longest x1 41.1 us: shards(): squared = lax.psum(local_squares, ('dp', 'mp'))]
    all_gather x2 -> x0, blocking collectives: 70.2 us -> none  [the longest x1 38.8 us: shards(): lax.all_gather(lowered[0], 'dp', axis=0, tiled=True)]
  transfers between devices with their start and end apart: 14 -> 42, of which waited for: 10 -> 20; matrix products, arithmetic and copies ran while one was open for 28% -> 10% of each run, Pallas kernels for 0% -> 14%
where the time goes in v2:
time: 392 us; the launch traced here: 389 us
  starting transfers between devices  109 us (28%)
  waiting for transfers between devices  98.4 us (25%)
  Pallas kernels  97 us (25%)
  local copies, waits for them, and re-layouts  52.5 us (13%)
  other arithmetic  26.3 us (7%)
  between operations  5.51 us (1%)
    ppermute x24, waiting for transfers between devices, cube_permute(): return lax.ppermute(values, ('dp', 'mp'), pairs)  64 us
    ppermute x24, starting transfers between devices, cube_permute(): return lax.ppermute(values, ('dp', 'mp'), pairs)  63.7 us
    ppermute x18, starting transfers between devices, bit_permute(): lax.ppermute(values, ('dp', 'mp'), [(device, device ^ 1 << bit) for devic...  45.4 us
    unnamed x137, local copies, waits for them, and re-layouts  42.2 us
    pallas_call x1, Pallas kernels, feed(): pl.pallas_call(feed_body, grid_spec=pltpu.PrefetchScalarGridSpec(num_scal...  40.9 us
    ppermute x18, waiting for transfers between devices, bit_permute(): lax.ppermute(values, ('dp', 'mp'), [(device, device ^ 1 << bit) for devic...  34.4 us
    add x9, other arithmetic, cube_scatter(): keep, other = (keep[:half] + other[:half], arrived)  13.9 us
    pallas_call x1, Pallas kernels, project(): pl.pallas_call(project_body, grid_spec=pltpu.PrefetchScalarGridSpec(num_s...  9.93 us
  transfers between devices with their start and end apart: 42, of which 20 were waited for; matrix products, arithmetic and copies ran while one was open for 10% of the time, Pallas kernels for 14%

profile of v2, /device:TPU:0, one launch (start us, length us, event | category | flops | bytes accessed | tf_op | source)
XLA Modules:
  0.0 388.7 jit_solution(5080582196512207203)
XLA Ops:
  5.9 3.6 collective-permute-start
  9.7 2.9 collective-permute-start.7
  14.8 1.5 collective-permute-start.6
  16.3 13.0 %collective-permute-start.1 = (bf16[2,96,768]{2,1,0:T(8,128)(2,1)S(1)}, bf16[2,96,768]{2,1,0:T(8,128)(2,1)S(1)}, u32[]{:S(2)}, u32[]{:S(2)}) collective-permute-start(bf16[2,96,768]{2,1,0:T(8,128)(2,1)S(1)} %pad_maximum_fusion.6), channel_id=1, source_target_pairs={{0,8},{1,17},{2,10},{3,19},{4,12},{5,21},{6,14},{7,23},{8,0},{9,25... | collective-permute-start | bytes 884744 | tf_op jit(solution)/shard_map/ppermute | solution.py:633
  29.3 3.1 collective-permute-start.12
  32.5 3.2 collective-permute-start.8
  35.7 10.0 %collective-permute-done.1 = bf16[2,96,768]{2,1,0:T(8,128)(2,1)S(1)} collective-permute-done((bf16[2,96,768]{2,1,0:T(8,128)(2,1)S(1)}, bf16[2,96,768]{2,1,0:T(8,128)(2,1)S(1)}, u32[]{:S(2)}, u32[]{:S(2)}) %collective-permute-start.1) | collective-permute-done | bytes 294944 | tf_op jit(solution)/shard_map/ppermute | solution.py:633
  45.7 1.9 collective-permute-start.2
  49.6 2.4 collective-permute-done.12
  52.1 1.9 collective-permute-start.13
  54.0 2.2 collective-permute-done.2
  56.3 2.0 collective-permute-start.3
  58.4 1.9 collective-permute-start.9
  61.7 7.1 %collective-permute-done.13 = bf16[4,48,1536]{2,1,0:T(8,128)(2,1)S(1)} collective-permute-done((bf16[4,48,1536]{2,1,0:T(8,128)(2,1)S(1)}, bf16[4,48,1536]{2,1,0:T(8,128)(2,1)S(1)}, u32[]{:S(2)}, u32[]{:S(2)}) %collective-permute-start.13) | collective-permute-done | bytes 589856 | tf_op jit(solution)/shard_map/ppermute | solution.py:633
  68.9 2.0 collective-permute-start.14
  70.9 10.5 %collective-permute-done.9 = bf16[4,48,1536]{2,1,0:T(8,128)(2,1)S(1)} collective-permute-done((bf16[4,48,1536]{2,1,0:T(8,128)(2,1)S(1)}, bf16[4,48,1536]{2,1,0:T(8,128)(2,1)S(1)}, u32[]{:S(2)}, u32[]{:S(2)}) %collective-permute-start.9) | collective-permute-done | bytes 589856 | tf_op jit(solution)/shard_map/ppermute | solution.py:633
  81.6 2.0 collective-permute-start.10
  89.1 5.8 %collective-permute-start.16 = (bf16[16,48,1536]{2,1,0:T(8,128)(2,1)}, bf16[16,48,1536]{2,1,0:T(8,128)(2,1)}, u32[]{:S(2)}, u32[]{:S(2)}) collective-permute-start(bf16[16,48,1536]{2,1,0:T(8,128)(2,1)} %constant_dynamic-update-slice_fusion.10.mine_b), channel_id=1, source_target_pairs={{0,1},{1,0},{2,3},{3,2},{4,5},{5,4},{6,7},{7,6},{8,9},{9,8},{10,11... | collective-permute-start | bytes 7077896 | tf_op jit(solution)/shard_map/ppermute | solution.py:637
  94.8 3.0 collective-permute-done.10
  98.9 8.2 %collective-permute-start.15 = (bf16[16,48,1536]{2,1,0:T(8,128)(2,1)}, bf16[16,48,1536]{2,1,0:T(8,128)(2,1)}, u32[]{:S(2)}, u32[]{:S(2)}) collective-permute-start(bf16[16,48,1536]{2,1,0:T(8,128)(2,1)} %constant_dynamic-update-slice_fusion.5.mine_a), channel_id=1, source_target_pairs={{0,1},{1,0},{2,3},{3,2},{4,5},{5,4},{6,7},{7,6},{8,9},{9,8},{10,11... | collective-permute-start | bytes 7077896 | tf_op jit(solution)/shard_map/ppermute | solution.py:637
  108.5 2.6 prepare.1
  116.4 1.4 copy-done.21
  117.8 9.9 %project.1 = (bf16[1024,2304]{1,0:T(8,128)(2,1)S(1)}, bf16[4,768,768]{2,1,0:T(8,128)(2,1)}) custom-call(s32[1]{0:T(128)} %bitcast.3.core_ref, s32[4,8]{1,0:T(4,128)S(1)} %add_select_fusion.spots_ref, bf16[1024,768]{1,0:T(8,128)(2,1)S(1)} %copy-done.21, bf16[16,96,768]{2,1,0:T(8,128)(2,1)} %constant_dynamic-update-slice_fusion.mine_ref, ...), custom_call_target="tpu_custom_call" | custom-call | flops 3623878656 | bytes 12582912 | tf_op jit(solution)/shard_map/project/pallas_call | solution.py:293
  127.7 6.1 %attend_forward.1 = (bf16[1024,768]{1,0:T(8,128)(2,1)S(1)}, f32[6,2,1024]{2,1,0:T(2,128)S(1)}) custom-call(s32[1]{0:T(128)} %dynamic_slice.9.length_ref, bf16[1024,2304]{1,0:T(8,128)(2,1)S(1)} %get-tuple-element.53.q_ref.k_ref.v_ref, bf16[1024,2304]{1,0:T(8,128)(2,1)S(1)} %get-tuple-element.53.q_ref.k_ref.v_ref, ...), custom_call_target="tpu_custom_call" | custom-call | flops 8053063680 | bytes 6291456 | tf_op jit(solution)/shard_map/attend_forward/pallas_call | solution.py:116
  133.9 3.7 attend_out.1
  137.6 1.6 copy-done.10
  141.6 40.9 %feed.1 = (f32[1024,768]{1,0:T(8,128)}, f32[1024,768]{1,0:T(8,128)}, bf16[16,48,1536]{2,1,0:T(8,128)(2,1)}, bf16[16,48,1536]{2,1,0:T(8,128)(2,1)}, bf16[16,48,15...) custom-call(s32[2,2,8]{2,1,0:T(2,128)} %fusion.12.spots_ref, bf16[1024,768]{1,0:T(8,128)(2,1)} %copy-done.22, ...), custom_call_target="tpu_custom_call" | custom-call | flops 28991029248 | bytes 31457280 | tf_op jit(solution)/shard_map/feed/pallas_call | solution.py:427
  183.1 1.4 copy-done.5
  184.5 1.9 copy-done.11
  186.4 1.9 copy-done.12
  188.2 1.9 copy-done.13
  190.1 8.9 %middle_back.1 = (bf16[1024,768]{1,0:T(8,128)(2,1)}, f32[1024,768]{1,0:T(8,128)S(1)}, bf16[1024,768]{1,0:T(8,128)(2,1)S(1)}, f32[768,768]{1,0:T(8,128)S(1)}, f32[4,768]{1,0:T(4,128)S(1)}) custom-call(s32[1]{0:T(128)} %dynamic_slice.9.length_ref, f32[1024,768]{1,0:T(8,128)S(1)} %copy-done.13, f32[1024,768]{1,0:T(8,128)S(1)} %copy-done.12, ...), custom_call_target="tpu_custom_call" | custom-call | flops 2415919104 | bytes 22020096 | tf_op jit(solution)/shard_map/middle_back/pallas_call | solution.py:505
  199.0 1.6 copy-done.8
  200.6 9.5 %attend_backward.1.back_ref = bf16[3,1024,768]{2,1,0:T(8,128)(2,1)} custom-call(s32[1]{0:T(128)} %dynamic_slice.9.length_ref, bf16[1024,2304]{1,0:T(8,128)(2,1)} %copy-done.24, bf16[1024,2304]{1,0:T(8,128)(2,1)} %copy-done.24, bf16[1024,2304]{1,0:T(8,128)(2,1)} %copy-done.24, bf16[1024,768]{1,0:T(8,128)(2,1)S(1)} %get-tuple-element.63.do_ref, ...), custom_call_target="tpu_custom_call" | custom-call | flops 20132659200 | bytes 11010048 | tf_op jit(solution)/shard_map/attend_backward/pallas_call | solution.py:206
  210.1 2.3 copy-done.6
  212.5 8.6 %input_grad.1 = (bf16[16,96,768]{2,1,0:T(8,128)(2,1)S(1)}, bf16[16,96,768]{2,1,0:T(8,128)(2,1)}, f32[3,1,768]{2,1,0:T(1,128)S(1)}) custom-call(s32[1]{0:T(128)} %bitcast.3.core_ref, s32[4,8]{1,0:T(4,128)S(1)} %add_select_fusion.spots_ref, bf16[768,1024]{1,0:T(8,128)(2,1)S(1)} %copy-done.18, bf16[3,1024,768]{2,1,0:T(8,128)(2,1)S(1)} %copy-done.6, ...), custom_call_target="tpu_custom_call" | custom-call | flops 3623878656 | bytes 11010048 | tf_op jit(solution)/shard_map/input_grad/pallas_call | solution.py:567
  223.2 2.3 copy-done
  225.5 2.3 copy-done.7
  227.9 1.9 copy-done.9
  229.8 6.8 %token_back.1 = (bf16[1024,768]{1,0:T(8,128)(2,1)}, f32[2,768]{1,0:T(2,128)S(1)}) custom-call(bf16[3,1024,768]{2,1,0:T(8,128)(2,1)S(1)} %copy-done.7, bf16[4,768,768]{2,1,0:T(8,128)(2,1)S(1)} %copy-done, bf16[1024,768]{1,0:T(8,128)(2,1)S(1)} %copy-done.1, f32[1024,768]{1,0:T(8,128)S(1)} %copy-done.9, f32[6,768]{1,0:T(8,128)S(1)} %copy-done.16), custom_call_target="tpu_custom_call" | custom-call | flops 3623878656 | bytes 12582912 | tf_op jit(solution)/shard_map/token_back/pallas_call | solution.py:609
  236.6 3.0 slice_add_fusion.3
  239.6 18.4 %collective-permute-start.23 = (bf16[8,48,1536]{2,1,0:T(8,128)(2,1)}, bf16[8,48,1536]{2,1,0:T(8,128)(2,1)}, u32[]{:S(2)}, u32[]{:S(2)}) collective-permute-start(bf16[8,48,1536]{2,1,0:T(8,128)(2,1)} %get-tuple-element.157), channel_id=1, source_target_pairs={{0,2},{1,5},{2,0},{3,7},{4,6},{5,1},{6,4},{7,3},{8,10},{9,13},{10,... | collective-permute-start | bytes 3538952 | tf_op jit(solution)/shard_map/ppermute | solution.py:633
  258.1 3.1 slice_add_fusion.1
  261.2 3.3 slice_add_fusion.5
  264.5 2.0 collective-permute-start.18
  266.6 11.2 %collective-permute-start.37 = (f32[12,768]{1,0:T(8,128)S(1)}, f32[12,768]{1,0:T(8,128)S(1)}, u32[]{:S(2)}, u32[]{:S(2)}) collective-permute-start(f32[12,768]{1,0:T(8,128)S(1)} %concatenate.79), channel_id=1, source_target_pairs={{0,1},{1,0},{2,3},{3,2},{4,5},{5,4},{6,7},{7,6},{8,9},{9,8},{10,11... | collective-permute-start | bytes 110600 | tf_op jit(solution)/shard_map/ppermute | solution.py:637
  278.7 20.1 %collective-permute-done.38 = f32[12,768]{1,0:T(8,128)S(1)} collective-permute-done((f32[12,768]{1,0:T(8,128)S(1)}, f32[12,768]{1,0:T(8,128)S(1)}, u32[]{:S(2)}, u32[]{:S(2)}) %collective-permute-start.38) | collective-permute-done | bytes 36896 | tf_op jit(solution)/shard_map/ppermute | solution.py:637
  298.8 14.1 %collective-permute-start.39 = (f32[12,768]{1,0:T(8,128)S(1)}, f32[12,768]{1,0:T(8,128)S(1)}, u32[]{:S(2)}, u32[]{:S(2)}) collective-permute-start(f32[12,768]{1,0:T(8,128)S(1)} %add.346), channel_id=1, source_target_pairs={{0,4},{1,5},{2,6},{3,7},{4,0},{5,1},{6,2},{7,3},{8,12},{9,13},{10,... | collective-permute-start | bytes 110600 | tf_op jit(solution)/shard_map/ppermute | solution.py:637
  314.4 1.5 slice_add_fusion.7
  315.9 2.1 collective-permute-start.29
  317.9 1.4 slice_add_fusion.11
  319.5 4.7 %collective-permute-done.24 = bf16[4,48,1536]{2,1,0:T(8,128)(2,1)S(1)} collective-permute-done((bf16[4,48,1536]{2,1,0:T(8,128)(2,1)S(1)}, bf16[4,48,1536]{2,1,0:T(8,128)(2,1)S(1)}, u32[]{:S(2)}, u32[]{:S(2)}) %collective-permute-start.24) | collective-permute-done | bytes 589856 | tf_op jit(solution)/shard_map/ppermute | solution.py:633
  324.4 6.2 %collective-permute-done.29 = bf16[4,48,1536]{2,1,0:T(8,128)(2,1)S(1)} collective-permute-done((bf16[4,48,1536]{2,1,0:T(8,128)(2,1)S(1)}, bf16[4,48,1536]{2,1,0:T(8,128)(2,1)S(1)}, u32[]{:S(2)}, u32[]{:S(2)}) %collective-permute-start.29) | collective-permute-done | bytes 589856 | tf_op jit(solution)/shard_map/ppermute | solution.py:633
  330.7 6.2 %collective-permute-done.19 = bf16[4,96,768]{2,1,0:T(8,128)(2,1)S(1)} collective-permute-done((bf16[4,96,768]{2,1,0:T(8,128)(2,1)S(1)}, bf16[4,96,768]{2,1,0:T(8,128)(2,1)S(1)}, u32[]{:S(2)}, u32[]{:S(2)}) %collective-permute-start.19) | collective-permute-done | bytes 589856 | tf_op jit(solution)/shard_map/ppermute | solution.py:633
  337.1 2.6 collective-permute-start.26
  340.1 5.3 %collective-permute-done.20 = bf16[2,96,768]{2,1,0:T(8,128)(2,1)S(1)} collective-permute-done((bf16[2,96,768]{2,1,0:T(8,128)(2,1)S(1)}, bf16[2,96,768]{2,1,0:T(8,128)(2,1)S(1)}, u32[]{:S(2)}, u32[]{:S(2)}) %collective-permute-start.20) | collective-permute-done | bytes 294944 | tf_op jit(solution)/shard_map/ppermute | solution.py:633
  345.8 2.7 collective-permute-done.31
  348.6 3.7 collective-permute-done.21
  356.9 2.4 collective-permute-done.40
  360.1 1.8 collective-permute-start.34
  361.9 2.7 collective-permute-done.41
  365.8 3.3 collective-permute-done.35
  369.7 3.9 %collective-permute-done.36 = f32[8,128]{1,0:T(8,128)S(1)} collective-permute-done((f32[8,128]{1,0:T(8,128)S(1)}, f32[8,128]{1,0:T(8,128)S(1)}, u32[]{:S(2)}, u32[]{:S(2)}) %collective-permute-start.36) | collective-permute-done | bytes 4128 | tf_op jit(solution)/shard_map/ppermute | solution.py:637
  375.5 1.9 fusion.4
  (270 shorter events, 49.8 us)
Async XLA Ops:
  0.7 8.8 %copy-start.30 = (f32[96,768]{1,0:T(8,128)S(1)}, f32[96,768]{1,0:T(8,128)}, u32[]{:S(2)}) copy-start(f32[96,768]{1,0:T(8,128)} %param.31) | copy-start | bytes 884740
  0.7 8.8 %copy-start.29 = (f32[768,96]{0,1:T(8,128)S(1)}, f32[768,96]{0,1:T(8,128)}, u32[]{:S(2)}) copy-start(f32[768,96]{0,1:T(8,128)} %param.32) | copy-start | bytes 884740
  2.3 12.4 %collective-permute-start.5 = (f32[4,1152]{1,0:T(4,128)S(1)}, f32[4,1152]{1,0:T(4,128)S(1)}, u32[]{:S(2)}, u32[]{:S(2)}) collective-permute-start(f32[4,1152]{1,0:T(4,128)S(1)} %broadcast_select_fusion), channel_id=1, source_target_pairs={{0,1},{1,0},{2,3},{3,2},{4,5},{5,4},{6,7},{7,6},{8,9},{9,8},{10,11... | collective-permute-start | bytes 55304 | tf_op jit(solution)/shard_map/ppermute | solution.py:637
  3.8 5.9 %copy-start.32 = (f32[192,96]{0,1:T(8,128)}, f32[192,96]{0,1:T(8,128)S(1)}, u32[]{:S(2)}) copy-start(f32[192,96]{0,1:T(8,128)S(1)} %copy.66) | copy-start | bytes 221188
  5.9 10.4 %collective-permute-start = (bf16[1,96,768]{2,1,0:T(8,128)(2,1)S(1)}, bf16[1,96,768]{2,1,0:T(8,128)(2,1)S(1)}, u32[]{:S(2)}, u32[]{:S(2)}) collective-permute-start(bf16[1,96,768]{2,1,0:T(8,128)(2,1)S(1)} %get-tuple-element.155), channel_id=1, source_target_pairs={{0,16},{1,3},{2,18},{3,1},{4,20},{5,7},{6,22},{7,5},{8,24},{9,11},... | collective-permute-start | bytes 442376 | tf_op jit(solution)/shard_map/ppermute | solution.py:633
  9.7 19.7 %collective-permute-start.11 = (bf16[1,48,1536]{2,1,0:T(8,128)(2,1)S(1)}, bf16[1,48,1536]{2,1,0:T(8,128)(2,1)S(1)}, u32[]{:S(2)}, u32[]{:S(2)}) collective-permute-start(bf16[1,48,1536]{2,1,0:T(8,128)(2,1)S(1)} %get-tuple-element.174), channel_id=1, source_target_pairs={{0,16},{1,3},{2,18},{3,1},{4,20},{5,7},{6,22},{7,5},{8,24},{9,11},... | collective-permute-start | bytes 442376 | tf_op jit(solution)/shard_map/ppermute | solution.py:633
  9.7 22.7 %collective-permute-start.7 = (bf16[1,48,1536]{2,1,0:T(8,128)(2,1)S(1)}, bf16[1,48,1536]{2,1,0:T(8,128)(2,1)S(1)}, u32[]{:S(2)}, u32[]{:S(2)}) collective-permute-start(bf16[1,48,1536]{2,1,0:T(8,128)(2,1)S(1)} %get-tuple-element.175), channel_id=1, source_target_pairs={{0,16},{1,3},{2,18},{3,1},{4,20},{5,7},{6,22},{7,5},{8,24},{9,11},... | collective-permute-start | bytes 442376 | tf_op jit(solution)/shard_map/ppermute | solution.py:633
  14.8 99.9 %collective-permute-start.6 = (f32[4,1152]{1,0:T(4,128)S(1)}, f32[4,1152]{1,0:T(4,128)S(1)}, u32[]{:S(2)}, u32[]{:S(2)}) collective-permute-start(f32[4,1152]{1,0:T(4,128)S(1)} %fusion.14), channel_id=1, source_target_pairs={{0,2},{1,3},{2,0},{3,1},{4,6},{5,7},{6,4},{7,5},{8,10},{9,11},{10,... | collective-permute-start | bytes 55304 | tf_op jit(solution)/shard_map/ppermute | solution.py:637
  16.3 29.4 %collective-permute-start.1 = (bf16[2,96,768]{2,1,0:T(8,128)(2,1)S(1)}, bf16[2,96,768]{2,1,0:T(8,128)(2,1)S(1)}, u32[]{:S(2)}, u32[]{:S(2)}) collective-permute-start(bf16[2,96,768]{2,1,0:T(8,128)(2,1)S(1)} %pad_maximum_fusion.6), channel_id=1, source_target_pairs={{0,8},{1,17},{2,10},{3,19},{4,12},{5,21},{6,14},{7,23},{8,0},{9,25... | collective-permute-start | bytes 884744 | tf_op jit(solution)/shard_map/ppermute | solution.py:633
  29.3 22.7 %collective-permute-start.12 = (bf16[2,48,1536]{2,1,0:T(8,128)(2,1)S(1)}, bf16[2,48,1536]{2,1,0:T(8,128)(2,1)S(1)}, u32[]{:S(2)}, u32[]{:S(2)}) collective-permute-start(bf16[2,48,1536]{2,1,0:T(8,128)(2,1)S(1)} %pad_maximum_fusion.8), channel_id=1, source_target_pairs={{0,8},{1,17},{2,10},{3,19},{4,12},{5,21},{6,14},{7,23},{8,0},{9,25... | collective-permute-start | bytes 884744 | tf_op jit(solution)/shard_map/ppermute | solution.py:633
  32.5 25.8 %collective-permute-start.8 = (bf16[2,48,1536]{2,1,0:T(8,128)(2,1)S(1)}, bf16[2,48,1536]{2,1,0:T(8,128)(2,1)S(1)}, u32[]{:S(2)}, u32[]{:S(2)}) collective-permute-start(bf16[2,48,1536]{2,1,0:T(8,128)(2,1)S(1)} %pad_maximum_fusion.7), channel_id=1, source_target_pairs={{0,8},{1,17},{2,10},{3,19},{4,12},{5,21},{6,14},{7,23},{8,0},{9,25... | collective-permute-start | bytes 884744 | tf_op jit(solution)/shard_map/ppermute | solution.py:633
  45.7 10.4 %collective-permute-start.2 = (bf16[4,96,768]{2,1,0:T(8,128)(2,1)S(1)}, bf16[4,96,768]{2,1,0:T(8,128)(2,1)S(1)}, u32[]{:S(2)}, u32[]{:S(2)}) collective-permute-start(bf16[4,96,768]{2,1,0:T(8,128)(2,1)S(1)} %pad_maximum_fusion.3), channel_id=1, source_target_pairs={{0,4},{1,9},{2,6},{3,11},{4,0},{5,13},{6,2},{7,15},{8,12},{9,1},{1... | collective-permute-start | bytes 1769480 | tf_op jit(solution)/shard_map/ppermute | solution.py:633
  52.1 16.7 %collective-permute-start.13 = (bf16[4,48,1536]{2,1,0:T(8,128)(2,1)S(1)}, bf16[4,48,1536]{2,1,0:T(8,128)(2,1)S(1)}, u32[]{:S(2)}, u32[]{:S(2)}) collective-permute-start(bf16[4,48,1536]{2,1,0:T(8,128)(2,1)S(1)} %pad_maximum_fusion.5), channel_id=1, source_target_pairs={{0,4},{1,9},{2,6},{3,11},{4,0},{5,13},{6,2},{7,15},{8,12},{9,1},{1... | collective-permute-start | bytes 1769480 | tf_op jit(solution)/shard_map/ppermute | solution.py:633
  56.3 28.1 %collective-permute-start.3 = (bf16[8,96,768]{2,1,0:T(8,128)(2,1)S(1)}, bf16[8,96,768]{2,1,0:T(8,128)(2,1)S(1)}, u32[]{:S(2)}, u32[]{:S(2)}) collective-permute-start(bf16[8,96,768]{2,1,0:T(8,128)(2,1)S(1)} %pad_maximum_fusion), channel_id=1, source_target_pairs={{0,2},{1,5},{2,0},{3,7},{4,6},{5,1},{6,4},{7,3},{8,10},{9,13},{10,... | collective-permute-start | bytes 3538952 | tf_op jit(solution)/shard_map/ppermute | solution.py:633
  58.4 23.0 %collective-permute-start.9 = (bf16[4,48,1536]{2,1,0:T(8,128)(2,1)S(1)}, bf16[4,48,1536]{2,1,0:T(8,128)(2,1)S(1)}, u32[]{:S(2)}, u32[]{:S(2)}) collective-permute-start(bf16[4,48,1536]{2,1,0:T(8,128)(2,1)S(1)} %pad_maximum_fusion.4), channel_id=1, source_target_pairs={{0,4},{1,9},{2,6},{3,11},{4,0},{5,13},{6,2},{7,15},{8,12},{9,1},{1... | collective-permute-start | bytes 1769480 | tf_op jit(solution)/shard_map/ppermute | solution.py:633
  68.9 19.0 %collective-permute-start.14 = (bf16[8,48,1536]{2,1,0:T(8,128)(2,1)S(1)}, bf16[8,48,1536]{2,1,0:T(8,128)(2,1)S(1)}, u32[]{:S(2)}, u32[]{:S(2)}) collective-permute-start(bf16[8,48,1536]{2,1,0:T(8,128)(2,1)S(1)} %pad_maximum_fusion.2), channel_id=1, source_target_pairs={{0,2},{1,5},{2,0},{3,7},{4,6},{5,1},{6,4},{7,3},{8,10},{9,13},{10,... | collective-permute-start | bytes 3538952 | tf_op jit(solution)/shard_map/ppermute | solution.py:633
  81.6 16.3 %collective-permute-start.10 = (bf16[8,48,1536]{2,1,0:T(8,128)(2,1)S(1)}, bf16[8,48,1536]{2,1,0:T(8,128)(2,1)S(1)}, u32[]{:S(2)}, u32[]{:S(2)}) collective-permute-start(bf16[8,48,1536]{2,1,0:T(8,128)(2,1)S(1)} %pad_maximum_fusion.1), channel_id=1, source_target_pairs={{0,2},{1,5},{2,0},{3,7},{4,6},{5,1},{6,4},{7,3},{8,10},{9,13},{10,... | collective-permute-start | bytes 3538952 | tf_op jit(solution)/shard_map/ppermute | solution.py:633
  85.5 30.9 %collective-permute-start.4 = (bf16[16,96,768]{2,1,0:T(8,128)(2,1)}, bf16[16,96,768]{2,1,0:T(8,128)(2,1)}, u32[]{:S(2)}, u32[]{:S(2)}) collective-permute-start(bf16[16,96,768]{2,1,0:T(8,128)(2,1)} %constant_dynamic-update-slice_fusion.mine_ref), channel_id=1, source_target_pairs={{0,1},{1,0},{2,3},{3,2},{4,5},{5,4},{6,7},{7,6},{8,9},{9,8},{10,11... | collective-permute-start | bytes 7077896 | tf_op jit(solution)/shard_map/ppermute | solution.py:637
  87.9 20.6 %copy-start.2 = (bf16[1024,768]{1,0:T(8,128)(2,1)S(1)}, bf16[1024,768]{1,0:T(8,128)(2,1)}, u32[]{:S(2)}) copy-start(bf16[1024,768]{1,0:T(8,128)(2,1)} %up_ref.5) | copy-start | bytes 4718596
  89.1 19.4 %copy-start.1 = (bf16[1024,768]{1,0:T(8,128)(2,1)S(1)}, bf16[1024,768]{1,0:T(8,128)(2,1)}, u32[]{:S(2)}) copy-start(bf16[1024,768]{1,0:T(8,128)(2,1)} %x_ref.5) | copy-start | bytes 4718596
  89.1 19.4 %copy-start.16 = (f32[6,768]{1,0:T(8,128)S(1)}, f32[6,768]{1,0:T(8,128)}, u32[]{:S(2)}) copy-start(f32[6,768]{1,0:T(8,128)} %vec_ref.7) | copy-start | bytes 55300
  89.1 52.5 %collective-permute-start.16 = (bf16[16,48,1536]{2,1,0:T(8,128)(2,1)}, bf16[16,48,1536]{2,1,0:T(8,128)(2,1)}, u32[]{:S(2)}, u32[]{:S(2)}) collective-permute-start(bf16[16,48,1536]{2,1,0:T(8,128)(2,1)} %constant_dynamic-update-slice_fusion.10.mine_b), channel_id=1, source_target_pairs={{0,1},{1,0},{2,3},{3,2},{4,5},{5,4},{6,7},{7,6},{8,9},{9,8},{10,11... | collective-permute-start | bytes 7077896 | tf_op jit(solution)/shard_map/ppermute | solution.py:637
  98.9 42.6 %collective-permute-start.15 = (bf16[16,48,1536]{2,1,0:T(8,128)(2,1)}, bf16[16,48,1536]{2,1,0:T(8,128)(2,1)}, u32[]{:S(2)}, u32[]{:S(2)}) collective-permute-start(bf16[16,48,1536]{2,1,0:T(8,128)(2,1)} %constant_dynamic-update-slice_fusion.5.mine_a), channel_id=1, source_target_pairs={{0,1},{1,0},{2,3},{3,2},{4,5},{5,4},{6,7},{7,6},{8,9},{9,8},{10,11... | collective-permute-start | bytes 7077896 | tf_op jit(solution)/shard_map/ppermute | solution.py:637
  127.7 6.1 %copy-start.24 = (bf16[1024,2304]{1,0:T(8,128)(2,1)}, bf16[1024,2304]{1,0:T(8,128)(2,1)S(1)}, u32[]{:S(2)}) copy-start(bf16[1024,2304]{1,0:T(8,128)(2,1)S(1)} %get-tuple-element.53.q_ref.k_ref.v_ref) | copy-start | bytes 14155780
  127.7 6.1 %slice-start = ((s8[4718592]{0:T(1024)(128)(4,1)}), s8[4194304]{0:T(1024)(128)(4,1)S(1)}, s32[]{:S(2)}) async-start(s8[4718592]{0:T(1024)(128)(4,1)} %bitcast.61), calls=%async_computation | async-start | bytes 8388608
  127.7 6.1 %slice-start.1 = ((s8[4718592]{0:T(1024)(128)(4,1)}), s8[524288]{0:T(1024)(128)(4,1)S(1)}, s32[]{:S(2)}) async-start(s8[4718592]{0:T(1024)(128)(4,1)} %bitcast.61), calls=%async_computation.1 | async-start | bytes 1048576
  133.8 3.8 copy-start.4
  141.6 41.5 %copy-start.3 = (bf16[1024,768]{1,0:T(8,128)(2,1)S(1)}, bf16[1024,768]{1,0:T(8,128)(2,1)}, u32[]{:S(2)}) copy-start(bf16[1024,768]{1,0:T(8,128)(2,1)} %up_ref.5) | copy-start | bytes 4718596
  182.5 54.1 %collective-permute-start.22 = (bf16[16,48,1536]{2,1,0:T(8,128)(2,1)}, bf16[16,48,1536]{2,1,0:T(8,128)(2,1)}, u32[]{:S(2)}, u32[]{:S(2)}) collective-permute-start(bf16[16,48,1536]{2,1,0:T(8,128)(2,1)} %get-tuple-element.72), channel_id=1, source_target_pairs={{0,1},{1,0},{2,3},{3,2},{4,5},{5,4},{6,7},{7,6},{8,9},{9,8},{10,11... | collective-permute-start | bytes 7077896 | tf_op jit(solution)/shard_map/ppermute | solution.py:637
  182.6 75.5 %collective-permute-start.27 = (bf16[16,48,1536]{2,1,0:T(8,128)(2,1)}, bf16[16,48,1536]{2,1,0:T(8,128)(2,1)}, u32[]{:S(2)}, u32[]{:S(2)}) collective-permute-start(bf16[16,48,1536]{2,1,0:T(8,128)(2,1)} %get-tuple-element.74), channel_id=1, source_target_pairs={{0,1},{1,0},{2,3},{3,2},{4,5},{5,4},{6,7},{7,6},{8,9},{9,8},{10,11... | collective-permute-start | bytes 7077896 | tf_op jit(solution)/shard_map/ppermute | solution.py:637
  200.6 9.5 %copy-start.18 = (bf16[768,1024]{1,0:T(8,128)(2,1)S(1)}, bf16[768,1024]{1,0:T(8,128)(2,1)}, u32[]{:S(2)}) copy-start(bf16[768,1024]{1,0:T(8,128)(2,1)} %copy-done.17) | copy-start | bytes 4718596
  212.5 10.1 %copy-start.45 = (f32[6,1,512]{2,1,0:T(1,128)S(1)}, f32[6,1,512]{2,1,0:T(1,128)}, u32[]{:S(2)}) copy-start(f32[6,1,512]{2,1,0:T(1,128)} %get-tuple-element.78) | copy-start | bytes 36868
  222.5 38.8 %collective-permute-start.17 = (bf16[16,96,768]{2,1,0:T(8,128)(2,1)}, bf16[16,96,768]{2,1,0:T(8,128)(2,1)}, u32[]{:S(2)}, u32[]{:S(2)}) collective-permute-start(bf16[16,96,768]{2,1,0:T(8,128)(2,1)} %get-tuple-element.70), channel_id=1, source_target_pairs={{0,1},{1,0},{2,3},{3,2},{4,5},{5,4},{6,7},{7,6},{8,9},{9,8},{10,11... | collective-permute-start | bytes 7077896 | tf_op jit(solution)/shard_map/ppermute | solution.py:637
  229.8 6.8 %copy-start.27 = (bf16[16,48,1536]{2,1,0:T(8,128)(2,1)S(1)}, bf16[16,48,1536]{2,1,0:T(8,128)(2,1)}, u32[]{:S(2)}) copy-start(bf16[16,48,1536]{2,1,0:T(8,128)(2,1)} %get-tuple-element.71) | copy-start | bytes 7077892
  236.6 21.5 %copy-start.26 = (bf16[16,48,1536]{2,1,0:T(8,128)(2,1)S(1)}, bf16[16,48,1536]{2,1,0:T(8,128)(2,1)}, u32[]{:S(2)}) copy-start(bf16[16,48,1536]{2,1,0:T(8,128)(2,1)} %get-tuple-element.73) | copy-start | bytes 7077892
  239.6 73.2 %collective-permute-start.23 = (bf16[8,48,1536]{2,1,0:T(8,128)(2,1)}, bf16[8,48,1536]{2,1,0:T(8,128)(2,1)}, u32[]{:S(2)}, u32[]{:S(2)}) collective-permute-start(bf16[8,48,1536]{2,1,0:T(8,128)(2,1)} %get-tuple-element.157), channel_id=1, source_target_pairs={{0,2},{1,5},{2,0},{3,7},{4,6},{5,1},{6,4},{7,3},{8,10},{9,13},{10,... | collective-permute-start | bytes 3538952 | tf_op jit(solution)/shard_map/ppermute | solution.py:633
  261.1 53.2 %collective-permute-start.28 = (bf16[8,48,1536]{2,1,0:T(8,128)(2,1)}, bf16[8,48,1536]{2,1,0:T(8,128)(2,1)}, u32[]{:S(2)}, u32[]{:S(2)}) collective-permute-start(bf16[8,48,1536]{2,1,0:T(8,128)(2,1)} %get-tuple-element.159), channel_id=1, source_target_pairs={{0,2},{1,5},{2,0},{3,7},{4,6},{5,1},{6,4},{7,3},{8,10},{9,13},{10,... | collective-permute-start | bytes 3538952 | tf_op jit(solution)/shard_map/ppermute | solution.py:633
  264.5 53.4 %collective-permute-start.18 = (bf16[8,96,768]{2,1,0:T(8,128)(2,1)}, bf16[8,96,768]{2,1,0:T(8,128)(2,1)}, u32[]{:S(2)}, u32[]{:S(2)}) collective-permute-start(bf16[8,96,768]{2,1,0:T(8,128)(2,1)} %get-tuple-element.161), channel_id=1, source_target_pairs={{0,2},{1,5},{2,0},{3,7},{4,6},{5,1},{6,4},{7,3},{8,10},{9,13},{10,... | collective-permute-start | bytes 3538952 | tf_op jit(solution)/shard_map/ppermute | solution.py:633
  266.6 12.1 %collective-permute-start.37 = (f32[12,768]{1,0:T(8,128)S(1)}, f32[12,768]{1,0:T(8,128)S(1)}, u32[]{:S(2)}, u32[]{:S(2)}) collective-permute-start(f32[12,768]{1,0:T(8,128)S(1)} %concatenate.79), channel_id=1, source_target_pairs={{0,1},{1,0},{2,3},{3,2},{4,5},{5,4},{6,7},{7,6},{8,9},{9,8},{10,11... | collective-permute-start | bytes 110600 | tf_op jit(solution)/shard_map/ppermute | solution.py:637
  278.7 20.1 %collective-permute-start.38 = (f32[12,768]{1,0:T(8,128)S(1)}, f32[12,768]{1,0:T(8,128)S(1)}, u32[]{:S(2)}, u32[]{:S(2)}) collective-permute-start(f32[12,768]{1,0:T(8,128)S(1)} %add.345), channel_id=1, source_target_pairs={{0,2},{1,3},{2,0},{3,1},{4,6},{5,7},{6,4},{7,5},{8,10},{9,11},{10,... | collective-permute-start | bytes 110600 | tf_op jit(solution)/shard_map/ppermute | solution.py:637
  298.8 56.3 %collective-permute-start.39 = (f32[12,768]{1,0:T(8,128)S(1)}, f32[12,768]{1,0:T(8,128)S(1)}, u32[]{:S(2)}, u32[]{:S(2)}) collective-permute-start(f32[12,768]{1,0:T(8,128)S(1)} %add.346), channel_id=1, source_target_pairs={{0,4},{1,5},{2,6},{3,7},{4,0},{5,1},{6,2},{7,3},{8,12},{9,13},{10,... | collective-permute-start | bytes 110600 | tf_op jit(solution)/shard_map/ppermute | solution.py:637
  314.3 9.9 %collective-permute-start.24 = (bf16[4,48,1536]{2,1,0:T(8,128)(2,1)S(1)}, bf16[4,48,1536]{2,1,0:T(8,128)(2,1)S(1)}, u32[]{:S(2)}, u32[]{:S(2)}) collective-permute-start(bf16[4,48,1536]{2,1,0:T(8,128)(2,1)S(1)} %get-tuple-element.163), channel_id=1, source_target_pairs={{0,4},{1,9},{2,6},{3,11},{4,0},{5,13},{6,2},{7,15},{8,12},{9,1},{1... | collective-permute-start | bytes 1769480 | tf_op jit(solution)/shard_map/ppermute | solution.py:633
  314.4 3.6 copy-start.25
  315.9 14.7 %collective-permute-start.29 = (bf16[4,48,1536]{2,1,0:T(8,128)(2,1)S(1)}, bf16[4,48,1536]{2,1,0:T(8,128)(2,1)S(1)}, u32[]{:S(2)}, u32[]{:S(2)}) collective-permute-start(bf16[4,48,1536]{2,1,0:T(8,128)(2,1)S(1)} %get-tuple-element.165), channel_id=1, source_target_pairs={{0,4},{1,9},{2,6},{3,11},{4,0},{5,13},{6,2},{7,15},{8,12},{9,1},{1... | collective-permute-start | bytes 1769480 | tf_op jit(solution)/shard_map/ppermute | solution.py:633
  319.4 17.5 %collective-permute-start.19 = (bf16[4,96,768]{2,1,0:T(8,128)(2,1)S(1)}, bf16[4,96,768]{2,1,0:T(8,128)(2,1)S(1)}, u32[]{:S(2)}, u32[]{:S(2)}) collective-permute-start(bf16[4,96,768]{2,1,0:T(8,128)(2,1)S(1)} %get-tuple-element.167), channel_id=1, source_target_pairs={{0,4},{1,9},{2,6},{3,11},{4,0},{5,13},{6,2},{7,15},{8,12},{9,1},{1... | collective-permute-start | bytes 1769480 | tf_op jit(solution)/shard_map/ppermute | solution.py:633
  324.3 12.7 %collective-permute-start.25 = (bf16[2,48,1536]{2,1,0:T(8,128)(2,1)S(1)}, bf16[2,48,1536]{2,1,0:T(8,128)(2,1)S(1)}, u32[]{:S(2)}, u32[]{:S(2)}) collective-permute-start(bf16[2,48,1536]{2,1,0:T(8,128)(2,1)S(1)} %get-tuple-element.169), channel_id=1, source_target_pairs={{0,8},{1,17},{2,10},{3,19},{4,12},{5,21},{6,14},{7,23},{8,0},{9,25... | collective-permute-start | bytes 884744 | tf_op jit(solution)/shard_map/ppermute | solution.py:633
  330.6 9.1 %collective-permute-start.30 = (bf16[2,48,1536]{2,1,0:T(8,128)(2,1)S(1)}, bf16[2,48,1536]{2,1,0:T(8,128)(2,1)S(1)}, u32[]{:S(2)}, u32[]{:S(2)}) collective-permute-start(bf16[2,48,1536]{2,1,0:T(8,128)(2,1)S(1)} %get-tuple-element.171), channel_id=1, source_target_pairs={{0,8},{1,17},{2,10},{3,19},{4,12},{5,21},{6,14},{7,23},{8,0},{9,25... | collective-permute-start | bytes 884744 | tf_op jit(solution)/shard_map/ppermute | solution.py:633
  336.9 8.5 %collective-permute-start.20 = (bf16[2,96,768]{2,1,0:T(8,128)(2,1)S(1)}, bf16[2,96,768]{2,1,0:T(8,128)(2,1)S(1)}, u32[]{:S(2)}, u32[]{:S(2)}) collective-permute-start(bf16[2,96,768]{2,1,0:T(8,128)(2,1)S(1)} %get-tuple-element.173), channel_id=1, source_target_pairs={{0,8},{1,17},{2,10},{3,19},{4,12},{5,21},{6,14},{7,23},{8,0},{9,25... | collective-permute-start | bytes 884744 | tf_op jit(solution)/shard_map/ppermute | solution.py:633
  337.1 8.6 %collective-permute-start.26 = (bf16[1,48,1536]{2,1,0:T(8,128)(2,1)S(1)}, bf16[1,48,1536]{2,1,0:T(8,128)(2,1)S(1)}, u32[]{:S(2)}, u32[]{:S(2)}) collective-permute-start(bf16[1,48,1536]{2,1,0:T(8,128)(2,1)S(1)} %slice_add_fusion.20), channel_id=1, source_target_pairs={{0,16},{1,3},{2,18},{3,1},{4,20},{5,7},{6,22},{7,5},{8,24},{9,11},... | collective-permute-start | bytes 442376 | tf_op jit(solution)/shard_map/ppermute | solution.py:633
  339.7 8.8 %collective-permute-start.31 = (bf16[1,48,1536]{2,1,0:T(8,128)(2,1)S(1)}, bf16[1,48,1536]{2,1,0:T(8,128)(2,1)S(1)}, u32[]{:S(2)}, u32[]{:S(2)}) collective-permute-start(bf16[1,48,1536]{2,1,0:T(8,128)(2,1)S(1)} %slice_add_fusion.18), channel_id=1, source_target_pairs={{0,16},{1,3},{2,18},{3,1},{4,20},{5,7},{6,22},{7,5},{8,24},{9,11},... | collective-permute-start | bytes 442376 | tf_op jit(solution)/shard_map/ppermute | solution.py:633
  345.4 10.8 %copy-start.28 = (f32[96,3,192]{2,0,1:T(8,128)S(1)}, f32[96,3,192]{2,0,1:T(8,128)}, u32[]{:S(2)}) copy-start(f32[96,3,192]{2,0,1:T(8,128)} %param.29) | copy-start | bytes 663556
  345.4 6.8 %collective-permute-start.21 = (bf16[1,96,768]{2,1,0:T(8,128)(2,1)S(1)}, bf16[1,96,768]{2,1,0:T(8,128)(2,1)S(1)}, u32[]{:S(2)}, u32[]{:S(2)}) collective-permute-start(bf16[1,96,768]{2,1,0:T(8,128)(2,1)S(1)} %slice_add_fusion.22), channel_id=1, source_target_pairs={{0,16},{1,3},{2,18},{3,1},{4,20},{5,7},{6,22},{7,5},{8,24},{9,11},... | collective-permute-start | bytes 442376 | tf_op jit(solution)/shard_map/ppermute | solution.py:633
  345.7 10.7 %copy-start.40 = (f32[192,96]{1,0:T(8,128)S(1)}, f32[192,96]{1,0:T(8,128)}, u32[]{:S(2)}) copy-start(f32[192,96]{1,0:T(8,128)} %param.37) | copy-start | bytes 221188
  345.7 10.9 %copy-start.34 = (f32[96,3,192]{2,0,1:T(8,128)S(1)}, f32[96,3,192]{2,0,1:T(8,128)}, u32[]{:S(2)}) copy-start(f32[96,3,192]{2,0,1:T(8,128)} %param.36) | copy-start | bytes 663556
  348.5 8.0 %copy-start.41 = (f32[192,96]{1,0:T(8,128)S(1)}, f32[192,96]{1,0:T(8,128)}, u32[]{:S(2)}) copy-start(f32[192,96]{1,0:T(8,128)} %param.44) | copy-start | bytes 221188
  348.5 8.2 %copy-start.35 = (f32[96,3,192]{2,0,1:T(8,128)S(1)}, f32[96,3,192]{2,0,1:T(8,128)}, u32[]{:S(2)}) copy-start(f32[96,3,192]{2,0,1:T(8,128)} %param.43) | copy-start | bytes 663556
  355.0 1.2 collective-permute-start.32
  355.1 4.2 %collective-permute-start.40 = (f32[12,768]{1,0:T(8,128)S(1)}, f32[12,768]{1,0:T(8,128)S(1)}, u32[]{:S(2)}, u32[]{:S(2)}) collective-permute-start(f32[12,768]{1,0:T(8,128)S(1)} %add.347), channel_id=1, source_target_pairs={{0,8},{1,9},{2,10},{3,11},{4,12},{5,13},{6,14},{7,15},{8,0},{9,1},... | collective-permute-start | bytes 110600 | tf_op jit(solution)/shard_map/ppermute | solution.py:637
  356.2 3.9 %collective-permute-start.33 = (f32[8,128]{1,0:T(8,128)S(1)}, f32[8,128]{1,0:T(8,128)S(1)}, u32[]{:S(2)}, u32[]{:S(2)}) collective-permute-start(f32[8,128]{1,0:T(8,128)S(1)} %broadcast_add_fusion), channel_id=1, source_target_pairs={{0,2},{1,3},{2,0},{3,1},{4,6},{5,7},{6,4},{7,5},{8,10},{9,11},{10,... | collective-permute-start | bytes 12296 | tf_op jit(solution)/shard_map/ppermute | solution.py:637
  359.3 5.3 %collective-permute-start.41 = (f32[12,768]{1,0:T(8,128)S(1)}, f32[12,768]{1,0:T(8,128)S(1)}, u32[]{:S(2)}, u32[]{:S(2)}) collective-permute-start(f32[12,768]{1,0:T(8,128)S(1)} %add.348), channel_id=1, source_target_pairs={{0,16},{1,17},{2,18},{3,19},{4,20},{5,21},{6,22},{7,23},{8,24},{9,... | collective-permute-start | bytes 110600 | tf_op jit(solution)/shard_map/ppermute | solution.py:637
  360.1 5.3 %collective-permute-start.34 = (f32[8,128]{1,0:T(8,128)S(1)}, f32[8,128]{1,0:T(8,128)S(1)}, u32[]{:S(2)}, u32[]{:S(2)}) collective-permute-start(f32[8,128]{1,0:T(8,128)S(1)} %fusion.24), channel_id=1, source_target_pairs={{0,4},{1,5},{2,6},{3,7},{4,0},{5,1},{6,2},{7,3},{8,12},{9,13},{10,... | collective-permute-start | bytes 12296 | tf_op jit(solution)/shard_map/ppermute | solution.py:637
  365.5 3.7 collective-permute-start.35
  369.1 4.5 %collective-permute-start.36 = (f32[8,128]{1,0:T(8,128)S(1)}, f32[8,128]{1,0:T(8,128)S(1)}, u32[]{:S(2)}, u32[]{:S(2)}) collective-permute-start(f32[8,128]{1,0:T(8,128)S(1)} %add.343), channel_id=1, source_target_pairs={{0,16},{1,17},{2,18},{3,19},{4,20},{5,21},{6,22},{7,23},{8,24},{9,... | collective-permute-start | bytes 12296 | tf_op jit(solution)/shard_map/ppermute | solution.py:637
  380.2 3.5 copy-start.36
  (31 other events, 68.0 us)
